TPU v7x, 256 devices: a whole 4x4x8 slice. The times are simulated.
256 devices in a mesh: cuts: 16 (over y_lo, z), fsdp: 16 (over x, y_hi, core).
Axes of the slice: x: 4, y: 4 (y_hi: 2, y_lo: 2; y = y_hi * 2 + y_lo), z: 8, core: 2. Of those that a mesh axis runs over, the one named last changes fastest.
Arguments:
- tokens: bfloat16 [32768, 2560], P(('cuts', 'fsdp')), may hold values from -6 to 6
- upstream: bfloat16 [32768, 6912], P(('cuts', 'fsdp')), may hold values from -24 to 24
- gate_weight: bfloat16 [2560, 6912], P(None, 'fsdp'), may hold values from -0.125 to 0.125
- probe: bfloat16 [2560, 6912], P(None, 'fsdp'), may hold values from -6 to 6
Outputs:
- curvature: float32 [2560, 6912], P(None, 'fsdp')
All inputs are finite; a program needn't handle non-finite values.
Results may differ from a plain program's by a relative error of at most 0.0029.
Values may be sent and summed in bfloat16 or wider, within the bound.
No kernel may reach another device: no remote copies, remote signals or barrier semaphores. Data moves between devices by JAX's collectives and lax.ppermute only.
A program may use at most 128 MiB of HBM per device.

v0:
```python
import jax
import jax.numpy as jnp
from jax import lax
from jax.sharding import PartitionSpec as P


def weigh_rows(token_piece, grad_rows, gate_weight, probe):
    gate_out = jnp.dot(token_piece, gate_weight, preferred_element_type=jnp.float32)
    tangent = jnp.dot(token_piece, probe, preferred_element_type=jnp.float32)
    logistic = jax.nn.sigmoid(gate_out)
    bend_factor = logistic * (1.0 - logistic) * (2.0 + gate_out * (1.0 - 2.0 * logistic))
    return (grad_rows.astype(jnp.float32) * bend_factor * tangent).astype(jnp.bfloat16)


def on_device(tokens, upstream, gate_weight, probe):
    spread = lax.all_to_all(upstream, "fsdp", split_axis=1, concat_axis=0, tiled=True)
    token_count = tokens.shape[0] * lax.axis_size("fsdp") * lax.axis_size("cuts")
    token_piece = lax.all_gather(tokens, "fsdp", axis=0, tiled=True)
    weighted = weigh_rows(token_piece, spread, gate_weight, probe)
    product = lax.dot_general(
        token_piece, weighted, (((0,), (0,)), ((), ())), preferred_element_type=jnp.float32
    )
    summed = lax.psum(product, "cuts")
    return probe.astype(jnp.float32) * (summed / token_count)


def solution(mesh):
    return jax.shard_map(
        on_device,
        mesh=mesh,
        in_specs=(
            P(("cuts", "fsdp"), None),
            P(("cuts", "fsdp"), None),
            P(None, "fsdp"),
            P(None, "fsdp"),
        ),
        out_specs=P(None, "fsdp"),
        check_vma=False,
    )
```

profile of v0, /device:TPU:16, one launch (start us, length us, event | category | flops | bytes accessed | tf_op | source)
XLA Modules:
  0.0 308.3 jit_solution(9846188742704740682)
XLA Ops:
  6.5 0.0 copy-start
  6.5 0.0 all-gather.2.cloned.1.call-start
  6.5 0.7 all-gather.2.cloned.1.call-update
  7.3 3.8 %copy.6 = bf16[128,6912]{0,1:T(8,128)(2,1)} copy(bf16[128,6912]{1,0:T(8,128)(2,1)} %param.5) | data formatting | bytes 3538944 | tf_op args[1]
  11.1 7.3 %all-to-all-start = ((bf16[128,16,432]{0,2,1:T(8,128)(2,1)}), bf16[128,16,432]{0,2,1:T(8,128)(2,1)}, u32[]{:S(2)}, u32[]{:S(2)}) async-start(bf16[128,16,432]{0,2,1:T(8,128)(2,1)} %bitcast.17), calls=%async_computation | async-start | bytes 3538944 | tf_op jit(solution)/shard_map/all_to_all | solution.py:16
  18.4 0.0 all-reduce.2.cloned.1.call-start
  18.4 90.7 %all-gather.2.cloned.1.call-done = bf16[2048,2560]{1,0:T(8,128)(2,1)} async-done(((bf16[128,2560]{1,0:T(8,128)(2,1)}), bf16[2048,2560]{1,0:T(8,128)(2,1)}) %all-gather.2.cloned.1.call-update) | async-done | bytes 10485776 | tf_op jit(solution)/shard_map/all_gather | solution.py:18
  109.1 0.0 copy-done
  109.1 9.4 %fusion.8 = f32[2048,432]{0,1:T(8,128)} fusion(bf16[2048,2560]{1,0:T(8,128)(2,1)} %all-gather.2.cloned.1.call-done, bf16[2560,432]{0,1:T(8,128)(2,1)S(1)} %copy-done), kind=kOutput, calls=%fused_computation.12 | convolution fusion | flops 4529848320 | bytes 16236544 | tf_op jit(solution)/shard_map/dot_general | solution.py:8
  118.5 0.0 all-to-all-done
  118.5 21.5 %convolution_bitcast_fusion = f32[2560,432]{0,1:T(8,128)} fusion(bf16[2048,2560]{1,0:T(8,128)(2,1)} %all-gather.2.cloned.1.call-done, f32[2048,432]{0,1:T(8,128)} %fusion.8, bf16[2560,432]{0,1:T(8,128)(2,1)} %param.7, bf16[128,16,432]{0,2,1:T(8,128)(2,1)} %all-to-all-done), kind=kOutput, calls=%fused_computation.1 | convolution fusion | flops 9072082944 | bytes 22429696 | tf_op jit(solution)/shard_map/dot_general | solution.py:20
  140.0 0.0 all-reduce.2.cloned.1.call-update
  140.0 155.7 %all-reduce.2.cloned.1.call-done = f32[2560,432]{0,1:T(8,128)} async-done(((f32[2560,432]{0,1:T(8,128)}), f32[2560,432]{0,1:T(8,128)}) %all-reduce.2.cloned.1.call-update) | async-done | bytes 4423696 | tf_op jit(solution)/shard_map/psum | solution.py:23
  295.7 5.7 %multiply_multiply_fusion = f32[2560,432]{0,1:T(8,128)} fusion(f32[2560,432]{0,1:T(8,128)} %all-reduce.2.cloned.1.call-done, bf16[2560,432]{0,1:T(8,128)(2,1)} %param.7), kind=kLoop, calls=%fused_computation.2 | loop fusion | flops 3317760 | bytes 11059200 | tf_op jit(solution)/shard_map/mul | solution.py:24
Async XLA Ops:
  6.5 102.5 %copy-start = (bf16[2560,432]{0,1:T(8,128)(2,1)S(1)}, bf16[2560,432]{0,1:T(8,128)(2,1)}, u32[]{:S(2)}) copy-start(bf16[2560,432]{0,1:T(8,128)(2,1)} %param.6) | copy-start | bytes 6635524
  6.5 102.5 %all-gather.2.cloned.1.call-start = ((), (), s32[]{:S(2)}) async-start(), calls=%async_computation.1 | async-start | bytes 11141120 | tf_op jit(solution)/shard_map/all_gather | solution.py:18
  11.1 107.4 %all-to-all-start = ((bf16[128,16,432]{0,2,1:T(8,128)(2,1)}), bf16[128,16,432]{0,2,1:T(8,128)(2,1)}, u32[]{:S(2)}, u32[]{:S(2)}) async-start(bf16[128,16,432]{0,2,1:T(8,128)(2,1)} %bitcast.17), calls=%async_computation | async-start | bytes 3538944 | tf_op jit(solution)/shard_map/all_to_all | solution.py:16
  18.4 277.4 %all-reduce.2.cloned.1.call-start = ((), (), s32[]{:S(2)}) async-start(), calls=%async_computation.2 | async-start | bytes 8847360 | tf_op jit(solution)/shard_map/psum | solution.py:23
Sparse Core Ops, SparseCore 0:
  10.1 98.9 all-gather.1
  140.1 155.5 all-reduce.1
where the time goes:
time: 309 us; the launch traced here: 308 us
  waiting for transfers between devices  247 us (80%)
  matrix products  30.9 us (10%)
  between operations  13.4 us (4%)
  starting transfers between devices  7.32 us (2%)
  other arithmetic  5.71 us (2%)
  local copies, waits for them, and re-layouts  3.84 us (1%)
    psum x1, waiting for transfers between devices, on_device(): summed = lax.psum(product, 'cuts')  156 us
    all_gather x1, waiting for transfers between devices, on_device(): token_piece = lax.all_gather(tokens, 'fsdp', axis=0, tiled=True)  90.7 us
    dot_general x1, matrix products, on_device(): lax.dot_general(token_piece, weighted, (((0,), (0,)), ((), ())), preferre...  21.5 us
    dot_general x1, matrix products, weigh_rows(): jnp.dot(token_piece, gate_weight, preferred_element_type=jnp.float32)  9.37 us
    all_to_all x1, starting transfers between devices, on_device(): lax.all_to_all(upstream, 'fsdp', split_axis=1, concat_axis=0, tiled=True)  7.28 us
  transfers between devices with their start and end apart: 3, of which 2 were waited for; matrix products, arithmetic and copies ran while one was open for 4% of the time, Pallas kernels for 0%

commit v1 on v0

v1 whole, which is shorter than its diff:
```python
import jax
import jax.numpy as jnp
from jax import lax
from jax.experimental import pallas as pl
from jax.experimental.pallas import tpu as pltpu
from jax.sharding import PartitionSpec as P

AXES = ("cuts", "fsdp")
NX, NY, NZ, NC = 4, 4, 8, 2
F32, BF16 = jnp.float32, jnp.bfloat16
VMEM_LIMIT = 62_000_000

PIECE = 56


def device(x, y, z, core):
    return ((y % 2) * NZ + z) * (NX * 2 * NC) + (x * 2 + y // 2) * NC + core


def moves(step):
    chips = [(x, y, z, c) for x in range(NX) for y in range(NY) for z in range(NZ) for c in range(NC)]
    return [(device(*at), device(*step(*at))) for at in chips]


X_UP = moves(lambda x, y, z, c: ((x + 1) % NX, y, z, c))
X_DOWN = moves(lambda x, y, z, c: ((x - 1) % NX, y, z, c))
Z_UP = moves(lambda x, y, z, c: (x, y, (z + 1) % NZ, c))
Z_DOWN = moves(lambda x, y, z, c: (x, y, (z - 1) % NZ, c))
Y_MATE = moves(lambda x, y, z, c: (x, 3 - y, z, c))
Y_CUT = moves(lambda x, y, z, c: (x, y ^ 1, z, c))
CORE = moves(lambda x, y, z, c: (x, y, z, 1 - c))

REPLICAS = [
    [device(x, (low, 3 - low)[high], z, c) for x in range(NX) for high in range(2) for c in range(NC)]
    for low in range(2)
    for z in range(NZ)
]
Z_RINGS = [
    [device(x, y, z, c) for z in range(NZ)] for x in range(NX) for y in range(NY) for c in range(NC)
]


def send(value, pairs):
    return lax.ppermute(value, AXES, pairs)


def after(values, *before):
    return lax.optimization_barrier((*values, *before))[: len(values)]


def params():
    return pltpu.CompilerParams(vmem_limit_bytes=VMEM_LIMIT)


def factor_kernel(weighing, table_ref, gate_ref, probe_ref, *refs):
    tokens_ref, out_ref = refs[-1], refs[-2]
    grads, groups = (refs[:2], refs[2:-2]) if weighing else ((), refs[:-2])
    n = out_ref.shape[2]

    def take(mine_ref, core_ref):
        tokens_ref[:n] = mine_ref[...]
        tokens_ref[n:] = core_ref[...]

    if len(groups) == 2:
        take(*groups)
    else:
        pl.when(pl.program_id(0) == 0)(lambda: take(*groups[:2]))
        pl.when(pl.program_id(0) > 0)(lambda: take(*groups[2:]))
    across = (((1,), (1,)), ((), ()))
    gate = lax.dot_general(gate_ref[...], tokens_ref[...], across, preferred_element_type=F32)
    tangent = lax.dot_general(probe_ref[...], tokens_ref[...], across, preferred_element_type=F32)
    s = 1.0 / (1.0 + jnp.exp(-gate))
    bend = s * (1.0 - s) * (2.0 + gate * (1.0 - 2.0 * s))
    for side in range(2):
        at = slice(side * n, side * n + n)
        if weighing:
            out_ref[side] = (grads[side][0].astype(F32) * bend[:, at] * tangent[:, at]).astype(BF16)
        else:
            out_ref[side] = bend[:, at] * tangent[:, at]


def factor(table, first, gate_t, probe_t, spread, *tokens):
    hidden, depth = gate_t.shape
    rows = 128
    total = sum(t.shape[0] for t in tokens[::2])
    later = int(len(tokens) == 4)
    block = lambda skip: pl.BlockSpec((rows, depth), lambda j, o: (jnp.maximum(j - skip, 0), 0))
    only = pl.BlockSpec((rows, depth), lambda j, o: (0, 0))
    weighing = spread is not None
    return pl.pallas_call(
        lambda *refs: factor_kernel(weighing, *refs),
        grid_spec=pltpu.PrefetchScalarGridSpec(
            num_scalar_prefetch=1,
            grid=(total // rows,),
            in_specs=[pl.BlockSpec((hidden, depth), lambda j, o: (0, 0))] * 2
            + [
                pl.BlockSpec((1, hidden, rows), lambda j, o, side=side: (o[first + 2 * j + side], 0, 0))
                for side in range(2)
            ]
            * weighing
            + [only, only] * later
            + [block(later), block(later)],
            out_specs=pl.BlockSpec((2, hidden, rows), lambda j, o: (0, 0, j)),
            scratch_shapes=[pltpu.VMEM((2 * rows, depth), BF16)],
        ),
        out_shape=jax.ShapeDtypeStruct((2, hidden, total), BF16 if weighing else F32),
        compiler_params=params(),
        cost_estimate=pl.CostEstimate(flops=0, bytes_accessed=0, transcendentals=0),
        name="factor",
    )(table, gate_t, probe_t, *[spread, spread] * weighing, *tokens)


def weigh_kernel(table_ref, grad_ref, *refs):
    factor_refs, out_ref = refs[:-1], refs[-1]
    for side in range(2):
        at = 0
        for factor_ref in factor_refs:
            for k in range(0, factor_ref.shape[2], 128):
                grad = grad_ref[table_ref[2 * at + side]].astype(F32)
                to = (side * 8 + at) * 128
                out_ref[:, to : to + 128] = (grad * factor_ref[side, :, k : k + 128]).astype(BF16)
                at += 1


def weigh(table, spread, factors):
    _, hidden, _ = factors[0].shape
    block = hidden // 3
    return pl.pallas_call(
        weigh_kernel,
        grid_spec=pltpu.PrefetchScalarGridSpec(
            num_scalar_prefetch=1,
            grid=(3,),
            in_specs=[pl.BlockSpec((16, block, 128), lambda i, o: (0, i, 0))]
            + [pl.BlockSpec((2, block, f.shape[2]), lambda i, o: (0, i, 0)) for f in factors],
            out_specs=pl.BlockSpec((block, 2048), lambda i, o: (i, 0)),
        ),
        out_shape=jax.ShapeDtypeStruct((hidden, 2048), BF16),
        compiler_params=params(),
        name="weigh",
    )(table, spread, *factors)


def starts():
    return [min(PIECE * k, 432 - PIECE) for k in range(NZ)]


def outer_kernel(table_ref, weighted_ref, *refs):
    out_ref, tokens_ref = refs[-2], refs[-1]
    at = 0
    for ref in refs[:-2]:
        tokens_ref[at : at + ref.shape[0]] = ref[...]
        at += ref.shape[0]
    total = jnp.dot(weighted_ref[...], tokens_ref[...], preferred_element_type=F32)
    for k, row in enumerate(starts()):
        out_ref[k] = total[row : row + PIECE, :].astype(out_ref.dtype)


def outer(table, first, weighted, tokens, width, dtype):
    wide = 256
    hidden, depth = weighted.shape
    return pl.pallas_call(
        outer_kernel,
        grid_spec=pltpu.PrefetchScalarGridSpec(
            num_scalar_prefetch=1,
            grid=(width // wide,),
            in_specs=[pl.BlockSpec(weighted.shape, lambda j, c: (0, 0))]
            + [pl.BlockSpec((t.shape[0], wide), lambda j, c: (0, c[first + j])) for t in tokens],
            out_specs=pl.BlockSpec((NZ, PIECE, wide), lambda j, c: (0, 0, j)),
            scratch_shapes=[pltpu.VMEM((depth, wide), BF16)],
        ),
        out_shape=jax.ShapeDtypeStruct((NZ, PIECE, width), dtype),
        compiler_params=params(),
        cost_estimate=pl.CostEstimate(
            flops=2 * hidden * depth * width, bytes_accessed=2 * depth * width + 2 * hidden * depth, transcendentals=0
        ),
        name="outer",
    )(table, weighted, *tokens)


LOW = 27
AWAYS = (0, -1, 1, -2, 2, -3, 3, 4)


def finish_kernel(scale, table_ref, probe_ref, *refs):
    out_ref = refs[-1]
    side, j = pl.program_id(0), pl.program_id(1)
    z = table_ref[LOW - 1]

    def put(ref, away):
        row = jnp.minimum(lax.rem(z + away + NZ, NZ) * PIECE, out_ref.shape[0] - PIECE)
        out_ref[pl.ds(pl.multiple_of(row, 8), PIECE), :] = ref[...].astype(F32)

    for at in range(2):
        pieces = refs[9 * at : 9 * at + 9]

        @pl.when(side == at)
        def _():
            for ref, away in zip(pieces[:7], AWAYS):
                put(ref, away)

        for end in range(2):
            pl.when((side == at) & (j == end))(lambda: put(pieces[7 + end], AWAYS[7]))

    for row in range(0, out_ref.shape[0], 16):
        rows = slice(row, row + 16)
        out_ref[rows, :] = probe_ref[rows, :].astype(F32) * (out_ref[rows, :] * scale)


def finish(table, probe_t, sides, scale):
    hidden, depth = probe_t.shape
    wide = depth // 4
    column = lambda h, j, p: (0, 2 * lax.rem(p[LOW] + h, 2) + j)
    ring = [pl.BlockSpec((PIECE, wide), lambda h, j, p, at=at: (0, jnp.where(h == at, j, 1 - at))) for at in range(2)]
    end = pl.BlockSpec((PIECE, wide), lambda h, j, p: (0, 0))
    return pl.pallas_call(
        lambda *refs: finish_kernel(scale, *refs),
        grid_spec=pltpu.PrefetchScalarGridSpec(
            num_scalar_prefetch=1,
            grid=(2, 2),
            in_specs=[pl.BlockSpec((hidden, wide), column), *([ring[0]] * 7 + [end] * 2 + [ring[1]] * 7 + [end] * 2)],
            out_specs=pl.BlockSpec((hidden, wide), column),
        ),
        out_shape=jax.ShapeDtypeStruct(probe_t.shape, F32),
        compiler_params=params(),
        name="finish",
    )(table, probe_t, *sides[0], *sides[1])


def on_device(tokens, upstream, gate_weight, probe):
    cut, part = lax.axis_index("cuts"), lax.axis_index("fsdp")
    low, z = cut // NZ, cut % NZ
    x, high, core = part // 4, (part // 2) % 2, part % 2
    gate_t, probe_t = gate_weight.T, probe.T
    hidden, depth = gate_t.shape
    rows = tokens.shape[0]

    blocks = ((0, 0), (-1, 0), (1, 0), (0, 1), (2, 0), (-1, 1), (1, 1), (2, 1))
    per_half = depth // 2 // 256
    first = 4
    rest = per_half - first
    away, own = ((1 - low) * per_half, low * per_half)
    table = [((x + dx) % NX) * 4 + (high ^ dy) * 2 + (core ^ flip) for dx, dy in blocks for flip in range(2)]
    table += [side + n for side in (away, own) for n in range(first, per_half)]
    table += [side + n for side in (away, own) for n in range(first)]
    table = jnp.stack([*table, z, low]).astype(jnp.int32)

    turned = upstream.T.reshape(16, hidden, rows)
    mate, left, right = send(tokens, Y_MATE), send(tokens, X_UP), send(tokens, X_DOWN)
    core_tokens = send(tokens, CORE)
    spread = lax.all_to_all(
        turned, AXES, split_axis=0, concat_axis=0, axis_index_groups=REPLICAS, tiled=True
    )
    left, right, mate, table = after((left, right, mate, table), turned)
    beside, across, over = send(mate, X_UP), send(right, X_DOWN), send(right, Y_MATE)
    ring = jnp.concatenate([left, right, mate], 0)
    core_ring = send(ring, CORE)
    near = (tokens, core_tokens, ring, core_ring)
    weight_0 = factor(table, 0, gate_t, probe_t, None, *near)
    beside, across, over = after((beside, across, over), weight_0)
    cuts = (0, 48, 96, rows)
    last = [a[n:m] for a, n, m in zip((beside, over, across), cuts, cuts[1:])]
    beside, across, over = after((beside, across, over), *last)
    last = [send(last[0], X_UP), send(last[1], X_DOWN), send(last[2], Y_MATE)]
    far = jnp.concatenate([across, beside, over], 0)
    core_far = send(far, CORE)
    weight_1 = factor(table, 8, gate_t, probe_t, None, far, core_far)
    last = after(last, weight_1)
    corner = jnp.concatenate(last, 0)
    core_corner = send(corner, CORE)
    weight_2 = factor(table, 14, gate_t, probe_t, None, corner, core_corner)
    weighted = weigh(table, spread, (weight_0, weight_1, weight_2))

    pieces = (tokens, ring, far, corner, core_tokens, core_ring, core_far, core_corner)
    half = rest * 256
    ring_sum = lambda a: lax.all_to_all(
        a, AXES, split_axis=0, concat_axis=0, axis_index_groups=Z_RINGS, tiled=True
    ).astype(F32).sum(0)
    away = outer(table, 16 + 2 * rest, weighted, pieces, first * 256, BF16)
    come = send(away, Y_CUT)
    (table,) = after((table,), away)
    late = outer(table, 16, weighted, pieces, 2 * half, BF16)
    (table,) = after((table,), late)
    own = outer(table, 16 + 2 * rest + first, weighted, pieces, first * 256, F32)
    late = ring_sum(late)
    own = ring_sum((own + come.astype(F32)).astype(BF16))
    late = late[:, half:] + send(late[:, :half].astype(BF16), Y_CUT).astype(F32)
    own = jnp.concatenate([own.astype(BF16), late.astype(BF16)], 1)

    sides = []
    for piece in (own, send(own, Y_CUT)):
        up = down = piece
        gathered = [piece]
        for _ in range(3):
            up, down = send(up, Z_UP), send(down, Z_DOWN)
            gathered += [up, down]
        quarter = depth // 4
        sides.append([*gathered, send(up[:, :quarter], Z_UP), send(down[:, quarter:], Z_DOWN)])
    scale = 1.0 / (rows * lax.axis_size("fsdp") * lax.axis_size("cuts"))
    return finish(table, probe_t, sides, scale).T


def solution(mesh):
    return jax.shard_map(
        on_device,
        mesh=mesh,
        in_specs=(
            P(AXES, None),
            P(AXES, None),
            P(None, "fsdp"),
            P(None, "fsdp"),
        ),
        out_specs=P(None, "fsdp"),
        check_vma=False,
    )
```

time: 309 us -> 195 us (0.63)
  waiting for transfers between devices: 247 us -> 66.9 us
  Pallas kernels: 0 us -> 54.9 us
  starting transfers between devices: 7.32 us -> 55.1 us
  matrix products: 30.9 us -> 0 us
  between operations: 13.4 us -> 0.61 us
  local copies, waits for them, and re-layouts: 3.84 us -> 13.4 us
    psum x1 -> x0, waiting for transfers between devices: 156 us -> none  [on_device(): summed = lax.psum(product, 'cuts')]
    all_gather x1 -> x0, waiting for transfers between devices: 90.7 us -> none  [on_device(): token_piece = lax.all_gather(tokens, 'fsdp', axis=0, tiled=True)]
    pallas_call x0 -> x8, Pallas kernels: none -> 54.9 us  [the longest x3 24.8 us: factor(): pl.pallas_call(lambda *refs: factor_kernel(weighing, *refs), grid_spec=pl...]
    ppermute x0 -> x32, starting transfers between devices: none -> 37 us  [send(): return lax.ppermute(value, AXES, pairs)]
    all_to_all x1 -> x3, waiting for transfers between devices: 0.01 us -> 34.4 us  [the longest x2 28.1 us: on_device(): lax.all_to_all(a, AXES, split_axis=0, concat_axis=0, axis_index_groups=Z_...]
    ppermute x0 -> x32, waiting for transfers between devices: none -> 32.5 us  [send(): return lax.ppermute(value, AXES, pairs)]
    dot_general x2 -> x0, matrix products: 30.9 us -> none  [the longest x1 21.5 us: on_device(): lax.dot_general(token_piece, weighted, (((0,), (0,)), ((), ())), preferre...]
    all_to_all x1 -> x3, starting transfers between devices: 7.28 us -> 18.1 us  [the longest x2 12 us: on_device(): lax.all_to_all(a, AXES, split_axis=0, concat_axis=0, axis_index_groups=Z_...]
  transfers between devices with their start and end apart: 3 -> 35, of which waited for: 2 -> 19; matrix products, arithmetic and copies ran while one was open for 4% -> 4% of each run, Pallas kernels for 0% -> 19%
where the time goes in v1:
time: 195 us; the launch traced here: 194 us
  waiting for transfers between devices  66.9 us (34%)
  starting transfers between devices  55.1 us (28%)
  Pallas kernels  54.9 us (28%)
  local copies, waits for them, and re-layouts  13.4 us (7%)
  other arithmetic  2.97 us (2%)
    ppermute x32, starting transfers between devices, send(): return lax.ppermute(value, AXES, pairs)  37 us
    ppermute x32, waiting for transfers between devices, send(): return lax.ppermute(value, AXES, pairs)  32.5 us
    all_to_all x2, waiting for transfers between devices, on_device(): lax.all_to_all(a, AXES, split_axis=0, concat_axis=0, axis_index_groups=Z_...  28.1 us
    pallas_call x3, Pallas kernels, factor(): pl.pallas_call(lambda *refs: factor_kernel(weighing, *refs), grid_spec=pl...  24.8 us
    pallas_call x3, Pallas kernels, outer(): pl.pallas_call(outer_kernel, grid_spec=pltpu.PrefetchScalarGridSpec(num_s...  19 us
    all_to_all x2, starting transfers between devices, on_device(): lax.all_to_all(a, AXES, split_axis=0, concat_axis=0, axis_index_groups=Z_...  12 us
    all_to_all x1, waiting for transfers between devices, on_device(): lax.all_to_all(turned, AXES, split_axis=0, concat_axis=0, axis_index_grou...  6.27 us
    all_to_all x1, starting transfers between devices, on_device(): lax.all_to_all(turned, AXES, split_axis=0, concat_axis=0, axis_index_grou...  6.1 us
  transfers between devices with their start and end apart: 35, of which 19 were waited for; matrix products, arithmetic and copies ran while one was open for 4% of the time, Pallas kernels for 19%

profile of v1, /device:TPU:16, one launch (start us, length us, event | category | flops | bytes accessed | tf_op | source)
XLA Modules:
  0.0 193.9 jit_solution(16837969403325843556)
XLA Ops:
  0.5 2.8 %collective-permute-start.1 = (bf16[128,2560]{1,0:T(8,128)(2,1)}, bf16[128,2560]{1,0:T(8,128)(2,1)S(1)}, u32[]{:S(2)}, u32[]{:S(2)}) collective-permute-start(bf16[128,2560]{1,0:T(8,128)(2,1)} %refs_0_.5), channel_id=1, source_target_pairs={{0,12},{1,13},{16,28},{17,29},{32,44},{33,45},{48,60},{49,61},{64,... | collective-permute-start | bytes 1966088 | tf_op jit(solution)/shard_map/ppermute | solution.py:44
  3.2 3.8 %copy.5 = bf16[6912,128]{1,0:T(8,128)(2,1)} copy(bf16[6912,128]{0,1:T(8,128)(2,1)} %bitcast.41) | data formatting | bytes 3538944 | tf_op jit(solution)/shard_map/transpose | solution.py:247
  7.7 8.9 %collective-permute-done.2 = bf16[128,2560]{1,0:T(8,128)(2,1)S(1)} collective-permute-done((bf16[128,2560]{1,0:T(8,128)(2,1)}, bf16[128,2560]{1,0:T(8,128)(2,1)S(1)}, u32[]{:S(2)}, u32[]{:S(2)}) %collective-permute-start.2) | collective-permute-done | bytes 655392 | tf_op jit(solution)/shard_map/ppermute | solution.py:44
  17.2 3.3 %collective-permute-done = bf16[128,2560]{1,0:T(8,128)(2,1)S(1)} collective-permute-done((bf16[128,2560]{1,0:T(8,128)(2,1)}, bf16[128,2560]{1,0:T(8,128)(2,1)S(1)}, u32[]{:S(2)}, u32[]{:S(2)}) %collective-permute-start) | collective-permute-done | bytes 655392 | tf_op jit(solution)/shard_map/ppermute | solution.py:44
  21.6 1.6 collective-permute-start.7
  23.2 3.2 %collective-permute-start.6 = (bf16[128,2560]{1,0:T(8,128)(2,1)}, bf16[128,2560]{1,0:T(8,128)(2,1)}, u32[]{:S(2)}, u32[]{:S(2)}) collective-permute-start(bf16[128,2560]{1,0:T(8,128)(2,1)} %copy-done.7), channel_id=1, source_target_pairs={{0,12},{1,13},{16,28},{17,29},{32,44},{33,45},{48,60},{49,61},{64,... | collective-permute-start | bytes 1966088 | tf_op jit(solution)/shard_map/ppermute | solution.py:44
  26.5 0.8 copy-done.5
  27.3 1.3 copy-done.2
  28.6 10.7 %factor.3.refs_0_ = f32[2,432,512]{2,1,0:T(8,128)} custom-call(s32[28]{0:T(128)} %stack.115.refs_0_.table_ref, bf16[432,2560]{1,0:T(8,128)(2,1)} %bitcast.37, bf16[432,2560]{1,0:T(8,128)(2,1)} %bitcast.33, bf16[128,2560]{1,0:T(8,128)(2,1)} %refs_0_.5, bf16[128,2560]{1,0:T(8,128)(2,1)} %copy-done.5, bf16[384,2560]{1,0:T(8,128)(2,1)} %copy-done.1, ...), custom_call_target="tpu_custom_call" | custom-call | tf_op jit(solution)/shard_map/factor/pallas_call | solution.py:90
  39.3 0.9 collective-permute-done.5
  40.9 0.9 slice.30
  41.8 1.0 slice.29
  42.8 1.1 constant_dynamic-update-slice_fusion.5
  44.0 1.1 constant_dynamic-update-slice_fusion.3.refs_3_.refs_2_
  45.2 3.8 %collective-permute-start.10 = (bf16[48,2560]{1,0:T(8,128)(2,1)S(1)}, bf16[48,2560]{1,0:T(8,128)(2,1)S(1)}, u32[]{:S(2)}, u32[]{:S(2)}) collective-permute-start(bf16[48,2560]{1,0:T(8,128)(2,1)S(1)} %slice.29), channel_id=1, source_target_pairs={{0,12},{1,13},{16,28},{17,29},{32,44},{33,45},{48,60},{49,61},{64,... | collective-permute-start | bytes 737288 | tf_op jit(solution)/shard_map/ppermute | solution.py:44
  49.4 6.1 %all-to-all-start = ((bf16[16,432,128]{2,1,0:T(8,128)(2,1)}), bf16[16,432,128]{2,1,0:T(8,128)(2,1)}, u32[]{:S(2)}, u32[]{:S(2)}) async-start(bf16[16,432,128]{2,1,0:T(8,128)(2,1)} %bitcast.40), calls=%async_computation | async-start | bytes 3538944 | tf_op jit(solution)/shard_map/all_to_all | solution.py:250
  55.6 8.6 %factor.4.refs_1_ = f32[2,432,384]{2,1,0:T(8,128)} custom-call(s32[28]{0:T(128)} %stack.115.refs_0_.table_ref, bf16[432,2560]{1,0:T(8,128)(2,1)} %bitcast.38, bf16[432,2560]{1,0:T(8,128)(2,1)} %bitcast.34, bf16[384,2560]{1,0:T(8,128)(2,1)} %copy-done, bf16[384,2560]{1,0:T(8,128)(2,1)} %collective-permute-done.8.refs_4_.refs_6_), custom_call_target="tpu_custom_call" | custom-call | tf_op jit(solution)/shard_map/factor/pallas_call | solution.py:90
  64.7 2.0 %collective-permute-done.12.refs_4_.refs_7_ = bf16[128,2560]{1,0:T(8,128)(2,1)S(1)} collective-permute-done((bf16[128,2560]{1,0:T(8,128)(2,1)S(1)}, bf16[128,2560]{1,0:T(8,128)(2,1)S(1)}, u32[]{:S(2)}, u32[]{:S(2)}) %collective-permute-start.12) | collective-permute-done | bytes 655392 | tf_op jit(solution)/shard_map/ppermute | solution.py:44
  66.7 0.8 copy-done.6
  67.5 5.5 %factor.5.refs_2_ = f32[2,432,128]{2,1,0:T(8,128)} custom-call(s32[28]{0:T(128)} %stack.115.refs_0_.table_ref, bf16[432,2560]{1,0:T(8,128)(2,1)} %bitcast.39, bf16[432,2560]{1,0:T(8,128)(2,1)} %bitcast.35, bf16[128,2560]{1,0:T(8,128)(2,1)} %copy-done.3, bf16[128,2560]{1,0:T(8,128)(2,1)} %copy-done.6), custom_call_target="tpu_custom_call" | custom-call | tf_op jit(solution)/shard_map/factor/pallas_call | solution.py:90
  73.0 6.3 %all-to-all-done.grad_ref = bf16[16,432,128]{2,1,0:T(8,128)(2,1)} async-done(((bf16[16,432,128]{2,1,0:T(8,128)(2,1)}), bf16[16,432,128]{2,1,0:T(8,128)(2,1)}, u32[]{:S(2)}, u32[]{:S(2)}) %all-to-all-start) | async-done | bytes 1769504 | tf_op jit(solution)/shard_map/all_to_all | solution.py:250
  79.3 5.2 %weigh.1.weighted_ref = bf16[432,2048]{1,0:T(8,128)(2,1)} custom-call(s32[28]{0:T(128)} %stack.115.refs_0_.table_ref, bf16[16,432,128]{2,1,0:T(8,128)(2,1)} %all-to-all-done.grad_ref, f32[2,432,512]{2,1,0:T(8,128)} %factor.3.refs_0_, f32[2,432,384]{2,1,0:T(8,128)} %factor.4.refs_1_, f32[2,432,128]{2,1,0:T(8,128)} %factor.5.refs_2_), custom_call_target="tpu_custom_call" | custom-call | tf_op jit(solution)/shard_map/weigh/pallas_call | solution.py:128
  84.4 6.9 %outer.3 = bf16[8,56,1024]{2,1,0:T(8,128)(2,1)} custom-call(s32[28]{0:T(128)} %stack.115.refs_0_.table_ref, bf16[432,2048]{1,0:T(8,128)(2,1)} %weigh.1.weighted_ref, bf16[128,2560]{1,0:T(8,128)(2,1)} %refs_0_.5, bf16[384,2560]{1,0:T(8,128)(2,1)} %copy-done.1, bf16[384,2560]{1,0:T(8,128)(2,1)} %copy-done, bf16[128,2560]{1,0:T(8,128)(2,1)} %copy-done.3, ...), custom_call_target="tpu_custom_call" | custom-call | flops 1811939328 | bytes 5963776 | tf_op jit(solution)/shard_map/outer/pallas_call | solution.py:161
  91.4 3.7 %collective-permute-start.13 = (bf16[8,56,1024]{2,1,0:T(8,128)(2,1)}, bf16[8,56,1024]{2,1,0:T(8,128)(2,1)S(1)}, u32[]{:S(2)}, u32[]{:S(2)}) collective-permute-start(bf16[8,56,1024]{2,1,0:T(8,128)(2,1)} %outer.3), channel_id=1, source_target_pairs={{0,128},{1,129},{16,144},{17,145},{32,160},{33,161},{48,176},{49,1... | collective-permute-start | bytes 2752520 | tf_op jit(solution)/shard_map/ppermute | solution.py:44
  95.1 4.9 %outer.4 = bf16[8,56,512]{2,1,0:T(8,128)(2,1)} custom-call(s32[28]{0:T(128)} %stack.115.refs_0_.table_ref, bf16[432,2048]{1,0:T(8,128)(2,1)} %weigh.1.weighted_ref, bf16[128,2560]{1,0:T(8,128)(2,1)} %refs_0_.5, bf16[384,2560]{1,0:T(8,128)(2,1)} %copy-done.1, bf16[384,2560]{1,0:T(8,128)(2,1)} %copy-done, bf16[128,2560]{1,0:T(8,128)(2,1)} %copy-done.3, ...), custom_call_target="tpu_custom_call" | custom-call | flops 905969664 | bytes 3866624 | tf_op jit(solution)/shard_map/outer/pallas_call | solution.py:161
  100.0 8.5 %all-to-all-start.2 = ((bf16[8,56,512]{2,1,0:T(8,128)(2,1)}), bf16[8,56,512]{2,1,0:T(8,128)(2,1)S(1)}, u32[]{:S(2)}, u32[]{:S(2)}) async-start(bf16[8,56,512]{2,1,0:T(8,128)(2,1)} %outer.4), calls=%async_computation.2 | async-start | bytes 917504 | tf_op jit(solution)/shard_map/all_to_all | solution.py:275
  108.5 7.1 %outer.5 = f32[8,56,1024]{2,1,0:T(8,128)} custom-call(s32[28]{0:T(128)} %stack.115.refs_0_.table_ref, bf16[432,2048]{1,0:T(8,128)(2,1)} %weigh.1.weighted_ref, bf16[128,2560]{1,0:T(8,128)(2,1)} %refs_0_.5, bf16[384,2560]{1,0:T(8,128)(2,1)} %copy-done.1, bf16[384,2560]{1,0:T(8,128)(2,1)} %copy-done, bf16[128,2560]{1,0:T(8,128)(2,1)} %copy-done.3, ...), custom_call_target="tpu_custom_call" | custom-call | flops 1811939328 | bytes 5963776 | tf_op jit(solution)/shard_map/outer/pallas_call | solution.py:161
  116.1 2.7 %add_convert_fusion = bf16[8,56,1024]{2,1,0:T(8,128)(2,1)} fusion(f32[8,56,1024]{2,1,0:T(8,128)} %outer.5, bf16[8,56,1024]{2,1,0:T(8,128)(2,1)S(1)} %collective-permute-done.13), kind=kLoop, calls=%fused_computation | loop fusion | flops 1376256 | bytes 3670016 | tf_op jit(solution)/shard_map/convert_element_type | solution.py:285
  118.8 5.9 %all-to-all-done.2 = bf16[8,56,512]{2,1,0:T(8,128)(2,1)S(1)} async-done(((bf16[8,56,512]{2,1,0:T(8,128)(2,1)}), bf16[8,56,512]{2,1,0:T(8,128)(2,1)S(1)}, u32[]{:S(2)}, u32[]{:S(2)}) %all-to-all-start.2) | async-done | bytes 458784 | tf_op jit(solution)/shard_map/all_to_all | solution.py:275
  124.7 3.6 %all-to-all-start.1 = ((bf16[8,56,1024]{2,1,0:T(8,128)(2,1)}), bf16[8,56,1024]{2,1,0:T(8,128)(2,1)S(1)}, u32[]{:S(2)}, u32[]{:S(2)}) async-start(bf16[8,56,1024]{2,1,0:T(8,128)(2,1)} %add_convert_fusion), calls=%async_computation.1 | async-start | bytes 1835008 | tf_op jit(solution)/shard_map/all_to_all | solution.py:275
  128.4 0.8 collective-permute-start.14
  129.2 3.1 %collective-permute-done.14 = bf16[56,256]{1,0:T(8,128)(2,1)S(1)} collective-permute-done((bf16[56,256]{1,0:T(8,128)(2,1)S(1)}, bf16[56,256]{1,0:T(8,128)(2,1)S(1)}, u32[]{:S(2)}, u32[]{:S(2)}) %collective-permute-start.14) | collective-permute-done | bytes 28704 | tf_op jit(solution)/shard_map/ppermute | solution.py:44
  132.3 22.2 %all-to-all-done.1 = bf16[8,56,1024]{2,1,0:T(8,128)(2,1)S(1)} async-done(((bf16[8,56,1024]{2,1,0:T(8,128)(2,1)}), bf16[8,56,1024]{2,1,0:T(8,128)(2,1)S(1)}, u32[]{:S(2)}, u32[]{:S(2)}) %all-to-all-start.1) | async-done | bytes 917536 | tf_op jit(solution)/shard_map/all_to_all | solution.py:275
  155.2 2.0 %collective-permute-start.15 = (bf16[56,1280]{1,0:T(8,128)(2,1)S(1)}, bf16[56,1280]{1,0:T(8,128)(2,1)S(1)}, u32[]{:S(2)}, u32[]{:S(2)}) collective-permute-start(bf16[56,1280]{1,0:T(8,128)(2,1)S(1)} %pad_maximum_fusion.refs_2_), channel_id=1, source_target_pairs={{0,16},{1,17},{16,32},{17,33},{32,48},{33,49},{48,64},{49,65},{64,... | collective-permute-start | bytes 430088 | tf_op jit(solution)/shard_map/ppermute | solution.py:44
  157.2 2.8 %collective-permute-done.23.refs_11_ = bf16[56,1280]{1,0:T(8,128)(2,1)S(1)} collective-permute-done((bf16[56,1280]{1,0:T(8,128)(2,1)S(1)}, bf16[56,1280]{1,0:T(8,128)(2,1)S(1)}, u32[]{:S(2)}, u32[]{:S(2)}) %collective-permute-start.23) | collective-permute-done | bytes 143392 | tf_op jit(solution)/shard_map/ppermute | solution.py:44
  160.0 2.0 %collective-permute-start.24 = (bf16[56,1280]{1,0:T(8,128)(2,1)S(1)}, bf16[56,1280]{1,0:T(8,128)(2,1)S(1)}, u32[]{:S(2)}, u32[]{:S(2)}) collective-permute-start(bf16[56,1280]{1,0:T(8,128)(2,1)S(1)} %collective-permute-done.23.refs_11_), channel_id=1, source_target_pairs={{0,16},{1,17},{16,32},{17,33},{32,48},{33,49},{48,64},{49,65},{64,... | collective-permute-start | bytes 430088 | tf_op jit(solution)/shard_map/ppermute | solution.py:44
  162.0 1.2 collective-permute-start.18
  163.2 0.8 collective-permute-start.17
  164.0 1.6 collective-permute-done.25.refs_13_
  165.6 1.8 collective-permute-start.27
  168.7 2.0 %collective-permute-start.20 = (bf16[56,1280]{1,0:T(8,128)(2,1)S(1)}, bf16[56,1280]{1,0:T(8,128)(2,1)S(1)}, u32[]{:S(2)}, u32[]{:S(2)}) collective-permute-start(bf16[56,1280]{1,0:T(8,128)(2,1)S(1)} %collective-permute-done.18.refs_6_), channel_id=1, source_target_pairs={{0,112},{1,113},{16,0},{17,1},{32,16},{33,17},{48,32},{49,33},{64,... | collective-permute-start | bytes 430088 | tf_op jit(solution)/shard_map/ppermute | solution.py:44
  171.0 1.1 collective-permute-done.27.refs_15_
  172.1 2.2 %collective-permute-start.29 = (bf16[56,1280]{1,0:T(8,128)(2,1)S(1)}, bf16[56,1280]{1,0:T(8,128)(2,1)S(1)}, u32[]{:S(2)}, u32[]{:S(2)}) collective-permute-start(bf16[56,1280]{1,0:T(8,128)(2,1)S(1)} %collective-permute-done.27.refs_15_), channel_id=1, source_target_pairs={{0,112},{1,113},{16,0},{17,1},{32,16},{33,17},{48,32},{49,33},{64,... | collective-permute-start | bytes 430088 | tf_op jit(solution)/shard_map/ppermute | solution.py:44
  175.1 2.9 %collective-permute-start.22 = (bf16[56,640]{1,0:T(8,128)(2,1)S(1)}, bf16[56,640]{1,0:T(8,128)(2,1)S(1)}, u32[]{:S(2)}, u32[]{:S(2)}) collective-permute-start(bf16[56,640]{1,0:T(8,128)(2,1)S(1)} %slice.40), channel_id=1, source_target_pairs={{0,112},{1,113},{16,0},{17,1},{32,16},{33,17},{48,32},{49,33},{64,... | collective-permute-start | bytes 215048 | tf_op jit(solution)/shard_map/ppermute | solution.py:44
  178.1 3.3 %collective-permute-start.31 = (bf16[56,640]{1,0:T(8,128)(2,1)S(1)}, bf16[56,640]{1,0:T(8,128)(2,1)S(1)}, u32[]{:S(2)}, u32[]{:S(2)}) collective-permute-start(bf16[56,640]{1,0:T(8,128)(2,1)S(1)} %slice.42), channel_id=1, source_target_pairs={{0,112},{1,113},{16,0},{17,1},{32,16},{33,17},{48,32},{49,33},{64,... | collective-permute-start | bytes 215048 | tf_op jit(solution)/shard_map/ppermute | solution.py:44
  181.5 2.0 %collective-permute-done.21.refs_9_ = bf16[56,640]{1,0:T(8,128)(2,1)S(1)} collective-permute-done((bf16[56,640]{1,0:T(8,128)(2,1)S(1)}, bf16[56,640]{1,0:T(8,128)(2,1)S(1)}, u32[]{:S(2)}, u32[]{:S(2)}) %collective-permute-start.21) | collective-permute-done | bytes 71712 | tf_op jit(solution)/shard_map/ppermute | solution.py:44
  183.6 3.5 %collective-permute-done.30.refs_18_ = bf16[56,640]{1,0:T(8,128)(2,1)S(1)} collective-permute-done((bf16[56,640]{1,0:T(8,128)(2,1)S(1)}, bf16[56,640]{1,0:T(8,128)(2,1)S(1)}, u32[]{:S(2)}, u32[]{:S(2)}) %collective-permute-start.30) | collective-permute-done | bytes 71712 | tf_op jit(solution)/shard_map/ppermute | solution.py:44
  187.8 5.9 %finish.1 = f32[432,2560]{1,0:T(8,128)} custom-call(s32[28]{0:T(128)} %stack.115.refs_0_.table_ref, bf16[432,2560]{1,0:T(8,128)(2,1)} %bitcast.36, bf16[56,1280]{1,0:T(8,128)(2,1)} %copy-done.9, bf16[56,1280]{1,0:T(8,128)(2,1)} %copy-done.16, bf16[56,1280]{1,0:T(8,128)(2,1)} %copy-done.15, bf16[56,1280]{1,0:T(8,128)(2,1)} %copy-done.20, ...), custom_call_target="tpu_custom_call" | custom-call | tf_op jit(solution)/shard_map/finish/pallas_call | solution.py:215
  (108 shorter events, 8.9 us)
Async XLA Ops:
  0.0 16.7 %collective-permute-start.2 = (bf16[128,2560]{1,0:T(8,128)(2,1)}, bf16[128,2560]{1,0:T(8,128)(2,1)S(1)}, u32[]{:S(2)}, u32[]{:S(2)}) collective-permute-start(bf16[128,2560]{1,0:T(8,128)(2,1)} %refs_0_.5), channel_id=1, source_target_pairs={{0,130},{1,131},{16,146},{17,147},{32,162},{33,163},{48,178},{49,1... | collective-permute-start | bytes 1966088 | tf_op jit(solution)/shard_map/ppermute | solution.py:44
  0.5 16.8 %collective-permute-start.1 = (bf16[128,2560]{1,0:T(8,128)(2,1)}, bf16[128,2560]{1,0:T(8,128)(2,1)S(1)}, u32[]{:S(2)}, u32[]{:S(2)}) collective-permute-start(bf16[128,2560]{1,0:T(8,128)(2,1)} %refs_0_.5), channel_id=1, source_target_pairs={{0,12},{1,13},{16,28},{17,29},{32,44},{33,45},{48,60},{49,61},{64,... | collective-permute-start | bytes 1966088 | tf_op jit(solution)/shard_map/ppermute | solution.py:44
  3.2 17.3 %collective-permute-start = (bf16[128,2560]{1,0:T(8,128)(2,1)}, bf16[128,2560]{1,0:T(8,128)(2,1)S(1)}, u32[]{:S(2)}, u32[]{:S(2)}) collective-permute-start(bf16[128,2560]{1,0:T(8,128)(2,1)} %refs_0_.5), channel_id=1, source_target_pairs={{0,4},{1,5},{16,20},{17,21},{32,36},{33,37},{48,52},{49,53},{64,68... | collective-permute-start | bytes 1966088 | tf_op jit(solution)/shard_map/ppermute | solution.py:44
  20.7 5.7 %collective-permute-start.4 = (bf16[384,2560]{1,0:T(8,128)(2,1)S(1)}, bf16[384,2560]{1,0:T(8,128)(2,1)S(1)}, u32[]{:S(2)}, u32[]{:S(2)}) collective-permute-start(bf16[384,2560]{1,0:T(8,128)(2,1)S(1)} %constant_dynamic-update-slice_fusion.refs_5_.refs_1_), channel_id=1, source_target_pairs={{0,1},{1,0},{16,17},{17,16},{32,33},{33,32},{48,49},{49,48},{64,65... | collective-permute-start | bytes 5898248 | tf_op jit(solution)/shard_map/ppermute | solution.py:44
  21.6 4.8 %collective-permute-start.3 = (bf16[128,2560]{1,0:T(8,128)(2,1)S(1)}, bf16[128,2560]{1,0:T(8,128)(2,1)S(1)}, u32[]{:S(2)}, u32[]{:S(2)}) collective-permute-start(bf16[128,2560]{1,0:T(8,128)(2,1)S(1)} %copy-done.4), channel_id=1, source_target_pairs={{0,1},{1,0},{16,17},{17,16},{32,33},{33,32},{48,49},{49,48},{64,65... | collective-permute-start | bytes 1966088 | tf_op jit(solution)/shard_map/ppermute | solution.py:44
  21.6 18.6 %collective-permute-start.5 = (bf16[128,2560]{1,0:T(8,128)(2,1)}, bf16[128,2560]{1,0:T(8,128)(2,1)S(1)}, u32[]{:S(2)}, u32[]{:S(2)}) collective-permute-start(bf16[128,2560]{1,0:T(8,128)(2,1)} %copy-done.8), channel_id=1, source_target_pairs={{0,4},{1,5},{16,20},{17,21},{32,36},{33,37},{48,52},{49,53},{64,68... | collective-permute-start | bytes 1966088 | tf_op jit(solution)/shard_map/ppermute | solution.py:44
  21.6 18.6 %collective-permute-start.7 = (bf16[128,2560]{1,0:T(8,128)(2,1)}, bf16[128,2560]{1,0:T(8,128)(2,1)}, u32[]{:S(2)}, u32[]{:S(2)}) collective-permute-start(bf16[128,2560]{1,0:T(8,128)(2,1)} %copy-done.7), channel_id=1, source_target_pairs={{0,130},{1,131},{16,146},{17,147},{32,162},{33,163},{48,178},{49,1... | collective-permute-start | bytes 1966088 | tf_op jit(solution)/shard_map/ppermute | solution.py:44
  23.2 17.7 %collective-permute-start.6 = (bf16[128,2560]{1,0:T(8,128)(2,1)}, bf16[128,2560]{1,0:T(8,128)(2,1)}, u32[]{:S(2)}, u32[]{:S(2)}) collective-permute-start(bf16[128,2560]{1,0:T(8,128)(2,1)} %copy-done.7), channel_id=1, source_target_pairs={{0,12},{1,13},{16,28},{17,29},{32,44},{33,45},{48,60},{49,61},{64,... | collective-permute-start | bytes 1966088 | tf_op jit(solution)/shard_map/ppermute | solution.py:44
  45.1 10.4 %copy-start = (bf16[384,2560]{1,0:T(8,128)(2,1)}, bf16[384,2560]{1,0:T(8,128)(2,1)S(1)}, u32[]{:S(2)}) copy-start(bf16[384,2560]{1,0:T(8,128)(2,1)S(1)} %constant_dynamic-update-slice_fusion.3.refs_3_.refs_2_) | copy-start | bytes 5898244
  45.1 10.4 %collective-permute-start.8 = (bf16[384,2560]{1,0:T(8,128)(2,1)S(1)}, bf16[384,2560]{1,0:T(8,128)(2,1)}, u32[]{:S(2)}, u32[]{:S(2)}) collective-permute-start(bf16[384,2560]{1,0:T(8,128)(2,1)S(1)} %constant_dynamic-update-slice_fusion.3.refs_3_.refs_2_), channel_id=1, source_target_pairs={{0,1},{1,0},{16,17},{17,16},{32,33},{33,32},{48,49},{49,48},{64,65... | collective-permute-start | bytes 5898248 | tf_op jit(solution)/shard_map/ppermute | solution.py:44
  45.2 19.0 %collective-permute-start.10 = (bf16[48,2560]{1,0:T(8,128)(2,1)S(1)}, bf16[48,2560]{1,0:T(8,128)(2,1)S(1)}, u32[]{:S(2)}, u32[]{:S(2)}) collective-permute-start(bf16[48,2560]{1,0:T(8,128)(2,1)S(1)} %slice.29), channel_id=1, source_target_pairs={{0,12},{1,13},{16,28},{17,29},{32,44},{33,45},{48,60},{49,61},{64,... | collective-permute-start | bytes 737288 | tf_op jit(solution)/shard_map/ppermute | solution.py:44
  49.0 15.2 %collective-permute-start.9 = (bf16[48,2560]{1,0:T(8,128)(2,1)S(1)}, bf16[48,2560]{1,0:T(8,128)(2,1)S(1)}, u32[]{:S(2)}, u32[]{:S(2)}) collective-permute-start(bf16[48,2560]{1,0:T(8,128)(2,1)S(1)} %slice.28), channel_id=1, source_target_pairs={{0,4},{1,5},{16,20},{17,21},{32,36},{33,37},{48,52},{49,53},{64,68... | collective-permute-start | bytes 737288 | tf_op jit(solution)/shard_map/ppermute | solution.py:44
  49.0 15.2 %collective-permute-start.11 = (bf16[32,2560]{1,0:T(8,128)(2,1)S(1)}, bf16[32,2560]{1,0:T(8,128)(2,1)S(1)}, u32[]{:S(2)}, u32[]{:S(2)}) collective-permute-start(bf16[32,2560]{1,0:T(8,128)(2,1)S(1)} %slice.30), channel_id=1, source_target_pairs={{0,130},{1,131},{16,146},{17,147},{32,162},{33,163},{48,178},{49,1... | collective-permute-start | bytes 491528 | tf_op jit(solution)/shard_map/ppermute | solution.py:44
  49.4 29.8 %all-to-all-start = ((bf16[16,432,128]{2,1,0:T(8,128)(2,1)}), bf16[16,432,128]{2,1,0:T(8,128)(2,1)}, u32[]{:S(2)}, u32[]{:S(2)}) async-start(bf16[16,432,128]{2,1,0:T(8,128)(2,1)} %bitcast.40), calls=%async_computation | async-start | bytes 3538944 | tf_op jit(solution)/shard_map/all_to_all | solution.py:250
  64.3 2.4 %collective-permute-start.12 = (bf16[128,2560]{1,0:T(8,128)(2,1)S(1)}, bf16[128,2560]{1,0:T(8,128)(2,1)S(1)}, u32[]{:S(2)}, u32[]{:S(2)}) collective-permute-start(bf16[128,2560]{1,0:T(8,128)(2,1)S(1)} %constant_dynamic-update-slice_fusion.6.refs_3_), channel_id=1, source_target_pairs={{0,1},{1,0},{16,17},{17,16},{32,33},{33,32},{48,49},{49,48},{64,65... | collective-permute-start | bytes 1966088 | tf_op jit(solution)/shard_map/ppermute | solution.py:44
  91.4 24.7 %collective-permute-start.13 = (bf16[8,56,1024]{2,1,0:T(8,128)(2,1)}, bf16[8,56,1024]{2,1,0:T(8,128)(2,1)S(1)}, u32[]{:S(2)}, u32[]{:S(2)}) collective-permute-start(bf16[8,56,1024]{2,1,0:T(8,128)(2,1)} %outer.3), channel_id=1, source_target_pairs={{0,128},{1,129},{16,144},{17,145},{32,160},{33,161},{48,176},{49,1... | collective-permute-start | bytes 2752520 | tf_op jit(solution)/shard_map/ppermute | solution.py:44
  100.0 24.7 %all-to-all-start.2 = ((bf16[8,56,512]{2,1,0:T(8,128)(2,1)}), bf16[8,56,512]{2,1,0:T(8,128)(2,1)S(1)}, u32[]{:S(2)}, u32[]{:S(2)}) async-start(bf16[8,56,512]{2,1,0:T(8,128)(2,1)} %outer.4), calls=%async_computation.2 | async-start | bytes 917504 | tf_op jit(solution)/shard_map/all_to_all | solution.py:275
  124.7 29.9 %all-to-all-start.1 = ((bf16[8,56,1024]{2,1,0:T(8,128)(2,1)}), bf16[8,56,1024]{2,1,0:T(8,128)(2,1)S(1)}, u32[]{:S(2)}, u32[]{:S(2)}) async-start(bf16[8,56,1024]{2,1,0:T(8,128)(2,1)} %add_convert_fusion), calls=%async_computation.1 | async-start | bytes 1835008 | tf_op jit(solution)/shard_map/all_to_all | solution.py:275
  128.4 4.0 %collective-permute-start.14 = (bf16[56,256]{1,0:T(8,128)(2,1)S(1)}, bf16[56,256]{1,0:T(8,128)(2,1)S(1)}, u32[]{:S(2)}, u32[]{:S(2)}) collective-permute-start(bf16[56,256]{1,0:T(8,128)(2,1)S(1)} %slice.47), channel_id=1, source_target_pairs={{0,128},{1,129},{16,144},{17,145},{32,160},{33,161},{48,176},{49,1... | collective-permute-start | bytes 86024 | tf_op jit(solution)/shard_map/ppermute | solution.py:44
  154.8 32.3 %copy-start.9 = (bf16[56,1280]{1,0:T(8,128)(2,1)}, bf16[56,1280]{1,0:T(8,128)(2,1)S(1)}, u32[]{:S(2)}) copy-start(bf16[56,1280]{1,0:T(8,128)(2,1)S(1)} %pad_maximum_fusion.refs_2_) | copy-start | bytes 430084
  154.8 5.2 %collective-permute-start.23 = (bf16[56,1280]{1,0:T(8,128)(2,1)S(1)}, bf16[56,1280]{1,0:T(8,128)(2,1)S(1)}, u32[]{:S(2)}, u32[]{:S(2)}) collective-permute-start(bf16[56,1280]{1,0:T(8,128)(2,1)S(1)} %pad_maximum_fusion.refs_2_), channel_id=1, source_target_pairs={{0,128},{1,129},{16,144},{17,145},{32,160},{33,161},{48,176},{49,1... | collective-permute-start | bytes 430088 | tf_op jit(solution)/shard_map/ppermute | solution.py:44
  155.2 6.8 %collective-permute-start.16 = (bf16[56,1280]{1,0:T(8,128)(2,1)S(1)}, bf16[56,1280]{1,0:T(8,128)(2,1)S(1)}, u32[]{:S(2)}, u32[]{:S(2)}) collective-permute-start(bf16[56,1280]{1,0:T(8,128)(2,1)S(1)} %pad_maximum_fusion.refs_2_), channel_id=1, source_target_pairs={{0,112},{1,113},{16,0},{17,1},{32,16},{33,17},{48,32},{49,33},{64,... | collective-permute-start | bytes 430088 | tf_op jit(solution)/shard_map/ppermute | solution.py:44
  155.2 8.0 %collective-permute-start.15 = (bf16[56,1280]{1,0:T(8,128)(2,1)S(1)}, bf16[56,1280]{1,0:T(8,128)(2,1)S(1)}, u32[]{:S(2)}, u32[]{:S(2)}) collective-permute-start(bf16[56,1280]{1,0:T(8,128)(2,1)S(1)} %pad_maximum_fusion.refs_2_), channel_id=1, source_target_pairs={{0,16},{1,17},{16,32},{17,33},{32,48},{33,49},{48,64},{49,65},{64,... | collective-permute-start | bytes 430088 | tf_op jit(solution)/shard_map/ppermute | solution.py:44
  160.0 27.1 %copy-start.14 = (bf16[56,1280]{1,0:T(8,128)(2,1)}, bf16[56,1280]{1,0:T(8,128)(2,1)S(1)}, u32[]{:S(2)}) copy-start(bf16[56,1280]{1,0:T(8,128)(2,1)S(1)} %collective-permute-done.23.refs_11_) | copy-start | bytes 430084
  160.0 5.7 %collective-permute-start.25 = (bf16[56,1280]{1,0:T(8,128)(2,1)S(1)}, bf16[56,1280]{1,0:T(8,128)(2,1)S(1)}, u32[]{:S(2)}, u32[]{:S(2)}) collective-permute-start(bf16[56,1280]{1,0:T(8,128)(2,1)S(1)} %collective-permute-done.23.refs_11_), channel_id=1, source_target_pairs={{0,112},{1,113},{16,0},{17,1},{32,16},{33,17},{48,32},{49,33},{64,... | collective-permute-start | bytes 430088 | tf_op jit(solution)/shard_map/ppermute | solution.py:44
  160.0 7.5 %collective-permute-start.24 = (bf16[56,1280]{1,0:T(8,128)(2,1)S(1)}, bf16[56,1280]{1,0:T(8,128)(2,1)S(1)}, u32[]{:S(2)}, u32[]{:S(2)}) collective-permute-start(bf16[56,1280]{1,0:T(8,128)(2,1)S(1)} %collective-permute-done.23.refs_11_), channel_id=1, source_target_pairs={{0,16},{1,17},{16,32},{17,33},{32,48},{33,49},{48,64},{49,65},{64,... | collective-permute-start | bytes 430088 | tf_op jit(solution)/shard_map/ppermute | solution.py:44
  162.0 25.0 %copy-start.15 = (bf16[56,1280]{1,0:T(8,128)(2,1)}, bf16[56,1280]{1,0:T(8,128)(2,1)S(1)}, u32[]{:S(2)}) copy-start(bf16[56,1280]{1,0:T(8,128)(2,1)S(1)} %collective-permute-done.16.refs_4_) | copy-start | bytes 430084
  162.0 6.7 %collective-permute-start.18 = (bf16[56,1280]{1,0:T(8,128)(2,1)S(1)}, bf16[56,1280]{1,0:T(8,128)(2,1)S(1)}, u32[]{:S(2)}, u32[]{:S(2)}) collective-permute-start(bf16[56,1280]{1,0:T(8,128)(2,1)S(1)} %collective-permute-done.16.refs_4_), channel_id=1, source_target_pairs={{0,112},{1,113},{16,0},{17,1},{32,16},{33,17},{48,32},{49,33},{64,... | collective-permute-start | bytes 430088 | tf_op jit(solution)/shard_map/ppermute | solution.py:44
  163.2 23.8 %copy-start.16 = (bf16[56,1280]{1,0:T(8,128)(2,1)}, bf16[56,1280]{1,0:T(8,128)(2,1)S(1)}, u32[]{:S(2)}) copy-start(bf16[56,1280]{1,0:T(8,128)(2,1)S(1)} %collective-permute-done.15.refs_3_) | copy-start | bytes 430084
  163.2 7.5 %collective-permute-start.17 = (bf16[56,1280]{1,0:T(8,128)(2,1)S(1)}, bf16[56,1280]{1,0:T(8,128)(2,1)S(1)}, u32[]{:S(2)}, u32[]{:S(2)}) collective-permute-start(bf16[56,1280]{1,0:T(8,128)(2,1)S(1)} %collective-permute-done.15.refs_3_), channel_id=1, source_target_pairs={{0,16},{1,17},{16,32},{17,33},{32,48},{33,49},{48,64},{49,65},{64,... | collective-permute-start | bytes 430088 | tf_op jit(solution)/shard_map/ppermute | solution.py:44
  165.6 21.4 %copy-start.17 = (bf16[56,1280]{1,0:T(8,128)(2,1)}, bf16[56,1280]{1,0:T(8,128)(2,1)S(1)}, u32[]{:S(2)}) copy-start(bf16[56,1280]{1,0:T(8,128)(2,1)S(1)} %collective-permute-done.25.refs_13_) | copy-start | bytes 430084
  165.6 6.5 %collective-permute-start.27 = (bf16[56,1280]{1,0:T(8,128)(2,1)S(1)}, bf16[56,1280]{1,0:T(8,128)(2,1)S(1)}, u32[]{:S(2)}, u32[]{:S(2)}) collective-permute-start(bf16[56,1280]{1,0:T(8,128)(2,1)S(1)} %collective-permute-done.25.refs_13_), channel_id=1, source_target_pairs={{0,112},{1,113},{16,0},{17,1},{32,16},{33,17},{48,32},{49,33},{64,... | collective-permute-start | bytes 430088 | tf_op jit(solution)/shard_map/ppermute | solution.py:44
  167.5 19.6 %copy-start.18 = (bf16[56,1280]{1,0:T(8,128)(2,1)}, bf16[56,1280]{1,0:T(8,128)(2,1)S(1)}, u32[]{:S(2)}) copy-start(bf16[56,1280]{1,0:T(8,128)(2,1)S(1)} %collective-permute-done.24.refs_12_) | copy-start | bytes 430084
  167.5 7.1 %collective-permute-start.26 = (bf16[56,1280]{1,0:T(8,128)(2,1)S(1)}, bf16[56,1280]{1,0:T(8,128)(2,1)S(1)}, u32[]{:S(2)}, u32[]{:S(2)}) collective-permute-start(bf16[56,1280]{1,0:T(8,128)(2,1)S(1)} %collective-permute-done.24.refs_12_), channel_id=1, source_target_pairs={{0,16},{1,17},{16,32},{17,33},{32,48},{33,49},{48,64},{49,65},{64,... | collective-permute-start | bytes 430088 | tf_op jit(solution)/shard_map/ppermute | solution.py:44
  168.7 18.4 %copy-start.19 = (bf16[56,1280]{1,0:T(8,128)(2,1)}, bf16[56,1280]{1,0:T(8,128)(2,1)S(1)}, u32[]{:S(2)}) copy-start(bf16[56,1280]{1,0:T(8,128)(2,1)S(1)} %collective-permute-done.18.refs_6_) | copy-start | bytes 430084
  168.7 6.4 %collective-permute-start.20 = (bf16[56,1280]{1,0:T(8,128)(2,1)S(1)}, bf16[56,1280]{1,0:T(8,128)(2,1)S(1)}, u32[]{:S(2)}, u32[]{:S(2)}) collective-permute-start(bf16[56,1280]{1,0:T(8,128)(2,1)S(1)} %collective-permute-done.18.refs_6_), channel_id=1, source_target_pairs={{0,112},{1,113},{16,0},{17,1},{32,16},{33,17},{48,32},{49,33},{64,... | collective-permute-start | bytes 430088 | tf_op jit(solution)/shard_map/ppermute | solution.py:44
  170.7 16.4 %copy-start.20 = (bf16[56,1280]{1,0:T(8,128)(2,1)}, bf16[56,1280]{1,0:T(8,128)(2,1)S(1)}, u32[]{:S(2)}) copy-start(bf16[56,1280]{1,0:T(8,128)(2,1)S(1)} %collective-permute-done.17.refs_5_) | copy-start | bytes 430084
  170.7 7.2 %collective-permute-start.19 = (bf16[56,1280]{1,0:T(8,128)(2,1)S(1)}, bf16[56,1280]{1,0:T(8,128)(2,1)S(1)}, u32[]{:S(2)}, u32[]{:S(2)}) collective-permute-start(bf16[56,1280]{1,0:T(8,128)(2,1)S(1)} %collective-permute-done.17.refs_5_), channel_id=1, source_target_pairs={{0,16},{1,17},{16,32},{17,33},{32,48},{33,49},{48,64},{49,65},{64,... | collective-permute-start | bytes 430088 | tf_op jit(solution)/shard_map/ppermute | solution.py:44
  172.1 15.0 %copy-start.21 = (bf16[56,1280]{1,0:T(8,128)(2,1)}, bf16[56,1280]{1,0:T(8,128)(2,1)S(1)}, u32[]{:S(2)}) copy-start(bf16[56,1280]{1,0:T(8,128)(2,1)S(1)} %collective-permute-done.27.refs_15_) | copy-start | bytes 430084
  172.1 5.9 %collective-permute-start.29 = (bf16[56,1280]{1,0:T(8,128)(2,1)S(1)}, bf16[56,1280]{1,0:T(8,128)(2,1)S(1)}, u32[]{:S(2)}, u32[]{:S(2)}) collective-permute-start(bf16[56,1280]{1,0:T(8,128)(2,1)S(1)} %collective-permute-done.27.refs_15_), channel_id=1, source_target_pairs={{0,112},{1,113},{16,0},{17,1},{32,16},{33,17},{48,32},{49,33},{64,... | collective-permute-start | bytes 430088 | tf_op jit(solution)/shard_map/ppermute | solution.py:44
  174.6 12.5 %copy-start.22 = (bf16[56,1280]{1,0:T(8,128)(2,1)}, bf16[56,1280]{1,0:T(8,128)(2,1)S(1)}, u32[]{:S(2)}) copy-start(bf16[56,1280]{1,0:T(8,128)(2,1)S(1)} %collective-permute-done.26.refs_14_) | copy-start | bytes 430084
  174.6 6.8 %collective-permute-start.28 = (bf16[56,1280]{1,0:T(8,128)(2,1)S(1)}, bf16[56,1280]{1,0:T(8,128)(2,1)S(1)}, u32[]{:S(2)}, u32[]{:S(2)}) collective-permute-start(bf16[56,1280]{1,0:T(8,128)(2,1)S(1)} %collective-permute-done.26.refs_14_), channel_id=1, source_target_pairs={{0,16},{1,17},{16,32},{17,33},{32,48},{33,49},{48,64},{49,65},{64,... | collective-permute-start | bytes 430088 | tf_op jit(solution)/shard_map/ppermute | solution.py:44
  175.1 12.1 %copy-start.10 = (bf16[56,1280]{1,0:T(8,128)(2,1)}, bf16[56,1280]{1,0:T(8,128)(2,1)S(1)}, u32[]{:S(2)}) copy-start(bf16[56,1280]{1,0:T(8,128)(2,1)S(1)} %collective-permute-done.20.refs_8_) | copy-start | bytes 430084
  175.1 6.4 %collective-permute-start.22 = (bf16[56,640]{1,0:T(8,128)(2,1)S(1)}, bf16[56,640]{1,0:T(8,128)(2,1)S(1)}, u32[]{:S(2)}, u32[]{:S(2)}) collective-permute-start(bf16[56,640]{1,0:T(8,128)(2,1)S(1)} %slice.40), channel_id=1, source_target_pairs={{0,112},{1,113},{16,0},{17,1},{32,16},{33,17},{48,32},{49,33},{64,... | collective-permute-start | bytes 215048 | tf_op jit(solution)/shard_map/ppermute | solution.py:44
  177.9 9.2 %copy-start.11 = (bf16[56,1280]{1,0:T(8,128)(2,1)}, bf16[56,1280]{1,0:T(8,128)(2,1)S(1)}, u32[]{:S(2)}) copy-start(bf16[56,1280]{1,0:T(8,128)(2,1)S(1)} %collective-permute-done.19.refs_7_) | copy-start | bytes 430084
  177.9 5.6 %collective-permute-start.21 = (bf16[56,640]{1,0:T(8,128)(2,1)S(1)}, bf16[56,640]{1,0:T(8,128)(2,1)S(1)}, u32[]{:S(2)}, u32[]{:S(2)}) collective-permute-start(bf16[56,640]{1,0:T(8,128)(2,1)S(1)} %slice.39), channel_id=1, source_target_pairs={{0,16},{1,17},{16,32},{17,33},{32,48},{33,49},{48,64},{49,65},{64,... | collective-permute-start | bytes 215048 | tf_op jit(solution)/shard_map/ppermute | solution.py:44
  178.1 5.5 %collective-permute-start.31 = (bf16[56,640]{1,0:T(8,128)(2,1)S(1)}, bf16[56,640]{1,0:T(8,128)(2,1)S(1)}, u32[]{:S(2)}, u32[]{:S(2)}) collective-permute-start(bf16[56,640]{1,0:T(8,128)(2,1)S(1)} %slice.42), channel_id=1, source_target_pairs={{0,112},{1,113},{16,0},{17,1},{32,16},{33,17},{48,32},{49,33},{64,... | collective-permute-start | bytes 215048 | tf_op jit(solution)/shard_map/ppermute | solution.py:44
  181.4 5.6 %collective-permute-start.30 = (bf16[56,640]{1,0:T(8,128)(2,1)S(1)}, bf16[56,640]{1,0:T(8,128)(2,1)S(1)}, u32[]{:S(2)}, u32[]{:S(2)}) collective-permute-start(bf16[56,640]{1,0:T(8,128)(2,1)S(1)} %slice.41), channel_id=1, source_target_pairs={{0,16},{1,17},{16,32},{17,33},{32,48},{33,49},{48,64},{49,65},{64,... | collective-permute-start | bytes 215048 | tf_op jit(solution)/shard_map/ppermute | solution.py:44
  (14 other events, 48.7 us)

commit v2 on v1

--- a/solution.py
+++ b/solution.py
@@ -9,6 +9,7 @@
 NX, NY, NZ, NC = 4, 4, 8, 2
 F32, BF16 = jnp.float32, jnp.bfloat16
 VMEM_LIMIT = 62_000_000
+VMEM_PART = 28_000_000
 
 PIECE = 56
 
@@ -48,8 +49,8 @@
     return lax.optimization_barrier((*values, *before))[: len(values)]
 
 
-def params():
-    return pltpu.CompilerParams(vmem_limit_bytes=VMEM_LIMIT)
+def params(limit=VMEM_LIMIT):
+    return pltpu.CompilerParams(vmem_limit_bytes=limit)
 
 
 def factor_kernel(weighing, table_ref, gate_ref, probe_ref, *refs):
@@ -104,14 +105,13 @@
             scratch_shapes=[pltpu.VMEM((2 * rows, depth), BF16)],
         ),
         out_shape=jax.ShapeDtypeStruct((2, hidden, total), BF16 if weighing else F32),
-        compiler_params=params(),
+        compiler_params=params(VMEM_PART),
         cost_estimate=pl.CostEstimate(flops=0, bytes_accessed=0, transcendentals=0),
         name="factor",
     )(table, gate_t, probe_t, *[spread, spread] * weighing, *tokens)
 
 
-def weigh_kernel(table_ref, grad_ref, *refs):
-    factor_refs, out_ref = refs[:-1], refs[-1]
+def weigh(table_ref, grad_ref, factor_refs, out_ref):
     for side in range(2):
         at = 0
         for factor_ref in factor_refs:
@@ -120,28 +120,6 @@
                 to = (side * 8 + at) * 128
                 out_ref[:, to : to + 128] = (grad * factor_ref[side, :, k : k + 128]).astype(BF16)
                 at += 1
-
-
-def weigh(table, spread, factors):
-    _, hidden, _ = factors[0].shape
-    block = hidden // 3
-    return pl.pallas_call(
-        weigh_kernel,
-        grid_spec=pltpu.PrefetchScalarGridSpec(
-            num_scalar_prefetch=1,
-            grid=(3,),
-            in_specs=[pl.BlockSpec((16, block, 128), lambda i, o: (0, i, 0))]
-            + [pl.BlockSpec((2, block, f.shape[2]), lambda i, o: (0, i, 0)) for f in factors],
-            out_specs=pl.BlockSpec((block, 2048), lambda i, o: (i, 0)),
-        ),
-        out_shape=jax.ShapeDtypeStruct((hidden, 2048), BF16),
-        compiler_params=params(),
-        name="weigh",
-    )(table, spread, *factors)
-
-
-def starts():
-    return [min(PIECE * k, 432 - PIECE) for k in range(NZ)]
 
 
 def outer_kernel(table_ref, weighted_ref, *refs):
@@ -155,26 +133,42 @@
         out_ref[k] = total[row : row + PIECE, :].astype(out_ref.dtype)
 
 
-def outer(table, first, weighted, tokens, width, dtype):
-    wide = 256
-    hidden, depth = weighted.shape
+def weigh_outer_kernel(table_ref, grad_ref, *refs):
+    factor_refs, weighted_ref = refs[:3], refs[-3]
+    pl.when(pl.program_id(0) == 0)(lambda: weigh(table_ref, grad_ref, factor_refs, weighted_ref))
+    outer_kernel(table_ref, weighted_ref, *refs[3:-3], refs[-2], refs[-1])
+
+
+def starts():
+    return [min(PIECE * k, 432 - PIECE) for k in range(NZ)]
+
+
+def outer(table, first, weighted, tokens, width, dtype, wide):
+    whole = lambda a: pl.BlockSpec(a.shape, lambda j, c: (0,) * a.ndim)
+    make = isinstance(weighted, tuple)
+    operands = weighted if make else (weighted,)
+    hidden, depth = operands[0].shape[-2 if make else 0], 2048
+    made = [(pl.BlockSpec((hidden, depth), lambda j, c: (0, 0)), jax.ShapeDtypeStruct((hidden, depth), BF16))] * make
+    outs = made + [
+        (pl.BlockSpec((NZ, PIECE, wide), lambda j, c: (0, 0, j)), jax.ShapeDtypeStruct((NZ, PIECE, width), dtype))
+    ]
     return pl.pallas_call(
-        outer_kernel,
+        weigh_outer_kernel if make else outer_kernel,
         grid_spec=pltpu.PrefetchScalarGridSpec(
             num_scalar_prefetch=1,
             grid=(width // wide,),
-            in_specs=[pl.BlockSpec(weighted.shape, lambda j, c: (0, 0))]
+            in_specs=[whole(a) for a in operands]
             + [pl.BlockSpec((t.shape[0], wide), lambda j, c: (0, c[first + j])) for t in tokens],
-            out_specs=pl.BlockSpec((NZ, PIECE, wide), lambda j, c: (0, 0, j)),
+            out_specs=[spec for spec, _ in outs],
             scratch_shapes=[pltpu.VMEM((depth, wide), BF16)],
         ),
-        out_shape=jax.ShapeDtypeStruct((NZ, PIECE, width), dtype),
+        out_shape=[shape for _, shape in outs],
         compiler_params=params(),
         cost_estimate=pl.CostEstimate(
             flops=2 * hidden * depth * width, bytes_accessed=2 * depth * width + 2 * hidden * depth, transcendentals=0
         ),
         name="outer",
-    )(table, weighted, *tokens)
+    )(table, *operands, *tokens)
 
 
 LOW = 27
@@ -221,7 +215,7 @@
             out_specs=pl.BlockSpec((hidden, wide), column),
         ),
         out_shape=jax.ShapeDtypeStruct(probe_t.shape, F32),
-        compiler_params=params(),
+        compiler_params=params(VMEM_PART),
         name="finish",
     )(table, probe_t, *sides[0], *sides[1])
 
@@ -268,19 +262,20 @@
     corner = jnp.concatenate(last, 0)
     core_corner = send(corner, CORE)
     weight_2 = factor(table, 14, gate_t, probe_t, None, corner, core_corner)
-    weighted = weigh(table, spread, (weight_0, weight_1, weight_2))
 
     pieces = (tokens, ring, far, corner, core_tokens, core_ring, core_far, core_corner)
     half = rest * 256
     ring_sum = lambda a: lax.all_to_all(
         a, AXES, split_axis=0, concat_axis=0, axis_index_groups=Z_RINGS, tiled=True
     ).astype(F32).sum(0)
-    away = outer(table, 16 + 2 * rest, weighted, pieces, first * 256, BF16)
+    weighted, away = outer(
+        table, 16 + 2 * rest, (spread, weight_0, weight_1, weight_2), pieces, first * 256, BF16, 256
+    )
     come = send(away, Y_CUT)
     (table,) = after((table,), away)
-    late = outer(table, 16, weighted, pieces, 2 * half, BF16)
+    (late,) = outer(table, 16, weighted, pieces, 2 * half, BF16, 256)
     (table,) = after((table,), late)
-    own = outer(table, 16 + 2 * rest + first, weighted, pieces, first * 256, F32)
+    (own,) = outer(table, 16 + 2 * rest + first, weighted, pieces, first * 256, F32, 256)
     late = ring_sum(late)
     own = ring_sum((own + come.astype(F32)).astype(BF16))
     late = late[:, half:] + send(late[:, :half].astype(BF16), Y_CUT).astype(F32)

time: 195 us -> 186 us (0.954)
  Pallas kernels: 54.9 us -> 39.7 us
  waiting for transfers between devices: 66.9 us -> 73.1 us
    pallas_call x3, Pallas kernels: 24.8 us -> 15 us  [factor(): pl.pallas_call(lambda *refs: factor_kernel(weighing, *refs), grid_spec=pl...]
    ppermute x32, waiting for transfers between devices: 32.5 us -> 38 us  [send(): return lax.ppermute(value, AXES, pairs)]
    pallas_call x4 -> x3, Pallas kernels: 24.1 us -> 20.8 us  [outer(): pl.pallas_call(weigh_outer_kernel if make else outer_kernel, grid_spec=pl...]
    unnamed x60 -> x42, local copies, waits for them, and re-layouts: 5.75 us -> 7.37 us
  transfers between devices with their start and end apart: 35 -> 35, of which waited for: 19 -> 20; matrix products, arithmetic and copies ran while one was open for 4% -> 4% of each run, Pallas kernels for 19% -> 15%
where the time goes in v2:
time: 186 us; the launch traced here: 185 us
  waiting for transfers between devices  73.1 us (39%)
  starting transfers between devices  56.2 us (30%)
  Pallas kernels  39.7 us (21%)
  local copies, waits for them, and re-layouts  11.6 us (6%)
  other arithmetic  4 us (2%)
    ppermute x32, starting transfers between devices, send(): return lax.ppermute(value, AXES, pairs)  38.1 us
    ppermute x32, waiting for transfers between devices, send(): return lax.ppermute(value, AXES, pairs)  38 us
    all_to_all x2, waiting for transfers between devices, on_device(): lax.all_to_all(a, AXES, split_axis=0, concat_axis=0, axis_index_groups=Z_...  27.1 us
    pallas_call x3, Pallas kernels, outer(): pl.pallas_call(weigh_outer_kernel if make else outer_kernel, grid_spec=pl...  20.8 us
    pallas_call x3, Pallas kernels, factor(): pl.pallas_call(lambda *refs: factor_kernel(weighing, *refs), grid_spec=pl...  15 us
    all_to_all x2, starting transfers between devices, on_device(): lax.all_to_all(a, AXES, split_axis=0, concat_axis=0, axis_index_groups=Z_...  12 us
    all_to_all x1, waiting for transfers between devices, on_device(): lax.all_to_all(turned, AXES, split_axis=0, concat_axis=0, axis_index_grou...  8 us
    unnamed x42, local copies, waits for them, and re-layouts  7.37 us
  transfers between devices with their start and end apart: 35, of which 20 were waited for; matrix products, arithmetic and copies ran while one was open for 4% of the time, Pallas kernels for 15%

profile of v2, /device:TPU:16, one launch (start us, length us, event | category | flops | bytes accessed | tf_op | source)
XLA Modules:
  0.0 185.1 jit_solution(574022509160527679)
XLA Ops:
  0.5 2.8 %collective-permute-start.1 = (bf16[128,2560]{1,0:T(8,128)(2,1)}, bf16[128,2560]{1,0:T(8,128)(2,1)S(1)}, u32[]{:S(2)}, u32[]{:S(2)}) collective-permute-start(bf16[128,2560]{1,0:T(8,128)(2,1)} %refs_0_.3), channel_id=1, source_target_pairs={{0,12},{1,13},{16,28},{17,29},{32,44},{33,45},{48,60},{49,61},{64,... | collective-permute-start | bytes 1966088 | tf_op jit(solution)/shard_map/ppermute | solution.py:45
  3.2 4.0 %copy.5 = bf16[6912,128]{1,0:T(8,128)(2,1)} copy(bf16[6912,128]{0,1:T(8,128)(2,1)} %bitcast.41) | data formatting | bytes 3538944 | tf_op jit(solution)/shard_map/transpose | solution.py:241
  7.3 9.4 %collective-permute-done.2 = bf16[128,2560]{1,0:T(8,128)(2,1)S(1)} collective-permute-done((bf16[128,2560]{1,0:T(8,128)(2,1)}, bf16[128,2560]{1,0:T(8,128)(2,1)S(1)}, u32[]{:S(2)}, u32[]{:S(2)}) %collective-permute-start.2) | collective-permute-done | bytes 655392 | tf_op jit(solution)/shard_map/ppermute | solution.py:45
  17.2 3.4 %collective-permute-done = bf16[128,2560]{1,0:T(8,128)(2,1)} collective-permute-done((bf16[128,2560]{1,0:T(8,128)(2,1)}, bf16[128,2560]{1,0:T(8,128)(2,1)}, u32[]{:S(2)}, u32[]{:S(2)}) %collective-permute-start) | collective-permute-done | bytes 655392 | tf_op jit(solution)/shard_map/ppermute | solution.py:45
  20.7 1.3 constant_dynamic-update-slice_fusion.2
  22.7 1.6 collective-permute-start.7
  24.2 3.2 %collective-permute-start.6 = (bf16[128,2560]{1,0:T(8,128)(2,1)S(1)}, bf16[128,2560]{1,0:T(8,128)(2,1)S(1)}, u32[]{:S(2)}, u32[]{:S(2)}) collective-permute-start(bf16[128,2560]{1,0:T(8,128)(2,1)S(1)} %collective-permute-done.1), channel_id=1, source_target_pairs={{0,12},{1,13},{16,28},{17,29},{32,44},{33,45},{48,60},{49,61},{64,... | collective-permute-start | bytes 1966088 | tf_op jit(solution)/shard_map/ppermute | solution.py:45
  27.5 6.9 %factor.3.refs_0_ = f32[2,432,512]{2,1,0:T(8,128)S(1)} custom-call(s32[28]{0:T(128)S(1)} %stack.115.refs_0_.table_ref, bf16[432,2560]{1,0:T(8,128)(2,1)S(1)} %bitcast.37, bf16[432,2560]{1,0:T(8,128)(2,1)S(1)} %bitcast.33, bf16[128,2560]{1,0:T(8,128)(2,1)S(1)} %copy-done.9, bf16[128,2560]{1,0:T(8,128)(2,1)S(1)} %collective-permute-done.3.refs_4_.refs_7_, ...), custom_call_target="tpu_custom_call" | custom-call | tf_op jit(solution)/shard_map/factor/pallas_call | solution.py:91
  34.5 6.1 %collective-permute-done.5 = bf16[128,2560]{1,0:T(8,128)(2,1)S(1)} collective-permute-done((bf16[128,2560]{1,0:T(8,128)(2,1)S(1)}, bf16[128,2560]{1,0:T(8,128)(2,1)S(1)}, u32[]{:S(2)}, u32[]{:S(2)}) %collective-permute-start.5) | collective-permute-done | bytes 655392 | tf_op jit(solution)/shard_map/ppermute | solution.py:45
  41.5 3.8 %collective-permute-start.10 = (bf16[48,2560]{1,0:T(8,128)(2,1)S(1)}, bf16[48,2560]{1,0:T(8,128)(2,1)S(1)}, u32[]{:S(2)}, u32[]{:S(2)}) collective-permute-start(bf16[48,2560]{1,0:T(8,128)(2,1)S(1)} %slice.29), channel_id=1, source_target_pairs={{0,12},{1,13},{16,28},{17,29},{32,44},{33,45},{48,60},{49,61},{64,... | collective-permute-start | bytes 737288 | tf_op jit(solution)/shard_map/ppermute | solution.py:45
  45.7 6.1 %all-to-all-start = ((bf16[16,432,128]{2,1,0:T(8,128)(2,1)}), bf16[16,432,128]{2,1,0:T(8,128)(2,1)}, u32[]{:S(2)}, u32[]{:S(2)}) async-start(bf16[16,432,128]{2,1,0:T(8,128)(2,1)} %bitcast.40), calls=%async_computation | async-start | bytes 3538944 | tf_op jit(solution)/shard_map/all_to_all | solution.py:244
  51.9 1.6 copy-done.3
  53.5 1.6 copy-done.7
  55.1 6.1 %factor.4.refs_1_ = f32[2,432,384]{2,1,0:T(8,128)S(1)} custom-call(s32[28]{0:T(128)S(1)} %stack.115.refs_0_.table_ref, bf16[432,2560]{1,0:T(8,128)(2,1)S(1)} %bitcast.38, bf16[432,2560]{1,0:T(8,128)(2,1)S(1)} %bitcast.34, bf16[384,2560]{1,0:T(8,128)(2,1)S(1)} %constant_dynamic-update-slice_fusion.3.refs_3_.refs_5_.refs_2_, ...), custom_call_target="tpu_custom_call" | custom-call | tf_op jit(solution)/shard_map/factor/pallas_call | solution.py:91
  61.2 1.1 copy-done.13
  62.8 1.9 %collective-permute-done.12.refs_4_.refs_10_.refs_7_ = bf16[128,2560]{1,0:T(8,128)(2,1)S(1)} collective-permute-done((bf16[128,2560]{1,0:T(8,128)(2,1)S(1)}, bf16[128,2560]{1,0:T(8,128)(2,1)S(1)}, u32[]{:S(2)}, u32[]{:S(2)}) %collective-permute-start.12) | collective-permute-done | bytes 655392 | tf_op jit(solution)/shard_map/ppermute | solution.py:45
  64.8 2.0 %factor.5.refs_2_ = f32[2,432,128]{2,1,0:T(8,128)S(1)} custom-call(s32[28]{0:T(128)S(1)} %stack.115.refs_0_.table_ref, bf16[432,2560]{1,0:T(8,128)(2,1)S(1)} %bitcast.39, bf16[432,2560]{1,0:T(8,128)(2,1)S(1)} %bitcast.35, bf16[128,2560]{1,0:T(8,128)(2,1)S(1)} %constant_dynamic-update-slice_fusion.6.refs_3_.refs_6_, ...), custom_call_target="tpu_custom_call" | custom-call | tf_op jit(solution)/shard_map/factor/pallas_call | solution.py:91
  66.8 0.8 copy-done.14
  67.6 8.0 %all-to-all-done.grad_ref = bf16[16,432,128]{2,1,0:T(8,128)(2,1)} async-done(((bf16[16,432,128]{2,1,0:T(8,128)(2,1)}), bf16[16,432,128]{2,1,0:T(8,128)(2,1)}, u32[]{:S(2)}, u32[]{:S(2)}) %all-to-all-start) | async-done | bytes 1769504 | tf_op jit(solution)/shard_map/all_to_all | solution.py:244
  75.6 8.7 %outer.3 = (bf16[432,2048]{1,0:T(8,128)(2,1)}, bf16[8,56,1024]{2,1,0:T(8,128)(2,1)}) custom-call(s32[28]{0:T(128)} %copy-done.15, bf16[16,432,128]{2,1,0:T(8,128)(2,1)} %all-to-all-done.grad_ref, f32[2,432,512]{2,1,0:T(8,128)} %copy-done.12, f32[2,432,384]{2,1,0:T(8,128)} %copy-done.13, f32[2,432,128]{2,1,0:T(8,128)} %copy-done.14, ...), custom_call_target="tpu_custom_call" | custom-call | flops 1811939328 | bytes 5963776 | tf_op jit(solution)/shard_map/outer/pallas_call | solution.py:155
  84.3 3.8 %collective-permute-start.13 = (bf16[8,56,1024]{2,1,0:T(8,128)(2,1)}, bf16[8,56,1024]{2,1,0:T(8,128)(2,1)S(1)}, u32[]{:S(2)}, u32[]{:S(2)}) collective-permute-start(bf16[8,56,1024]{2,1,0:T(8,128)(2,1)} %get-tuple-element.35), channel_id=1, source_target_pairs={{0,128},{1,129},{16,144},{17,145},{32,160},{33,161},{48,176},{49,1... | collective-permute-start | bytes 2752520 | tf_op jit(solution)/shard_map/ppermute | solution.py:45
  88.1 4.9 %outer.4 = bf16[8,56,512]{2,1,0:T(8,128)(2,1)} custom-call(s32[28]{0:T(128)} %copy-done.15, bf16[432,2048]{1,0:T(8,128)(2,1)} %get-tuple-element.37.weighted_ref, bf16[128,2560]{1,0:T(8,128)(2,1)} %refs_0_.3, bf16[384,2560]{1,0:T(8,128)(2,1)} %copy-done.1, bf16[384,2560]{1,0:T(8,128)(2,1)} %copy-done, bf16[128,2560]{1,0:T(8,128)(2,1)} %copy-done.8, ...), custom_call_target="tpu_custom_call" | custom-call | flops 905969664 | bytes 3866624 | tf_op jit(solution)/shard_map/outer/pallas_call | solution.py:155
  93.0 8.5 %all-to-all-start.2 = ((bf16[8,56,512]{2,1,0:T(8,128)(2,1)}), bf16[8,56,512]{2,1,0:T(8,128)(2,1)S(1)}, u32[]{:S(2)}, u32[]{:S(2)}) async-start(bf16[8,56,512]{2,1,0:T(8,128)(2,1)} %outer.4), calls=%async_computation.2 | async-start | bytes 917504 | tf_op jit(solution)/shard_map/all_to_all | solution.py:268
  101.5 7.1 %outer.5 = f32[8,56,1024]{2,1,0:T(8,128)} custom-call(s32[28]{0:T(128)} %copy-done.15, bf16[432,2048]{1,0:T(8,128)(2,1)} %get-tuple-element.37.weighted_ref, bf16[128,2560]{1,0:T(8,128)(2,1)} %refs_0_.3, bf16[384,2560]{1,0:T(8,128)(2,1)} %copy-done.1, bf16[384,2560]{1,0:T(8,128)(2,1)} %copy-done, bf16[128,2560]{1,0:T(8,128)(2,1)} %copy-done.8, ...), custom_call_target="tpu_custom_call" | custom-call | flops 1811939328 | bytes 5963776 | tf_op jit(solution)/shard_map/outer/pallas_call | solution.py:155
  109.1 2.7 %add_convert_fusion = bf16[8,56,1024]{2,1,0:T(8,128)(2,1)} fusion(f32[8,56,1024]{2,1,0:T(8,128)} %outer.5, bf16[8,56,1024]{2,1,0:T(8,128)(2,1)S(1)} %collective-permute-done.13), kind=kLoop, calls=%fused_computation | loop fusion | flops 1376256 | bytes 3670016 | tf_op jit(solution)/shard_map/convert_element_type | solution.py:280
  111.8 5.9 %all-to-all-done.2 = bf16[8,56,512]{2,1,0:T(8,128)(2,1)S(1)} async-done(((bf16[8,56,512]{2,1,0:T(8,128)(2,1)}), bf16[8,56,512]{2,1,0:T(8,128)(2,1)S(1)}, u32[]{:S(2)}, u32[]{:S(2)}) %all-to-all-start.2) | async-done | bytes 458784 | tf_op jit(solution)/shard_map/all_to_all | solution.py:268
  117.8 0.8 copy-done.17
  118.5 3.6 %all-to-all-start.1 = ((bf16[8,56,1024]{2,1,0:T(8,128)(2,1)}), bf16[8,56,1024]{2,1,0:T(8,128)(2,1)S(1)}, u32[]{:S(2)}, u32[]{:S(2)}) async-start(bf16[8,56,1024]{2,1,0:T(8,128)(2,1)} %add_convert_fusion), calls=%async_computation.1 | async-start | bytes 1835008 | tf_op jit(solution)/shard_map/all_to_all | solution.py:268
  122.1 1.1 convert_reduce_fusion
  123.2 1.0 collective-permute-start.14
  124.2 3.0 %collective-permute-done.14 = bf16[56,256]{1,0:T(8,128)(2,1)S(1)} collective-permute-done((bf16[56,256]{1,0:T(8,128)(2,1)S(1)}, bf16[56,256]{1,0:T(8,128)(2,1)S(1)}, u32[]{:S(2)}, u32[]{:S(2)}) %collective-permute-start.14) | collective-permute-done | bytes 28704 | tf_op jit(solution)/shard_map/ppermute | solution.py:45
  127.2 21.2 %all-to-all-done.1 = bf16[8,56,1024]{2,1,0:T(8,128)(2,1)S(1)} async-done(((bf16[8,56,1024]{2,1,0:T(8,128)(2,1)}), bf16[8,56,1024]{2,1,0:T(8,128)(2,1)S(1)}, u32[]{:S(2)}, u32[]{:S(2)}) %all-to-all-start.1) | async-done | bytes 917536 | tf_op jit(solution)/shard_map/all_to_all | solution.py:268
  149.0 2.0 %collective-permute-start.15 = (bf16[56,1280]{1,0:T(8,128)(2,1)S(1)}, bf16[56,1280]{1,0:T(8,128)(2,1)S(1)}, u32[]{:S(2)}, u32[]{:S(2)}) collective-permute-start(bf16[56,1280]{1,0:T(8,128)(2,1)S(1)} %pad_maximum_fusion.refs_2_), channel_id=1, source_target_pairs={{0,16},{1,17},{16,32},{17,33},{32,48},{33,49},{48,64},{49,65},{64,... | collective-permute-start | bytes 430088 | tf_op jit(solution)/shard_map/ppermute | solution.py:45
  151.0 2.8 %collective-permute-done.23.refs_11_ = bf16[56,1280]{1,0:T(8,128)(2,1)S(1)} collective-permute-done((bf16[56,1280]{1,0:T(8,128)(2,1)S(1)}, bf16[56,1280]{1,0:T(8,128)(2,1)S(1)}, u32[]{:S(2)}, u32[]{:S(2)}) %collective-permute-start.23) | collective-permute-done | bytes 143392 | tf_op jit(solution)/shard_map/ppermute | solution.py:45
  153.8 2.0 %collective-permute-start.24 = (bf16[56,1280]{1,0:T(8,128)(2,1)S(1)}, bf16[56,1280]{1,0:T(8,128)(2,1)S(1)}, u32[]{:S(2)}, u32[]{:S(2)}) collective-permute-start(bf16[56,1280]{1,0:T(8,128)(2,1)S(1)} %collective-permute-done.23.refs_11_), channel_id=1, source_target_pairs={{0,16},{1,17},{16,32},{17,33},{32,48},{33,49},{48,64},{49,65},{64,... | collective-permute-start | bytes 430088 | tf_op jit(solution)/shard_map/ppermute | solution.py:45
  155.8 1.2 collective-permute-start.18
  157.0 0.8 collective-permute-start.17
  157.8 1.5 collective-permute-done.25.refs_13_
  159.3 2.0 %collective-permute-start.27 = (bf16[56,1280]{1,0:T(8,128)(2,1)S(1)}, bf16[56,1280]{1,0:T(8,128)(2,1)S(1)}, u32[]{:S(2)}, u32[]{:S(2)}) collective-permute-start(bf16[56,1280]{1,0:T(8,128)(2,1)S(1)} %collective-permute-done.25.refs_13_), channel_id=1, source_target_pairs={{0,112},{1,113},{16,0},{17,1},{32,16},{33,17},{48,32},{49,33},{64,... | collective-permute-start | bytes 430088 | tf_op jit(solution)/shard_map/ppermute | solution.py:45
  161.6 0.8 collective-permute-done.18.refs_6_
  162.4 2.4 %collective-permute-start.20 = (bf16[56,1280]{1,0:T(8,128)(2,1)S(1)}, bf16[56,1280]{1,0:T(8,128)(2,1)S(1)}, u32[]{:S(2)}, u32[]{:S(2)}) collective-permute-start(bf16[56,1280]{1,0:T(8,128)(2,1)S(1)} %collective-permute-done.18.refs_6_), channel_id=1, source_target_pairs={{0,112},{1,113},{16,0},{17,1},{32,16},{33,17},{48,32},{49,33},{64,... | collective-permute-start | bytes 430088 | tf_op jit(solution)/shard_map/ppermute | solution.py:45
  164.8 0.9 collective-permute-done.27.refs_15_
  165.8 2.5 %collective-permute-start.29 = (bf16[56,1280]{1,0:T(8,128)(2,1)S(1)}, bf16[56,1280]{1,0:T(8,128)(2,1)S(1)}, u32[]{:S(2)}, u32[]{:S(2)}) collective-permute-start(bf16[56,1280]{1,0:T(8,128)(2,1)S(1)} %collective-permute-done.27.refs_15_), channel_id=1, source_target_pairs={{0,112},{1,113},{16,0},{17,1},{32,16},{33,17},{48,32},{49,33},{64,... | collective-permute-start | bytes 430088 | tf_op jit(solution)/shard_map/ppermute | solution.py:45
  169.0 3.1 %collective-permute-start.22 = (bf16[56,640]{1,0:T(8,128)(2,1)S(1)}, bf16[56,640]{1,0:T(8,128)(2,1)S(1)}, u32[]{:S(2)}, u32[]{:S(2)}) collective-permute-start(bf16[56,640]{1,0:T(8,128)(2,1)S(1)} %slice.40), channel_id=1, source_target_pairs={{0,112},{1,113},{16,0},{17,1},{32,16},{33,17},{48,32},{49,33},{64,... | collective-permute-start | bytes 215048 | tf_op jit(solution)/shard_map/ppermute | solution.py:45
  172.2 3.3 %collective-permute-start.31 = (bf16[56,640]{1,0:T(8,128)(2,1)S(1)}, bf16[56,640]{1,0:T(8,128)(2,1)S(1)}, u32[]{:S(2)}, u32[]{:S(2)}) collective-permute-start(bf16[56,640]{1,0:T(8,128)(2,1)S(1)} %slice.42), channel_id=1, source_target_pairs={{0,112},{1,113},{16,0},{17,1},{32,16},{33,17},{48,32},{49,33},{64,... | collective-permute-start | bytes 215048 | tf_op jit(solution)/shard_map/ppermute | solution.py:45
  175.6 2.1 %collective-permute-done.21.refs_9_ = bf16[56,640]{1,0:T(8,128)(2,1)S(1)} collective-permute-done((bf16[56,640]{1,0:T(8,128)(2,1)S(1)}, bf16[56,640]{1,0:T(8,128)(2,1)S(1)}, u32[]{:S(2)}, u32[]{:S(2)}) %collective-permute-start.21) | collective-permute-done | bytes 71712 | tf_op jit(solution)/shard_map/ppermute | solution.py:45
  177.7 3.4 %collective-permute-done.30.refs_18_ = bf16[56,640]{1,0:T(8,128)(2,1)S(1)} collective-permute-done((bf16[56,640]{1,0:T(8,128)(2,1)S(1)}, bf16[56,640]{1,0:T(8,128)(2,1)S(1)}, u32[]{:S(2)}, u32[]{:S(2)}) %collective-permute-start.30) | collective-permute-done | bytes 71712 | tf_op jit(solution)/shard_map/ppermute | solution.py:45
  181.1 4.0 %finish.1 = f32[432,2560]{1,0:T(8,128)} custom-call(s32[28]{0:T(128)S(1)} %copy-done.16, bf16[432,2560]{1,0:T(8,128)(2,1)S(1)} %bitcast.36, bf16[56,1280]{1,0:T(8,128)(2,1)S(1)} %pad_maximum_fusion.refs_2_, bf16[56,1280]{1,0:T(8,128)(2,1)S(1)} %collective-permute-done.15.refs_3_, bf16[56,1280]{1,0:T(8,128)(2,1)S(1)} %collective-permute-done.16.refs_4_, ...), custom_call_target="tpu_custom_call" | custom-call | tf_op jit(solution)/shard_map/finish/pallas_call | solution.py:209
  (89 shorter events, 5.9 us)
Async XLA Ops:
  0.0 16.7 %collective-permute-start.2 = (bf16[128,2560]{1,0:T(8,128)(2,1)}, bf16[128,2560]{1,0:T(8,128)(2,1)S(1)}, u32[]{:S(2)}, u32[]{:S(2)}) collective-permute-start(bf16[128,2560]{1,0:T(8,128)(2,1)} %refs_0_.3), channel_id=1, source_target_pairs={{0,130},{1,131},{16,146},{17,147},{32,162},{33,163},{48,178},{49,1... | collective-permute-start | bytes 1966088 | tf_op jit(solution)/shard_map/ppermute | solution.py:45
  0.5 16.8 %collective-permute-start.1 = (bf16[128,2560]{1,0:T(8,128)(2,1)}, bf16[128,2560]{1,0:T(8,128)(2,1)S(1)}, u32[]{:S(2)}, u32[]{:S(2)}) collective-permute-start(bf16[128,2560]{1,0:T(8,128)(2,1)} %refs_0_.3), channel_id=1, source_target_pairs={{0,12},{1,13},{16,28},{17,29},{32,44},{33,45},{48,60},{49,61},{64,... | collective-permute-start | bytes 1966088 | tf_op jit(solution)/shard_map/ppermute | solution.py:45
  3.2 17.4 %collective-permute-start = (bf16[128,2560]{1,0:T(8,128)(2,1)}, bf16[128,2560]{1,0:T(8,128)(2,1)}, u32[]{:S(2)}, u32[]{:S(2)}) collective-permute-start(bf16[128,2560]{1,0:T(8,128)(2,1)} %refs_0_.3), channel_id=1, source_target_pairs={{0,4},{1,5},{16,20},{17,21},{32,36},{33,37},{48,52},{49,53},{64,68... | collective-permute-start | bytes 1966088 | tf_op jit(solution)/shard_map/ppermute | solution.py:45
  3.2 24.3 %copy-start.6 = (bf16[2560,432]{0,1:T(8,128)(2,1)S(1)}, bf16[2560,432]{0,1:T(8,128)(2,1)}, u32[]{:S(2)}) copy-start(bf16[2560,432]{0,1:T(8,128)(2,1)} %param.6) | copy-start | bytes 6635524
  7.3 57.5 %copy-start.15 = (s32[28]{0:T(128)}, s32[28]{0:T(128)S(1)}, u32[]{:S(2)}) copy-start(s32[28]{0:T(128)S(1)} %stack.115.refs_0_.table_ref) | copy-start | bytes 340
  20.7 6.9 %copy-start.2 = (bf16[2560,432]{0,1:T(8,128)(2,1)S(1)}, bf16[2560,432]{0,1:T(8,128)(2,1)}, u32[]{:S(2)}) copy-start(bf16[2560,432]{0,1:T(8,128)(2,1)} %param.7) | copy-start | bytes 6635524
  22.0 12.4 %copy-start.1 = (bf16[384,2560]{1,0:T(8,128)(2,1)}, bf16[384,2560]{1,0:T(8,128)(2,1)S(1)}, u32[]{:S(2)}) copy-start(bf16[384,2560]{1,0:T(8,128)(2,1)S(1)} %constant_dynamic-update-slice_fusion.refs_5_.refs_4_.refs_1_) | copy-start | bytes 5898244
  22.1 5.4 %collective-permute-start.4 = (bf16[384,2560]{1,0:T(8,128)(2,1)S(1)}, bf16[384,2560]{1,0:T(8,128)(2,1)S(1)}, u32[]{:S(2)}, u32[]{:S(2)}) collective-permute-start(bf16[384,2560]{1,0:T(8,128)(2,1)S(1)} %constant_dynamic-update-slice_fusion.refs_5_.refs_4_.refs_1_), channel_id=1, source_target_pairs={{0,1},{1,0},{16,17},{17,16},{32,33},{33,32},{48,49},{49,48},{64,65... | collective-permute-start | bytes 5898248 | tf_op jit(solution)/shard_map/ppermute | solution.py:45
  22.2 5.3 %collective-permute-start.3 = (bf16[128,2560]{1,0:T(8,128)(2,1)S(1)}, bf16[128,2560]{1,0:T(8,128)(2,1)S(1)}, u32[]{:S(2)}, u32[]{:S(2)}) collective-permute-start(bf16[128,2560]{1,0:T(8,128)(2,1)S(1)} %copy-done.9), channel_id=1, source_target_pairs={{0,1},{1,0},{16,17},{17,16},{32,33},{33,32},{48,49},{49,48},{64,65... | collective-permute-start | bytes 1966088 | tf_op jit(solution)/shard_map/ppermute | solution.py:45
  22.7 18.0 %collective-permute-start.5 = (bf16[128,2560]{1,0:T(8,128)(2,1)S(1)}, bf16[128,2560]{1,0:T(8,128)(2,1)S(1)}, u32[]{:S(2)}, u32[]{:S(2)}) collective-permute-start(bf16[128,2560]{1,0:T(8,128)(2,1)S(1)} %collective-permute-done.2), channel_id=1, source_target_pairs={{0,4},{1,5},{16,20},{17,21},{32,36},{33,37},{48,52},{49,53},{64,68... | collective-permute-start | bytes 1966088 | tf_op jit(solution)/shard_map/ppermute | solution.py:45
  22.7 18.0 %collective-permute-start.7 = (bf16[128,2560]{1,0:T(8,128)(2,1)S(1)}, bf16[128,2560]{1,0:T(8,128)(2,1)S(1)}, u32[]{:S(2)}, u32[]{:S(2)}) collective-permute-start(bf16[128,2560]{1,0:T(8,128)(2,1)S(1)} %collective-permute-done.1), channel_id=1, source_target_pairs={{0,130},{1,131},{16,146},{17,147},{32,162},{33,163},{48,178},{49,1... | collective-permute-start | bytes 1966088 | tf_op jit(solution)/shard_map/ppermute | solution.py:45
  24.2 16.9 %collective-permute-start.6 = (bf16[128,2560]{1,0:T(8,128)(2,1)S(1)}, bf16[128,2560]{1,0:T(8,128)(2,1)S(1)}, u32[]{:S(2)}, u32[]{:S(2)}) collective-permute-start(bf16[128,2560]{1,0:T(8,128)(2,1)S(1)} %collective-permute-done.1), channel_id=1, source_target_pairs={{0,12},{1,13},{16,28},{17,29},{32,44},{33,45},{48,60},{49,61},{64,... | collective-permute-start | bytes 1966088 | tf_op jit(solution)/shard_map/ppermute | solution.py:45
  27.5 7.0 %copy-start.10 = (bf16[128,2560]{1,0:T(8,128)(2,1)}, bf16[128,2560]{1,0:T(8,128)(2,1)S(1)}, u32[]{:S(2)}) copy-start(bf16[128,2560]{1,0:T(8,128)(2,1)S(1)} %collective-permute-done.3.refs_4_.refs_7_) | copy-start | bytes 1966084
  27.5 7.0 %copy-start.5 = (bf16[384,2560]{1,0:T(8,128)(2,1)}, bf16[384,2560]{1,0:T(8,128)(2,1)S(1)}, u32[]{:S(2)}) copy-start(bf16[384,2560]{1,0:T(8,128)(2,1)S(1)} %collective-permute-done.4.refs_6_.refs_8_.refs_5_) | copy-start | bytes 5898244
  34.5 6.9 %copy-start.12 = (f32[2,432,512]{2,1,0:T(8,128)}, f32[2,432,512]{2,1,0:T(8,128)S(1)}, u32[]{:S(2)}) copy-start(f32[2,432,512]{2,1,0:T(8,128)S(1)} %factor.3.refs_0_) | copy-start | bytes 5308420
  41.4 19.8 %copy-start = (bf16[384,2560]{1,0:T(8,128)(2,1)}, bf16[384,2560]{1,0:T(8,128)(2,1)S(1)}, u32[]{:S(2)}) copy-start(bf16[384,2560]{1,0:T(8,128)(2,1)S(1)} %constant_dynamic-update-slice_fusion.3.refs_3_.refs_5_.refs_2_) | copy-start | bytes 5898244
  41.4 10.4 %collective-permute-start.8 = (bf16[384,2560]{1,0:T(8,128)(2,1)S(1)}, bf16[384,2560]{1,0:T(8,128)(2,1)}, u32[]{:S(2)}, u32[]{:S(2)}) collective-permute-start(bf16[384,2560]{1,0:T(8,128)(2,1)S(1)} %constant_dynamic-update-slice_fusion.3.refs_3_.refs_5_.refs_2_), channel_id=1, source_target_pairs={{0,1},{1,0},{16,17},{17,16},{32,33},{33,32},{48,49},{49,48},{64,65... | collective-permute-start | bytes 5898248 | tf_op jit(solution)/shard_map/ppermute | solution.py:45
  41.5 20.8 %collective-permute-start.10 = (bf16[48,2560]{1,0:T(8,128)(2,1)S(1)}, bf16[48,2560]{1,0:T(8,128)(2,1)S(1)}, u32[]{:S(2)}, u32[]{:S(2)}) collective-permute-start(bf16[48,2560]{1,0:T(8,128)(2,1)S(1)} %slice.29), channel_id=1, source_target_pairs={{0,12},{1,13},{16,28},{17,29},{32,44},{33,45},{48,60},{49,61},{64,... | collective-permute-start | bytes 737288 | tf_op jit(solution)/shard_map/ppermute | solution.py:45
  45.3 17.0 %collective-permute-start.9 = (bf16[48,2560]{1,0:T(8,128)(2,1)S(1)}, bf16[48,2560]{1,0:T(8,128)(2,1)S(1)}, u32[]{:S(2)}, u32[]{:S(2)}) collective-permute-start(bf16[48,2560]{1,0:T(8,128)(2,1)S(1)} %slice.28), channel_id=1, source_target_pairs={{0,4},{1,5},{16,20},{17,21},{32,36},{33,37},{48,52},{49,53},{64,68... | collective-permute-start | bytes 737288 | tf_op jit(solution)/shard_map/ppermute | solution.py:45
  45.3 17.0 %collective-permute-start.11 = (bf16[32,2560]{1,0:T(8,128)(2,1)S(1)}, bf16[32,2560]{1,0:T(8,128)(2,1)S(1)}, u32[]{:S(2)}, u32[]{:S(2)}) collective-permute-start(bf16[32,2560]{1,0:T(8,128)(2,1)S(1)} %slice.30), channel_id=1, source_target_pairs={{0,130},{1,131},{16,146},{17,147},{32,162},{33,163},{48,178},{49,1... | collective-permute-start | bytes 491528 | tf_op jit(solution)/shard_map/ppermute | solution.py:45
  45.7 29.8 %all-to-all-start = ((bf16[16,432,128]{2,1,0:T(8,128)(2,1)}), bf16[16,432,128]{2,1,0:T(8,128)(2,1)}, u32[]{:S(2)}, u32[]{:S(2)}) async-start(bf16[16,432,128]{2,1,0:T(8,128)(2,1)} %bitcast.40), calls=%async_computation | async-start | bytes 3538944 | tf_op jit(solution)/shard_map/all_to_all | solution.py:244
  51.8 1.6 copy-start.3
  62.4 4.4 %copy-start.8 = (bf16[128,2560]{1,0:T(8,128)(2,1)}, bf16[128,2560]{1,0:T(8,128)(2,1)S(1)}, u32[]{:S(2)}) copy-start(bf16[128,2560]{1,0:T(8,128)(2,1)S(1)} %constant_dynamic-update-slice_fusion.6.refs_3_.refs_6_) | copy-start | bytes 1966084
  62.4 2.4 %collective-permute-start.12 = (bf16[128,2560]{1,0:T(8,128)(2,1)S(1)}, bf16[128,2560]{1,0:T(8,128)(2,1)S(1)}, u32[]{:S(2)}, u32[]{:S(2)}) collective-permute-start(bf16[128,2560]{1,0:T(8,128)(2,1)S(1)} %constant_dynamic-update-slice_fusion.6.refs_3_.refs_6_), channel_id=1, source_target_pairs={{0,1},{1,0},{16,17},{17,16},{32,33},{33,32},{48,49},{49,48},{64,65... | collective-permute-start | bytes 1966088 | tf_op jit(solution)/shard_map/ppermute | solution.py:45
  64.8 2.0 %copy-start.11 = (bf16[128,2560]{1,0:T(8,128)(2,1)}, bf16[128,2560]{1,0:T(8,128)(2,1)S(1)}, u32[]{:S(2)}) copy-start(bf16[128,2560]{1,0:T(8,128)(2,1)S(1)} %collective-permute-done.12.refs_4_.refs_10_.refs_7_) | copy-start | bytes 1966084
  84.3 24.8 %collective-permute-start.13 = (bf16[8,56,1024]{2,1,0:T(8,128)(2,1)}, bf16[8,56,1024]{2,1,0:T(8,128)(2,1)S(1)}, u32[]{:S(2)}, u32[]{:S(2)}) collective-permute-start(bf16[8,56,1024]{2,1,0:T(8,128)(2,1)} %get-tuple-element.35), channel_id=1, source_target_pairs={{0,128},{1,129},{16,144},{17,145},{32,160},{33,161},{48,176},{49,1... | collective-permute-start | bytes 2752520 | tf_op jit(solution)/shard_map/ppermute | solution.py:45
  93.0 24.7 %all-to-all-start.2 = ((bf16[8,56,512]{2,1,0:T(8,128)(2,1)}), bf16[8,56,512]{2,1,0:T(8,128)(2,1)S(1)}, u32[]{:S(2)}, u32[]{:S(2)}) async-start(bf16[8,56,512]{2,1,0:T(8,128)(2,1)} %outer.4), calls=%async_computation.2 | async-start | bytes 917504 | tf_op jit(solution)/shard_map/all_to_all | solution.py:268
  111.8 69.3 %copy-start.4 = (bf16[2560,432]{0,1:T(8,128)(2,1)S(1)}, bf16[2560,432]{0,1:T(8,128)(2,1)}, u32[]{:S(2)}) copy-start(bf16[2560,432]{0,1:T(8,128)(2,1)} %param.7) | copy-start | bytes 6635524
  111.8 69.3 %copy-start.16 = (s32[28]{0:T(128)S(1)}, s32[28]{0:T(128)}, u32[]{:S(2)}) copy-start(s32[28]{0:T(128)} %copy-done.15) | copy-start | bytes 340
  118.5 29.9 %all-to-all-start.1 = ((bf16[8,56,1024]{2,1,0:T(8,128)(2,1)}), bf16[8,56,1024]{2,1,0:T(8,128)(2,1)S(1)}, u32[]{:S(2)}, u32[]{:S(2)}) async-start(bf16[8,56,1024]{2,1,0:T(8,128)(2,1)} %add_convert_fusion), calls=%async_computation.1 | async-start | bytes 1835008 | tf_op jit(solution)/shard_map/all_to_all | solution.py:268
  123.2 4.0 %collective-permute-start.14 = (bf16[56,256]{1,0:T(8,128)(2,1)S(1)}, bf16[56,256]{1,0:T(8,128)(2,1)S(1)}, u32[]{:S(2)}, u32[]{:S(2)}) collective-permute-start(bf16[56,256]{1,0:T(8,128)(2,1)S(1)} %slice.47), channel_id=1, source_target_pairs={{0,128},{1,129},{16,144},{17,145},{32,160},{33,161},{48,176},{49,1... | collective-permute-start | bytes 86024 | tf_op jit(solution)/shard_map/ppermute | solution.py:45
  148.6 5.2 %collective-permute-start.23 = (bf16[56,1280]{1,0:T(8,128)(2,1)S(1)}, bf16[56,1280]{1,0:T(8,128)(2,1)S(1)}, u32[]{:S(2)}, u32[]{:S(2)}) collective-permute-start(bf16[56,1280]{1,0:T(8,128)(2,1)S(1)} %pad_maximum_fusion.refs_2_), channel_id=1, source_target_pairs={{0,128},{1,129},{16,144},{17,145},{32,160},{33,161},{48,176},{49,1... | collective-permute-start | bytes 430088 | tf_op jit(solution)/shard_map/ppermute | solution.py:45
  149.0 6.8 %collective-permute-start.16 = (bf16[56,1280]{1,0:T(8,128)(2,1)S(1)}, bf16[56,1280]{1,0:T(8,128)(2,1)S(1)}, u32[]{:S(2)}, u32[]{:S(2)}) collective-permute-start(bf16[56,1280]{1,0:T(8,128)(2,1)S(1)} %pad_maximum_fusion.refs_2_), channel_id=1, source_target_pairs={{0,112},{1,113},{16,0},{17,1},{32,16},{33,17},{48,32},{49,33},{64,... | collective-permute-start | bytes 430088 | tf_op jit(solution)/shard_map/ppermute | solution.py:45
  149.0 8.0 %collective-permute-start.15 = (bf16[56,1280]{1,0:T(8,128)(2,1)S(1)}, bf16[56,1280]{1,0:T(8,128)(2,1)S(1)}, u32[]{:S(2)}, u32[]{:S(2)}) collective-permute-start(bf16[56,1280]{1,0:T(8,128)(2,1)S(1)} %pad_maximum_fusion.refs_2_), channel_id=1, source_target_pairs={{0,16},{1,17},{16,32},{17,33},{32,48},{33,49},{48,64},{49,65},{64,... | collective-permute-start | bytes 430088 | tf_op jit(solution)/shard_map/ppermute | solution.py:45
  153.8 5.5 %collective-permute-start.25 = (bf16[56,1280]{1,0:T(8,128)(2,1)S(1)}, bf16[56,1280]{1,0:T(8,128)(2,1)S(1)}, u32[]{:S(2)}, u32[]{:S(2)}) collective-permute-start(bf16[56,1280]{1,0:T(8,128)(2,1)S(1)} %collective-permute-done.23.refs_11_), channel_id=1, source_target_pairs={{0,112},{1,113},{16,0},{17,1},{32,16},{33,17},{48,32},{49,33},{64,... | collective-permute-start | bytes 430088 | tf_op jit(solution)/shard_map/ppermute | solution.py:45
  153.8 7.8 %collective-permute-start.24 = (bf16[56,1280]{1,0:T(8,128)(2,1)S(1)}, bf16[56,1280]{1,0:T(8,128)(2,1)S(1)}, u32[]{:S(2)}, u32[]{:S(2)}) collective-permute-start(bf16[56,1280]{1,0:T(8,128)(2,1)S(1)} %collective-permute-done.23.refs_11_), channel_id=1, source_target_pairs={{0,16},{1,17},{16,32},{17,33},{32,48},{33,49},{48,64},{49,65},{64,... | collective-permute-start | bytes 430088 | tf_op jit(solution)/shard_map/ppermute | solution.py:45
  155.8 6.6 %collective-permute-start.18 = (bf16[56,1280]{1,0:T(8,128)(2,1)S(1)}, bf16[56,1280]{1,0:T(8,128)(2,1)S(1)}, u32[]{:S(2)}, u32[]{:S(2)}) collective-permute-start(bf16[56,1280]{1,0:T(8,128)(2,1)S(1)} %collective-permute-done.16.refs_4_), channel_id=1, source_target_pairs={{0,112},{1,113},{16,0},{17,1},{32,16},{33,17},{48,32},{49,33},{64,... | collective-permute-start | bytes 430088 | tf_op jit(solution)/shard_map/ppermute | solution.py:45
  157.0 7.8 %collective-permute-start.17 = (bf16[56,1280]{1,0:T(8,128)(2,1)S(1)}, bf16[56,1280]{1,0:T(8,128)(2,1)S(1)}, u32[]{:S(2)}, u32[]{:S(2)}) collective-permute-start(bf16[56,1280]{1,0:T(8,128)(2,1)S(1)} %collective-permute-done.15.refs_3_), channel_id=1, source_target_pairs={{0,16},{1,17},{16,32},{17,33},{32,48},{33,49},{48,64},{49,65},{64,... | collective-permute-start | bytes 430088 | tf_op jit(solution)/shard_map/ppermute | solution.py:45
  159.3 6.5 %collective-permute-start.27 = (bf16[56,1280]{1,0:T(8,128)(2,1)S(1)}, bf16[56,1280]{1,0:T(8,128)(2,1)S(1)}, u32[]{:S(2)}, u32[]{:S(2)}) collective-permute-start(bf16[56,1280]{1,0:T(8,128)(2,1)S(1)} %collective-permute-done.25.refs_13_), channel_id=1, source_target_pairs={{0,112},{1,113},{16,0},{17,1},{32,16},{33,17},{48,32},{49,33},{64,... | collective-permute-start | bytes 430088 | tf_op jit(solution)/shard_map/ppermute | solution.py:45
  161.6 7.1 %collective-permute-start.26 = (bf16[56,1280]{1,0:T(8,128)(2,1)S(1)}, bf16[56,1280]{1,0:T(8,128)(2,1)S(1)}, u32[]{:S(2)}, u32[]{:S(2)}) collective-permute-start(bf16[56,1280]{1,0:T(8,128)(2,1)S(1)} %collective-permute-done.24.refs_12_), channel_id=1, source_target_pairs={{0,16},{1,17},{16,32},{17,33},{32,48},{33,49},{48,64},{49,65},{64,... | collective-permute-start | bytes 430088 | tf_op jit(solution)/shard_map/ppermute | solution.py:45
  162.4 6.6 %collective-permute-start.20 = (bf16[56,1280]{1,0:T(8,128)(2,1)S(1)}, bf16[56,1280]{1,0:T(8,128)(2,1)S(1)}, u32[]{:S(2)}, u32[]{:S(2)}) collective-permute-start(bf16[56,1280]{1,0:T(8,128)(2,1)S(1)} %collective-permute-done.18.refs_6_), channel_id=1, source_target_pairs={{0,112},{1,113},{16,0},{17,1},{32,16},{33,17},{48,32},{49,33},{64,... | collective-permute-start | bytes 430088 | tf_op jit(solution)/shard_map/ppermute | solution.py:45
  164.8 7.2 %collective-permute-start.19 = (bf16[56,1280]{1,0:T(8,128)(2,1)S(1)}, bf16[56,1280]{1,0:T(8,128)(2,1)S(1)}, u32[]{:S(2)}, u32[]{:S(2)}) collective-permute-start(bf16[56,1280]{1,0:T(8,128)(2,1)S(1)} %collective-permute-done.17.refs_5_), channel_id=1, source_target_pairs={{0,16},{1,17},{16,32},{17,33},{32,48},{33,49},{48,64},{49,65},{64,... | collective-permute-start | bytes 430088 | tf_op jit(solution)/shard_map/ppermute | solution.py:45
  165.8 6.4 %collective-permute-start.29 = (bf16[56,1280]{1,0:T(8,128)(2,1)S(1)}, bf16[56,1280]{1,0:T(8,128)(2,1)S(1)}, u32[]{:S(2)}, u32[]{:S(2)}) collective-permute-start(bf16[56,1280]{1,0:T(8,128)(2,1)S(1)} %collective-permute-done.27.refs_15_), channel_id=1, source_target_pairs={{0,112},{1,113},{16,0},{17,1},{32,16},{33,17},{48,32},{49,33},{64,... | collective-permute-start | bytes 430088 | tf_op jit(solution)/shard_map/ppermute | solution.py:45
  168.7 6.7 %collective-permute-start.28 = (bf16[56,1280]{1,0:T(8,128)(2,1)S(1)}, bf16[56,1280]{1,0:T(8,128)(2,1)S(1)}, u32[]{:S(2)}, u32[]{:S(2)}) collective-permute-start(bf16[56,1280]{1,0:T(8,128)(2,1)S(1)} %collective-permute-done.26.refs_14_), channel_id=1, source_target_pairs={{0,16},{1,17},{16,32},{17,33},{32,48},{33,49},{48,64},{49,65},{64,... | collective-permute-start | bytes 430088 | tf_op jit(solution)/shard_map/ppermute | solution.py:45
  169.0 6.6 %collective-permute-start.22 = (bf16[56,640]{1,0:T(8,128)(2,1)S(1)}, bf16[56,640]{1,0:T(8,128)(2,1)S(1)}, u32[]{:S(2)}, u32[]{:S(2)}) collective-permute-start(bf16[56,640]{1,0:T(8,128)(2,1)S(1)} %slice.40), channel_id=1, source_target_pairs={{0,112},{1,113},{16,0},{17,1},{32,16},{33,17},{48,32},{49,33},{64,... | collective-permute-start | bytes 215048 | tf_op jit(solution)/shard_map/ppermute | solution.py:45
  172.1 5.6 %collective-permute-start.21 = (bf16[56,640]{1,0:T(8,128)(2,1)S(1)}, bf16[56,640]{1,0:T(8,128)(2,1)S(1)}, u32[]{:S(2)}, u32[]{:S(2)}) collective-permute-start(bf16[56,640]{1,0:T(8,128)(2,1)S(1)} %slice.39), channel_id=1, source_target_pairs={{0,16},{1,17},{16,32},{17,33},{32,48},{33,49},{48,64},{49,65},{64,... | collective-permute-start | bytes 215048 | tf_op jit(solution)/shard_map/ppermute | solution.py:45
  172.2 5.5 %collective-permute-start.31 = (bf16[56,640]{1,0:T(8,128)(2,1)S(1)}, bf16[56,640]{1,0:T(8,128)(2,1)S(1)}, u32[]{:S(2)}, u32[]{:S(2)}) collective-permute-start(bf16[56,640]{1,0:T(8,128)(2,1)S(1)} %slice.42), channel_id=1, source_target_pairs={{0,112},{1,113},{16,0},{17,1},{32,16},{33,17},{48,32},{49,33},{64,... | collective-permute-start | bytes 215048 | tf_op jit(solution)/shard_map/ppermute | solution.py:45
  175.5 5.6 %collective-permute-start.30 = (bf16[56,640]{1,0:T(8,128)(2,1)S(1)}, bf16[56,640]{1,0:T(8,128)(2,1)S(1)}, u32[]{:S(2)}, u32[]{:S(2)}) collective-permute-start(bf16[56,640]{1,0:T(8,128)(2,1)S(1)} %slice.41), channel_id=1, source_target_pairs={{0,16},{1,17},{16,32},{17,33},{32,48},{33,49},{48,64},{49,65},{64,... | collective-permute-start | bytes 215048 | tf_op jit(solution)/shard_map/ppermute | solution.py:45
  (5 other events, 5.8 us)

commit v3 on v2

--- a/solution.py
+++ b/solution.py
@@ -27,6 +27,7 @@
 X_DOWN = moves(lambda x, y, z, c: ((x - 1) % NX, y, z, c))
 Z_UP = moves(lambda x, y, z, c: (x, y, (z + 1) % NZ, c))
 Z_DOWN = moves(lambda x, y, z, c: (x, y, (z - 1) % NZ, c))
+Z_AWAY = {d: moves(lambda x, y, z, c, d=d: (x, y, (z + d) % NZ, c)) for d in (4, 3, -3, 2, -2, 1, -1)}
 Y_MATE = moves(lambda x, y, z, c: (x, 3 - y, z, c))
 Y_CUT = moves(lambda x, y, z, c: (x, y ^ 1, z, c))
 CORE = moves(lambda x, y, z, c: (x, y, z, 1 - c))
@@ -277,7 +278,13 @@
     (table,) = after((table,), late)
     (own,) = outer(table, 16 + 2 * rest + first, weighted, pieces, first * 256, F32, 256)
     late = ring_sum(late)
-    own = ring_sum((own + come.astype(F32)).astype(BF16))
+    own = own + come.astype(F32)
+    parts = own.astype(BF16)
+    take = lambda a, d: lax.dynamic_index_in_dim(a, lax.rem(z + d + NZ, NZ), 0, keepdims=False)
+    come = [send(take(parts, d), pairs) for d, pairs in Z_AWAY.items()]
+    own = take(own, 0)
+    for other in come:
+        own = own + other.astype(F32)
     late = late[:, half:] + send(late[:, :half].astype(BF16), Y_CUT).astype(F32)
     own = jnp.concatenate([own.astype(BF16), late.astype(BF16)], 1)
 

time: 186 us -> 179 us (0.962)
  waiting for transfers between devices: 73.1 us -> 45.8 us
  starting transfers between devices: 56.2 us -> 76.9 us
    all_to_all x2 -> x1, waiting for transfers between devices: 27.1 us -> 0.01 us  [on_device(): lax.all_to_all(a, AXES, split_axis=0, concat_axis=0, axis_index_groups=Z_...]
    ppermute x32 -> x39, starting transfers between devices: 38.1 us -> 62.7 us  [send(): return lax.ppermute(value, AXES, pairs)]
    all_to_all x2 -> x1, starting transfers between devices: 12 us -> 8.47 us  [on_device(): lax.all_to_all(a, AXES, split_axis=0, concat_axis=0, axis_index_groups=Z_...]
    unnamed x42 -> x40, local copies, waits for them, and re-layouts: 7.37 us -> 6.61 us
    ppermute x32 -> x39, waiting for transfers between devices: 38 us -> 37.8 us  [send(): return lax.ppermute(value, AXES, pairs)]
  transfers between devices with their start and end apart: 35 -> 41, of which waited for: 20 -> 18; matrix products, arithmetic and copies ran while one was open for 4% -> 5% of each run, Pallas kernels for 15% -> 15%
where the time goes in v3:
time: 179 us
  starting transfers between devices  76.9 us (43%)
  waiting for transfers between devices  45.8 us (26%)
  Pallas kernels  39.7 us (22%)
  local copies, waits for them, and re-layouts  11.7 us (7%)
  other arithmetic  4.34 us (2%)
    ppermute x39, starting transfers between devices, send(): return lax.ppermute(value, AXES, pairs)  62.7 us
    ppermute x39, waiting for transfers between devices, send(): return lax.ppermute(value, AXES, pairs)  37.8 us
    pallas_call x3, Pallas kernels, outer(): pl.pallas_call(weigh_outer_kernel if make else outer_kernel, grid_spec=pl...  20.7 us
    pallas_call x3, Pallas kernels, factor(): pl.pallas_call(lambda *refs: factor_kernel(weighing, *refs), grid_spec=pl...  15 us
    all_to_all x1, starting transfers between devices, on_device(): lax.all_to_all(a, AXES, split_axis=0, concat_axis=0, axis_index_groups=Z_...  8.47 us
    all_to_all x1, waiting for transfers between devices, on_device(): lax.all_to_all(turned, AXES, split_axis=0, concat_axis=0, axis_index_grou...  7.98 us
    unnamed x40, local copies, waits for them, and re-layouts  6.61 us
    all_to_all x1, starting transfers between devices, on_device(): lax.all_to_all(turned, AXES, split_axis=0, concat_axis=0, axis_index_grou...  5.74 us
  transfers between devices with their start and end apart: 41, of which 18 were waited for; matrix products, arithmetic and copies ran while one was open for 5% of the time, Pallas kernels for 15%

profile of v3, /device:TPU:16, one launch (start us, length us, event | category | flops | bytes accessed | tf_op | source)
XLA Modules:
  0.0 178.8 jit_solution(15836646000190187185)
XLA Ops:
  0.0 1.5 collective-permute-start
  1.5 1.7 collective-permute-start.1
  3.7 4.0 %copy.5 = bf16[6912,128]{1,0:T(8,128)(2,1)} copy(bf16[6912,128]{0,1:T(8,128)(2,1)} %bitcast.71) | data formatting | bytes 3538944 | tf_op jit(solution)/shard_map/transpose | solution.py:242
  7.8 10.2 %collective-permute-done = bf16[128,2560]{1,0:T(8,128)(2,1)} collective-permute-done((bf16[128,2560]{1,0:T(8,128)(2,1)}, bf16[128,2560]{1,0:T(8,128)(2,1)}, u32[]{:S(2)}, u32[]{:S(2)}) %collective-permute-start) | collective-permute-done | bytes 655392 | tf_op jit(solution)/shard_map/ppermute | solution.py:46
  18.0 1.4 collective-permute-done.2
  19.4 1.3 constant_dynamic-update-slice_fusion.2
  21.6 3.0 %collective-permute-start.6 = (bf16[128,2560]{1,0:T(8,128)(2,1)S(1)}, bf16[128,2560]{1,0:T(8,128)(2,1)S(1)}, u32[]{:S(2)}, u32[]{:S(2)}) collective-permute-start(bf16[128,2560]{1,0:T(8,128)(2,1)S(1)} %collective-permute-done.1), channel_id=1, source_target_pairs={{0,12},{1,13},{16,28},{17,29},{32,44},{33,45},{48,60},{49,61},{64,... | collective-permute-start | bytes 1966088 | tf_op jit(solution)/shard_map/ppermute | solution.py:46
  25.8 6.9 %factor.3.refs_0_ = f32[2,432,512]{2,1,0:T(8,128)S(1)} custom-call(s32[28]{0:T(128)S(1)} %stack.115.refs_0_.table_ref, bf16[432,2560]{1,0:T(8,128)(2,1)S(1)} %bitcast.67, bf16[432,2560]{1,0:T(8,128)(2,1)S(1)} %bitcast.63, bf16[128,2560]{1,0:T(8,128)(2,1)S(1)} %copy-done.9, bf16[128,2560]{1,0:T(8,128)(2,1)S(1)} %collective-permute-done.3.refs_4_.refs_7_, ...), custom_call_target="tpu_custom_call" | custom-call | tf_op jit(solution)/shard_map/factor/pallas_call | solution.py:92
  32.7 6.6 %collective-permute-done.5 = bf16[128,2560]{1,0:T(8,128)(2,1)S(1)} collective-permute-done((bf16[128,2560]{1,0:T(8,128)(2,1)S(1)}, bf16[128,2560]{1,0:T(8,128)(2,1)S(1)}, u32[]{:S(2)}, u32[]{:S(2)}) %collective-permute-start.5) | collective-permute-done | bytes 655392 | tf_op jit(solution)/shard_map/ppermute | solution.py:46
  39.3 1.5 collective-permute-done.7
  41.1 1.6 collective-permute-start.10
  43.7 5.7 %all-to-all-start = ((bf16[16,432,128]{2,1,0:T(8,128)(2,1)}), bf16[16,432,128]{2,1,0:T(8,128)(2,1)}, u32[]{:S(2)}, u32[]{:S(2)}) async-start(bf16[16,432,128]{2,1,0:T(8,128)(2,1)} %bitcast.70), calls=%async_computation | async-start | bytes 3538944 | tf_op jit(solution)/shard_map/all_to_all | solution.py:245
  49.4 1.6 copy-done.3
  51.1 1.6 copy-done.7
  52.7 6.1 %factor.4.refs_1_ = f32[2,432,384]{2,1,0:T(8,128)S(1)} custom-call(s32[28]{0:T(128)S(1)} %stack.115.refs_0_.table_ref, bf16[432,2560]{1,0:T(8,128)(2,1)S(1)} %bitcast.68, bf16[432,2560]{1,0:T(8,128)(2,1)S(1)} %bitcast.64, bf16[384,2560]{1,0:T(8,128)(2,1)S(1)} %constant_dynamic-update-slice_fusion.3.refs_3_.refs_5_.refs_2_, ...), custom_call_target="tpu_custom_call" | custom-call | tf_op jit(solution)/shard_map/factor/pallas_call | solution.py:92
  58.8 1.1 copy-done.13
  60.4 1.9 %collective-permute-done.12.refs_4_.refs_10_.refs_7_ = bf16[128,2560]{1,0:T(8,128)(2,1)S(1)} collective-permute-done((bf16[128,2560]{1,0:T(8,128)(2,1)S(1)}, bf16[128,2560]{1,0:T(8,128)(2,1)S(1)}, u32[]{:S(2)}, u32[]{:S(2)}) %collective-permute-start.12) | collective-permute-done | bytes 655392 | tf_op jit(solution)/shard_map/ppermute | solution.py:46
  62.4 2.0 %factor.5.refs_2_ = f32[2,432,128]{2,1,0:T(8,128)S(1)} custom-call(s32[28]{0:T(128)S(1)} %stack.115.refs_0_.table_ref, bf16[432,2560]{1,0:T(8,128)(2,1)S(1)} %bitcast.69, bf16[432,2560]{1,0:T(8,128)(2,1)S(1)} %bitcast.65, bf16[128,2560]{1,0:T(8,128)(2,1)S(1)} %constant_dynamic-update-slice_fusion.6.refs_3_.refs_6_, ...), custom_call_target="tpu_custom_call" | custom-call | tf_op jit(solution)/shard_map/factor/pallas_call | solution.py:92
  65.2 8.0 %all-to-all-done.grad_ref = bf16[16,432,128]{2,1,0:T(8,128)(2,1)} async-done(((bf16[16,432,128]{2,1,0:T(8,128)(2,1)}), bf16[16,432,128]{2,1,0:T(8,128)(2,1)}, u32[]{:S(2)}, u32[]{:S(2)}) %all-to-all-start) | async-done | bytes 1769504 | tf_op jit(solution)/shard_map/all_to_all | solution.py:245
  73.2 8.7 %outer.3 = (bf16[432,2048]{1,0:T(8,128)(2,1)}, bf16[8,56,1024]{2,1,0:T(8,128)(2,1)}) custom-call(s32[28]{0:T(128)} %copy-done.15, bf16[16,432,128]{2,1,0:T(8,128)(2,1)} %all-to-all-done.grad_ref, f32[2,432,512]{2,1,0:T(8,128)} %copy-done.12, f32[2,432,384]{2,1,0:T(8,128)} %copy-done.13, f32[2,432,128]{2,1,0:T(8,128)} %copy-done.14, ...), custom_call_target="tpu_custom_call" | custom-call | flops 1811939328 | bytes 5963776 | tf_op jit(solution)/shard_map/outer/pallas_call | solution.py:156
  81.9 5.0 %collective-permute-start.13 = (bf16[8,56,1024]{2,1,0:T(8,128)(2,1)}, bf16[8,56,1024]{2,1,0:T(8,128)(2,1)S(1)}, u32[]{:S(2)}, u32[]{:S(2)}) collective-permute-start(bf16[8,56,1024]{2,1,0:T(8,128)(2,1)} %get-tuple-element.35), channel_id=1, source_target_pairs={{0,128},{1,129},{16,144},{17,145},{32,160},{33,161},{48,176},{49,1... | collective-permute-start | bytes 2752520 | tf_op jit(solution)/shard_map/ppermute | solution.py:46
  86.8 4.9 %outer.4 = bf16[8,56,512]{2,1,0:T(8,128)(2,1)} custom-call(s32[28]{0:T(128)} %copy-done.15, bf16[432,2048]{1,0:T(8,128)(2,1)} %get-tuple-element.37.weighted_ref, bf16[128,2560]{1,0:T(8,128)(2,1)} %refs_0_.3, bf16[384,2560]{1,0:T(8,128)(2,1)} %copy-done.1, bf16[384,2560]{1,0:T(8,128)(2,1)} %copy-done, bf16[128,2560]{1,0:T(8,128)(2,1)} %copy-done.8, ...), custom_call_target="tpu_custom_call" | custom-call | flops 905969664 | bytes 3866624 | tf_op jit(solution)/shard_map/outer/pallas_call | solution.py:156
  91.8 8.5 %all-to-all-start.1 = ((bf16[8,56,512]{2,1,0:T(8,128)(2,1)}), bf16[8,56,512]{2,1,0:T(8,128)(2,1)S(1)}, u32[]{:S(2)}, u32[]{:S(2)}) async-start(bf16[8,56,512]{2,1,0:T(8,128)(2,1)} %outer.4), calls=%async_computation.1 | async-start | bytes 917504 | tf_op jit(solution)/shard_map/all_to_all | solution.py:269
  100.3 7.1 %outer.5 = f32[8,56,1024]{2,1,0:T(8,128)} custom-call(s32[28]{0:T(128)} %copy-done.15, bf16[432,2048]{1,0:T(8,128)(2,1)} %get-tuple-element.37.weighted_ref, bf16[128,2560]{1,0:T(8,128)(2,1)} %refs_0_.3, bf16[384,2560]{1,0:T(8,128)(2,1)} %copy-done.1, bf16[384,2560]{1,0:T(8,128)(2,1)} %copy-done, bf16[128,2560]{1,0:T(8,128)(2,1)} %copy-done.8, ...), custom_call_target="tpu_custom_call" | custom-call | flops 1811939328 | bytes 5963776 | tf_op jit(solution)/shard_map/outer/pallas_call | solution.py:156
  107.9 3.2 %fusion.8 = (bf16[8,56,1024]{2,1,0:T(8,128)(2,1)S(1)}, f32[8,56,1024]{2,1,0:T(8,128)}) fusion(f32[8,56,1024]{2,1,0:T(8,128)} %outer.5, bf16[8,56,1024]{2,1,0:T(8,128)(2,1)S(1)} %collective-permute-done.13), kind=kLoop, calls=%fused_computation.30 | loop fusion | flops 1376256 | bytes 5505024 | tf_op jit(solution)/shard_map/convert_element_type | solution.py:282
  111.8 7.2 %collective-permute-start.14 = (bf16[56,1024]{1,0:T(8,128)(2,1)}, bf16[56,1024]{1,0:T(8,128)(2,1)S(1)}, u32[]{:S(2)}, u32[]{:S(2)}) collective-permute-start(bf16[56,1024]{1,0:T(8,128)(2,1)} %get-tuple-element.41), channel_id=1, source_target_pairs={{0,64},{1,65},{16,80},{17,81},{32,96},{33,97},{48,112},{49,113},{6... | collective-permute-start | bytes 344072 | tf_op jit(solution)/shard_map/ppermute | solution.py:46
  119.0 1.9 %collective-permute-start.15 = (bf16[56,1024]{1,0:T(8,128)(2,1)}, bf16[56,1024]{1,0:T(8,128)(2,1)S(1)}, u32[]{:S(2)}, u32[]{:S(2)}) collective-permute-start(bf16[56,1024]{1,0:T(8,128)(2,1)} %get-tuple-element.47), channel_id=1, source_target_pairs={{0,48},{1,49},{16,64},{17,65},{32,80},{33,81},{48,96},{49,97},{64,... | collective-permute-start | bytes 344072 | tf_op jit(solution)/shard_map/ppermute | solution.py:46
  121.0 1.8 %collective-permute-start.21 = (bf16[56,256]{1,0:T(8,128)(2,1)S(1)}, bf16[56,256]{1,0:T(8,128)(2,1)S(1)}, u32[]{:S(2)}, u32[]{:S(2)}) collective-permute-start(bf16[56,256]{1,0:T(8,128)(2,1)S(1)} %slice.47), channel_id=1, source_target_pairs={{0,128},{1,129},{16,144},{17,145},{32,160},{33,161},{48,176},{49,1... | collective-permute-start | bytes 86024 | tf_op jit(solution)/shard_map/ppermute | solution.py:46
  122.9 3.1 %collective-permute-start.16 = (bf16[56,1024]{1,0:T(8,128)(2,1)}, bf16[56,1024]{1,0:T(8,128)(2,1)S(1)}, u32[]{:S(2)}, u32[]{:S(2)}) collective-permute-start(bf16[56,1024]{1,0:T(8,128)(2,1)} %get-tuple-element.46), channel_id=1, source_target_pairs={{0,80},{1,81},{16,96},{17,97},{32,112},{33,113},{48,0},{49,1},{64,... | collective-permute-start | bytes 344072 | tf_op jit(solution)/shard_map/ppermute | solution.py:46
  126.0 1.5 collective-permute-start.17
  127.5 2.7 %collective-permute-start.18 = (bf16[56,1024]{1,0:T(8,128)(2,1)S(1)}, bf16[56,1024]{1,0:T(8,128)(2,1)S(1)}, u32[]{:S(2)}, u32[]{:S(2)}) collective-permute-start(bf16[56,1024]{1,0:T(8,128)(2,1)S(1)} %get-tuple-element.44), channel_id=1, source_target_pairs={{0,96},{1,97},{16,112},{17,113},{32,0},{33,1},{48,16},{49,17},{64,... | collective-permute-start | bytes 344072 | tf_op jit(solution)/shard_map/ppermute | solution.py:46
  131.1 2.8 %collective-permute-done.15 = bf16[56,1024]{1,0:T(8,128)(2,1)S(1)} collective-permute-done((bf16[56,1024]{1,0:T(8,128)(2,1)}, bf16[56,1024]{1,0:T(8,128)(2,1)S(1)}, u32[]{:S(2)}, u32[]{:S(2)}) %collective-permute-start.15) | collective-permute-done | bytes 114720 | tf_op jit(solution)/shard_map/ppermute | solution.py:46
  134.3 1.8 collective-permute-done.17
  136.0 3.5 %collective-permute-done.18 = bf16[56,1024]{1,0:T(8,128)(2,1)S(1)} collective-permute-done((bf16[56,1024]{1,0:T(8,128)(2,1)S(1)}, bf16[56,1024]{1,0:T(8,128)(2,1)S(1)}, u32[]{:S(2)}, u32[]{:S(2)}) %collective-permute-start.18) | collective-permute-done | bytes 114720 | tf_op jit(solution)/shard_map/ppermute | solution.py:46
  139.7 1.4 collective-permute-done.20
  141.1 1.1 fusion.6
  143.4 2.9 %collective-permute-start.23 = (bf16[56,1280]{1,0:T(8,128)(2,1)S(1)}, bf16[56,1280]{1,0:T(8,128)(2,1)S(1)}, u32[]{:S(2)}, u32[]{:S(2)}) collective-permute-start(bf16[56,1280]{1,0:T(8,128)(2,1)S(1)} %pad_maximum_fusion.refs_2_), channel_id=1, source_target_pairs={{0,112},{1,113},{16,0},{17,1},{32,16},{33,17},{48,32},{49,33},{64,... | collective-permute-start | bytes 430088 | tf_op jit(solution)/shard_map/ppermute | solution.py:46
  146.3 1.1 collective-permute-done.30.refs_11_
  147.8 2.9 %collective-permute-start.32 = (bf16[56,1280]{1,0:T(8,128)(2,1)S(1)}, bf16[56,1280]{1,0:T(8,128)(2,1)S(1)}, u32[]{:S(2)}, u32[]{:S(2)}) collective-permute-start(bf16[56,1280]{1,0:T(8,128)(2,1)S(1)} %collective-permute-done.30.refs_11_), channel_id=1, source_target_pairs={{0,112},{1,113},{16,0},{17,1},{32,16},{33,17},{48,32},{49,33},{64,... | collective-permute-start | bytes 430088 | tf_op jit(solution)/shard_map/ppermute | solution.py:46
  150.7 3.2 %collective-permute-start.25 = (bf16[56,1280]{1,0:T(8,128)(2,1)S(1)}, bf16[56,1280]{1,0:T(8,128)(2,1)S(1)}, u32[]{:S(2)}, u32[]{:S(2)}) collective-permute-start(bf16[56,1280]{1,0:T(8,128)(2,1)S(1)} %collective-permute-done.23.refs_4_), channel_id=1, source_target_pairs={{0,112},{1,113},{16,0},{17,1},{32,16},{33,17},{48,32},{49,33},{64,... | collective-permute-start | bytes 430088 | tf_op jit(solution)/shard_map/ppermute | solution.py:46
  153.9 1.4 collective-permute-done.31.refs_12_
  155.3 3.2 %collective-permute-start.34 = (bf16[56,1280]{1,0:T(8,128)(2,1)S(1)}, bf16[56,1280]{1,0:T(8,128)(2,1)S(1)}, u32[]{:S(2)}, u32[]{:S(2)}) collective-permute-start(bf16[56,1280]{1,0:T(8,128)(2,1)S(1)} %collective-permute-done.32.refs_13_), channel_id=1, source_target_pairs={{0,112},{1,113},{16,0},{17,1},{32,16},{33,17},{48,32},{49,33},{64,... | collective-permute-start | bytes 430088 | tf_op jit(solution)/shard_map/ppermute | solution.py:46
  158.5 3.2 %collective-permute-start.27 = (bf16[56,1280]{1,0:T(8,128)(2,1)S(1)}, bf16[56,1280]{1,0:T(8,128)(2,1)S(1)}, u32[]{:S(2)}, u32[]{:S(2)}) collective-permute-start(bf16[56,1280]{1,0:T(8,128)(2,1)S(1)} %collective-permute-done.25.refs_6_), channel_id=1, source_target_pairs={{0,112},{1,113},{16,0},{17,1},{32,16},{33,17},{48,32},{49,33},{64,... | collective-permute-start | bytes 430088 | tf_op jit(solution)/shard_map/ppermute | solution.py:46
  162.4 3.2 %collective-permute-start.36 = (bf16[56,1280]{1,0:T(8,128)(2,1)S(1)}, bf16[56,1280]{1,0:T(8,128)(2,1)S(1)}, u32[]{:S(2)}, u32[]{:S(2)}) collective-permute-start(bf16[56,1280]{1,0:T(8,128)(2,1)S(1)} %collective-permute-done.34.refs_15_), channel_id=1, source_target_pairs={{0,112},{1,113},{16,0},{17,1},{32,16},{33,17},{48,32},{49,33},{64,... | collective-permute-start | bytes 430088 | tf_op jit(solution)/shard_map/ppermute | solution.py:46
  165.8 3.3 %collective-permute-start.29 = (bf16[56,640]{1,0:T(8,128)(2,1)S(1)}, bf16[56,640]{1,0:T(8,128)(2,1)S(1)}, u32[]{:S(2)}, u32[]{:S(2)}) collective-permute-start(bf16[56,640]{1,0:T(8,128)(2,1)S(1)} %slice.40), channel_id=1, source_target_pairs={{0,112},{1,113},{16,0},{17,1},{32,16},{33,17},{48,32},{49,33},{64,... | collective-permute-start | bytes 215048 | tf_op jit(solution)/shard_map/ppermute | solution.py:46
  169.3 3.4 %collective-permute-start.38 = (bf16[56,640]{1,0:T(8,128)(2,1)S(1)}, bf16[56,640]{1,0:T(8,128)(2,1)S(1)}, u32[]{:S(2)}, u32[]{:S(2)}) collective-permute-start(bf16[56,640]{1,0:T(8,128)(2,1)S(1)} %slice.42), channel_id=1, source_target_pairs={{0,112},{1,113},{16,0},{17,1},{32,16},{33,17},{48,32},{49,33},{64,... | collective-permute-start | bytes 215048 | tf_op jit(solution)/shard_map/ppermute | solution.py:46
  172.7 2.1 %collective-permute-done.37.refs_18_ = bf16[56,640]{1,0:T(8,128)(2,1)S(1)} collective-permute-done((bf16[56,640]{1,0:T(8,128)(2,1)S(1)}, bf16[56,640]{1,0:T(8,128)(2,1)S(1)}, u32[]{:S(2)}, u32[]{:S(2)}) %collective-permute-start.37) | collective-permute-done | bytes 71712 | tf_op jit(solution)/shard_map/ppermute | solution.py:46
  174.8 4.0 %finish.1 = f32[432,2560]{1,0:T(8,128)} custom-call(s32[28]{0:T(128)S(1)} %copy-done.16, bf16[432,2560]{1,0:T(8,128)(2,1)S(1)} %bitcast.66, bf16[56,1280]{1,0:T(8,128)(2,1)S(1)} %pad_maximum_fusion.refs_2_, bf16[56,1280]{1,0:T(8,128)(2,1)S(1)} %collective-permute-done.22.refs_3_, bf16[56,1280]{1,0:T(8,128)(2,1)S(1)} %collective-permute-done.23.refs_4_, ...), custom_call_target="tpu_custom_call" | custom-call | tf_op jit(solution)/shard_map/finish/pallas_call | solution.py:210
  (100 shorter events, 10.7 us)
Async XLA Ops:
  0.0 18.0 %collective-permute-start = (bf16[128,2560]{1,0:T(8,128)(2,1)}, bf16[128,2560]{1,0:T(8,128)(2,1)}, u32[]{:S(2)}, u32[]{:S(2)}) collective-permute-start(bf16[128,2560]{1,0:T(8,128)(2,1)} %refs_0_.3), channel_id=1, source_target_pairs={{0,4},{1,5},{16,20},{17,21},{32,36},{33,37},{48,52},{49,53},{64,68... | collective-permute-start | bytes 1966088 | tf_op jit(solution)/shard_map/ppermute | solution.py:46
  1.5 16.5 %collective-permute-start.1 = (bf16[128,2560]{1,0:T(8,128)(2,1)}, bf16[128,2560]{1,0:T(8,128)(2,1)S(1)}, u32[]{:S(2)}, u32[]{:S(2)}) collective-permute-start(bf16[128,2560]{1,0:T(8,128)(2,1)} %refs_0_.3), channel_id=1, source_target_pairs={{0,12},{1,13},{16,28},{17,29},{32,44},{33,45},{48,60},{49,61},{64,... | collective-permute-start | bytes 1966088 | tf_op jit(solution)/shard_map/ppermute | solution.py:46
  3.2 16.1 %collective-permute-start.2 = (bf16[128,2560]{1,0:T(8,128)(2,1)}, bf16[128,2560]{1,0:T(8,128)(2,1)S(1)}, u32[]{:S(2)}, u32[]{:S(2)}) collective-permute-start(bf16[128,2560]{1,0:T(8,128)(2,1)} %refs_0_.3), channel_id=1, source_target_pairs={{0,130},{1,131},{16,146},{17,147},{32,162},{33,163},{48,178},{49,1... | collective-permute-start | bytes 1966088 | tf_op jit(solution)/shard_map/ppermute | solution.py:46
  3.7 22.1 %copy-start.6 = (bf16[2560,432]{0,1:T(8,128)(2,1)S(1)}, bf16[2560,432]{0,1:T(8,128)(2,1)}, u32[]{:S(2)}) copy-start(bf16[2560,432]{0,1:T(8,128)(2,1)} %param.6) | copy-start | bytes 6635524
  7.8 54.6 %copy-start.15 = (s32[28]{0:T(128)}, s32[28]{0:T(128)S(1)}, u32[]{:S(2)}) copy-start(s32[28]{0:T(128)S(1)} %stack.115.refs_0_.table_ref) | copy-start | bytes 340
  20.8 11.9 %copy-start.1 = (bf16[384,2560]{1,0:T(8,128)(2,1)}, bf16[384,2560]{1,0:T(8,128)(2,1)S(1)}, u32[]{:S(2)}) copy-start(bf16[384,2560]{1,0:T(8,128)(2,1)S(1)} %constant_dynamic-update-slice_fusion.refs_5_.refs_4_.refs_1_) | copy-start | bytes 5898244
  20.8 5.0 %collective-permute-start.4 = (bf16[384,2560]{1,0:T(8,128)(2,1)S(1)}, bf16[384,2560]{1,0:T(8,128)(2,1)S(1)}, u32[]{:S(2)}, u32[]{:S(2)}) collective-permute-start(bf16[384,2560]{1,0:T(8,128)(2,1)S(1)} %constant_dynamic-update-slice_fusion.refs_5_.refs_4_.refs_1_), channel_id=1, source_target_pairs={{0,1},{1,0},{16,17},{17,16},{32,33},{33,32},{48,49},{49,48},{64,65... | collective-permute-start | bytes 5898248 | tf_op jit(solution)/shard_map/ppermute | solution.py:46
  20.9 4.9 %collective-permute-start.3 = (bf16[128,2560]{1,0:T(8,128)(2,1)S(1)}, bf16[128,2560]{1,0:T(8,128)(2,1)S(1)}, u32[]{:S(2)}, u32[]{:S(2)}) collective-permute-start(bf16[128,2560]{1,0:T(8,128)(2,1)S(1)} %copy-done.9), channel_id=1, source_target_pairs={{0,1},{1,0},{16,17},{17,16},{32,33},{33,32},{48,49},{49,48},{64,65... | collective-permute-start | bytes 1966088 | tf_op jit(solution)/shard_map/ppermute | solution.py:46
  21.4 18.0 %collective-permute-start.5 = (bf16[128,2560]{1,0:T(8,128)(2,1)S(1)}, bf16[128,2560]{1,0:T(8,128)(2,1)S(1)}, u32[]{:S(2)}, u32[]{:S(2)}) collective-permute-start(bf16[128,2560]{1,0:T(8,128)(2,1)S(1)} %collective-permute-done.2), channel_id=1, source_target_pairs={{0,4},{1,5},{16,20},{17,21},{32,36},{33,37},{48,52},{49,53},{64,68... | collective-permute-start | bytes 1966088 | tf_op jit(solution)/shard_map/ppermute | solution.py:46
  21.6 17.7 %collective-permute-start.6 = (bf16[128,2560]{1,0:T(8,128)(2,1)S(1)}, bf16[128,2560]{1,0:T(8,128)(2,1)S(1)}, u32[]{:S(2)}, u32[]{:S(2)}) collective-permute-start(bf16[128,2560]{1,0:T(8,128)(2,1)S(1)} %collective-permute-done.1), channel_id=1, source_target_pairs={{0,12},{1,13},{16,28},{17,29},{32,44},{33,45},{48,60},{49,61},{64,... | collective-permute-start | bytes 1966088 | tf_op jit(solution)/shard_map/ppermute | solution.py:46
  24.6 16.2 %collective-permute-start.7 = (bf16[128,2560]{1,0:T(8,128)(2,1)S(1)}, bf16[128,2560]{1,0:T(8,128)(2,1)S(1)}, u32[]{:S(2)}, u32[]{:S(2)}) collective-permute-start(bf16[128,2560]{1,0:T(8,128)(2,1)S(1)} %collective-permute-done.1), channel_id=1, source_target_pairs={{0,130},{1,131},{16,146},{17,147},{32,162},{33,163},{48,178},{49,1... | collective-permute-start | bytes 1966088 | tf_op jit(solution)/shard_map/ppermute | solution.py:46
  32.7 8.3 %copy-start.12 = (f32[2,432,512]{2,1,0:T(8,128)}, f32[2,432,512]{2,1,0:T(8,128)S(1)}, u32[]{:S(2)}) copy-start(f32[2,432,512]{2,1,0:T(8,128)S(1)} %factor.3.refs_0_) | copy-start | bytes 5308420
  41.0 17.8 %copy-start = (bf16[384,2560]{1,0:T(8,128)(2,1)}, bf16[384,2560]{1,0:T(8,128)(2,1)S(1)}, u32[]{:S(2)}) copy-start(bf16[384,2560]{1,0:T(8,128)(2,1)S(1)} %constant_dynamic-update-slice_fusion.3.refs_3_.refs_5_.refs_2_) | copy-start | bytes 5898244
  41.0 8.4 %collective-permute-start.8 = (bf16[384,2560]{1,0:T(8,128)(2,1)S(1)}, bf16[384,2560]{1,0:T(8,128)(2,1)}, u32[]{:S(2)}, u32[]{:S(2)}) collective-permute-start(bf16[384,2560]{1,0:T(8,128)(2,1)S(1)} %constant_dynamic-update-slice_fusion.3.refs_3_.refs_5_.refs_2_), channel_id=1, source_target_pairs={{0,1},{1,0},{16,17},{17,16},{32,33},{33,32},{48,49},{49,48},{64,65... | collective-permute-start | bytes 5898248 | tf_op jit(solution)/shard_map/ppermute | solution.py:46
  41.1 18.8 %collective-permute-start.10 = (bf16[48,2560]{1,0:T(8,128)(2,1)S(1)}, bf16[48,2560]{1,0:T(8,128)(2,1)S(1)}, u32[]{:S(2)}, u32[]{:S(2)}) collective-permute-start(bf16[48,2560]{1,0:T(8,128)(2,1)S(1)} %slice.29), channel_id=1, source_target_pairs={{0,12},{1,13},{16,28},{17,29},{32,44},{33,45},{48,60},{49,61},{64,... | collective-permute-start | bytes 737288 | tf_op jit(solution)/shard_map/ppermute | solution.py:46
  42.7 17.2 %collective-permute-start.9 = (bf16[48,2560]{1,0:T(8,128)(2,1)S(1)}, bf16[48,2560]{1,0:T(8,128)(2,1)S(1)}, u32[]{:S(2)}, u32[]{:S(2)}) collective-permute-start(bf16[48,2560]{1,0:T(8,128)(2,1)S(1)} %slice.28), channel_id=1, source_target_pairs={{0,4},{1,5},{16,20},{17,21},{32,36},{33,37},{48,52},{49,53},{64,68... | collective-permute-start | bytes 737288 | tf_op jit(solution)/shard_map/ppermute | solution.py:46
  43.2 16.7 %collective-permute-start.11 = (bf16[32,2560]{1,0:T(8,128)(2,1)S(1)}, bf16[32,2560]{1,0:T(8,128)(2,1)S(1)}, u32[]{:S(2)}, u32[]{:S(2)}) collective-permute-start(bf16[32,2560]{1,0:T(8,128)(2,1)S(1)} %slice.30), channel_id=1, source_target_pairs={{0,130},{1,131},{16,146},{17,147},{32,162},{33,163},{48,178},{49,1... | collective-permute-start | bytes 491528 | tf_op jit(solution)/shard_map/ppermute | solution.py:46
  43.7 29.5 %all-to-all-start = ((bf16[16,432,128]{2,1,0:T(8,128)(2,1)}), bf16[16,432,128]{2,1,0:T(8,128)(2,1)}, u32[]{:S(2)}, u32[]{:S(2)}) async-start(bf16[16,432,128]{2,1,0:T(8,128)(2,1)} %bitcast.70), calls=%async_computation | async-start | bytes 3538944 | tf_op jit(solution)/shard_map/all_to_all | solution.py:245
  60.0 2.4 %collective-permute-start.12 = (bf16[128,2560]{1,0:T(8,128)(2,1)S(1)}, bf16[128,2560]{1,0:T(8,128)(2,1)S(1)}, u32[]{:S(2)}, u32[]{:S(2)}) collective-permute-start(bf16[128,2560]{1,0:T(8,128)(2,1)S(1)} %constant_dynamic-update-slice_fusion.6.refs_3_.refs_6_), channel_id=1, source_target_pairs={{0,1},{1,0},{16,17},{17,16},{32,33},{33,32},{48,49},{49,48},{64,65... | collective-permute-start | bytes 1966088 | tf_op jit(solution)/shard_map/ppermute | solution.py:46
  81.9 26.0 %collective-permute-start.13 = (bf16[8,56,1024]{2,1,0:T(8,128)(2,1)}, bf16[8,56,1024]{2,1,0:T(8,128)(2,1)S(1)}, u32[]{:S(2)}, u32[]{:S(2)}) collective-permute-start(bf16[8,56,1024]{2,1,0:T(8,128)(2,1)} %get-tuple-element.35), channel_id=1, source_target_pairs={{0,128},{1,129},{16,144},{17,145},{32,160},{33,161},{48,176},{49,1... | collective-permute-start | bytes 2752520 | tf_op jit(solution)/shard_map/ppermute | solution.py:46
  91.8 29.2 %all-to-all-start.1 = ((bf16[8,56,512]{2,1,0:T(8,128)(2,1)}), bf16[8,56,512]{2,1,0:T(8,128)(2,1)S(1)}, u32[]{:S(2)}, u32[]{:S(2)}) async-start(bf16[8,56,512]{2,1,0:T(8,128)(2,1)} %outer.4), calls=%async_computation.1 | async-start | bytes 917504 | tf_op jit(solution)/shard_map/all_to_all | solution.py:269
  111.1 63.8 %copy-start.4 = (bf16[2560,432]{0,1:T(8,128)(2,1)S(1)}, bf16[2560,432]{0,1:T(8,128)(2,1)}, u32[]{:S(2)}) copy-start(bf16[2560,432]{0,1:T(8,128)(2,1)} %param.7) | copy-start | bytes 6635524
  111.1 63.8 %copy-start.16 = (s32[28]{0:T(128)S(1)}, s32[28]{0:T(128)}, u32[]{:S(2)}) copy-start(s32[28]{0:T(128)} %copy-done.15) | copy-start | bytes 340
  111.8 18.3 %collective-permute-start.14 = (bf16[56,1024]{1,0:T(8,128)(2,1)}, bf16[56,1024]{1,0:T(8,128)(2,1)S(1)}, u32[]{:S(2)}, u32[]{:S(2)}) collective-permute-start(bf16[56,1024]{1,0:T(8,128)(2,1)} %get-tuple-element.41), channel_id=1, source_target_pairs={{0,64},{1,65},{16,80},{17,81},{32,96},{33,97},{48,112},{49,113},{6... | collective-permute-start | bytes 344072 | tf_op jit(solution)/shard_map/ppermute | solution.py:46
  119.0 14.9 %collective-permute-start.15 = (bf16[56,1024]{1,0:T(8,128)(2,1)}, bf16[56,1024]{1,0:T(8,128)(2,1)S(1)}, u32[]{:S(2)}, u32[]{:S(2)}) collective-permute-start(bf16[56,1024]{1,0:T(8,128)(2,1)} %get-tuple-element.47), channel_id=1, source_target_pairs={{0,48},{1,49},{16,64},{17,65},{32,80},{33,81},{48,96},{49,97},{64,... | collective-permute-start | bytes 344072 | tf_op jit(solution)/shard_map/ppermute | solution.py:46
  121.0 6.4 %collective-permute-start.21 = (bf16[56,256]{1,0:T(8,128)(2,1)S(1)}, bf16[56,256]{1,0:T(8,128)(2,1)S(1)}, u32[]{:S(2)}, u32[]{:S(2)}) collective-permute-start(bf16[56,256]{1,0:T(8,128)(2,1)S(1)} %slice.47), channel_id=1, source_target_pairs={{0,128},{1,129},{16,144},{17,145},{32,160},{33,161},{48,176},{49,1... | collective-permute-start | bytes 86024 | tf_op jit(solution)/shard_map/ppermute | solution.py:46
  122.9 11.4 %collective-permute-start.16 = (bf16[56,1024]{1,0:T(8,128)(2,1)}, bf16[56,1024]{1,0:T(8,128)(2,1)S(1)}, u32[]{:S(2)}, u32[]{:S(2)}) collective-permute-start(bf16[56,1024]{1,0:T(8,128)(2,1)} %get-tuple-element.46), channel_id=1, source_target_pairs={{0,80},{1,81},{16,96},{17,97},{32,112},{33,113},{48,0},{49,1},{64,... | collective-permute-start | bytes 344072 | tf_op jit(solution)/shard_map/ppermute | solution.py:46
  126.0 10.1 %collective-permute-start.17 = (bf16[56,1024]{1,0:T(8,128)(2,1)S(1)}, bf16[56,1024]{1,0:T(8,128)(2,1)S(1)}, u32[]{:S(2)}, u32[]{:S(2)}) collective-permute-start(bf16[56,1024]{1,0:T(8,128)(2,1)S(1)} %get-tuple-element.45), channel_id=1, source_target_pairs={{0,32},{1,33},{16,48},{17,49},{32,64},{33,65},{48,80},{49,81},{64,... | collective-permute-start | bytes 344072 | tf_op jit(solution)/shard_map/ppermute | solution.py:46
  127.5 12.1 %collective-permute-start.18 = (bf16[56,1024]{1,0:T(8,128)(2,1)S(1)}, bf16[56,1024]{1,0:T(8,128)(2,1)S(1)}, u32[]{:S(2)}, u32[]{:S(2)}) collective-permute-start(bf16[56,1024]{1,0:T(8,128)(2,1)S(1)} %get-tuple-element.44), channel_id=1, source_target_pairs={{0,96},{1,97},{16,112},{17,113},{32,0},{33,1},{48,16},{49,17},{64,... | collective-permute-start | bytes 344072 | tf_op jit(solution)/shard_map/ppermute | solution.py:46
  130.1 9.6 %collective-permute-start.19 = (bf16[56,1024]{1,0:T(8,128)(2,1)S(1)}, bf16[56,1024]{1,0:T(8,128)(2,1)S(1)}, u32[]{:S(2)}, u32[]{:S(2)}) collective-permute-start(bf16[56,1024]{1,0:T(8,128)(2,1)S(1)} %get-tuple-element.43), channel_id=1, source_target_pairs={{0,16},{1,17},{16,32},{17,33},{32,48},{33,49},{48,64},{49,65},{64,... | collective-permute-start | bytes 344072 | tf_op jit(solution)/shard_map/ppermute | solution.py:46
  133.9 7.2 %collective-permute-start.20 = (bf16[56,1024]{1,0:T(8,128)(2,1)S(1)}, bf16[56,1024]{1,0:T(8,128)(2,1)S(1)}, u32[]{:S(2)}, u32[]{:S(2)}) collective-permute-start(bf16[56,1024]{1,0:T(8,128)(2,1)S(1)} %get-tuple-element.42), channel_id=1, source_target_pairs={{0,112},{1,113},{16,0},{17,1},{32,16},{33,17},{48,32},{49,33},{64,... | collective-permute-start | bytes 344072 | tf_op jit(solution)/shard_map/ppermute | solution.py:46
  142.2 5.2 %collective-permute-start.30 = (bf16[56,1280]{1,0:T(8,128)(2,1)S(1)}, bf16[56,1280]{1,0:T(8,128)(2,1)S(1)}, u32[]{:S(2)}, u32[]{:S(2)}) collective-permute-start(bf16[56,1280]{1,0:T(8,128)(2,1)S(1)} %pad_maximum_fusion.refs_2_), channel_id=1, source_target_pairs={{0,128},{1,129},{16,144},{17,145},{32,160},{33,161},{48,176},{49,1... | collective-permute-start | bytes 430088 | tf_op jit(solution)/shard_map/ppermute | solution.py:46
  143.1 7.6 %collective-permute-start.22 = (bf16[56,1280]{1,0:T(8,128)(2,1)S(1)}, bf16[56,1280]{1,0:T(8,128)(2,1)S(1)}, u32[]{:S(2)}, u32[]{:S(2)}) collective-permute-start(bf16[56,1280]{1,0:T(8,128)(2,1)S(1)} %pad_maximum_fusion.refs_2_), channel_id=1, source_target_pairs={{0,16},{1,17},{16,32},{17,33},{32,48},{33,49},{48,64},{49,65},{64,... | collective-permute-start | bytes 430088 | tf_op jit(solution)/shard_map/ppermute | solution.py:46
  143.4 7.3 %collective-permute-start.23 = (bf16[56,1280]{1,0:T(8,128)(2,1)S(1)}, bf16[56,1280]{1,0:T(8,128)(2,1)S(1)}, u32[]{:S(2)}, u32[]{:S(2)}) collective-permute-start(bf16[56,1280]{1,0:T(8,128)(2,1)S(1)} %pad_maximum_fusion.refs_2_), channel_id=1, source_target_pairs={{0,112},{1,113},{16,0},{17,1},{32,16},{33,17},{48,32},{49,33},{64,... | collective-permute-start | bytes 430088 | tf_op jit(solution)/shard_map/ppermute | solution.py:46
  147.4 7.8 %collective-permute-start.31 = (bf16[56,1280]{1,0:T(8,128)(2,1)S(1)}, bf16[56,1280]{1,0:T(8,128)(2,1)S(1)}, u32[]{:S(2)}, u32[]{:S(2)}) collective-permute-start(bf16[56,1280]{1,0:T(8,128)(2,1)S(1)} %collective-permute-done.30.refs_11_), channel_id=1, source_target_pairs={{0,16},{1,17},{16,32},{17,33},{32,48},{33,49},{48,64},{49,65},{64,... | collective-permute-start | bytes 430088 | tf_op jit(solution)/shard_map/ppermute | solution.py:46
  147.8 7.5 %collective-permute-start.32 = (bf16[56,1280]{1,0:T(8,128)(2,1)S(1)}, bf16[56,1280]{1,0:T(8,128)(2,1)S(1)}, u32[]{:S(2)}, u32[]{:S(2)}) collective-permute-start(bf16[56,1280]{1,0:T(8,128)(2,1)S(1)} %collective-permute-done.30.refs_11_), channel_id=1, source_target_pairs={{0,112},{1,113},{16,0},{17,1},{32,16},{33,17},{48,32},{49,33},{64,... | collective-permute-start | bytes 430088 | tf_op jit(solution)/shard_map/ppermute | solution.py:46
  150.7 7.8 %collective-permute-start.24 = (bf16[56,1280]{1,0:T(8,128)(2,1)S(1)}, bf16[56,1280]{1,0:T(8,128)(2,1)S(1)}, u32[]{:S(2)}, u32[]{:S(2)}) collective-permute-start(bf16[56,1280]{1,0:T(8,128)(2,1)S(1)} %collective-permute-done.22.refs_3_), channel_id=1, source_target_pairs={{0,16},{1,17},{16,32},{17,33},{32,48},{33,49},{48,64},{49,65},{64,... | collective-permute-start | bytes 430088 | tf_op jit(solution)/shard_map/ppermute | solution.py:46
  150.7 7.8 %collective-permute-start.25 = (bf16[56,1280]{1,0:T(8,128)(2,1)S(1)}, bf16[56,1280]{1,0:T(8,128)(2,1)S(1)}, u32[]{:S(2)}, u32[]{:S(2)}) collective-permute-start(bf16[56,1280]{1,0:T(8,128)(2,1)S(1)} %collective-permute-done.23.refs_4_), channel_id=1, source_target_pairs={{0,112},{1,113},{16,0},{17,1},{32,16},{33,17},{48,32},{49,33},{64,... | collective-permute-start | bytes 430088 | tf_op jit(solution)/shard_map/ppermute | solution.py:46
  155.3 7.2 %collective-permute-start.33 = (bf16[56,1280]{1,0:T(8,128)(2,1)S(1)}, bf16[56,1280]{1,0:T(8,128)(2,1)S(1)}, u32[]{:S(2)}, u32[]{:S(2)}) collective-permute-start(bf16[56,1280]{1,0:T(8,128)(2,1)S(1)} %collective-permute-done.31.refs_12_), channel_id=1, source_target_pairs={{0,16},{1,17},{16,32},{17,33},{32,48},{33,49},{48,64},{49,65},{64,... | collective-permute-start | bytes 430088 | tf_op jit(solution)/shard_map/ppermute | solution.py:46
  155.3 7.2 %collective-permute-start.34 = (bf16[56,1280]{1,0:T(8,128)(2,1)S(1)}, bf16[56,1280]{1,0:T(8,128)(2,1)S(1)}, u32[]{:S(2)}, u32[]{:S(2)}) collective-permute-start(bf16[56,1280]{1,0:T(8,128)(2,1)S(1)} %collective-permute-done.32.refs_13_), channel_id=1, source_target_pairs={{0,112},{1,113},{16,0},{17,1},{32,16},{33,17},{48,32},{49,33},{64,... | collective-permute-start | bytes 430088 | tf_op jit(solution)/shard_map/ppermute | solution.py:46
  158.5 7.2 %collective-permute-start.26 = (bf16[56,1280]{1,0:T(8,128)(2,1)S(1)}, bf16[56,1280]{1,0:T(8,128)(2,1)S(1)}, u32[]{:S(2)}, u32[]{:S(2)}) collective-permute-start(bf16[56,1280]{1,0:T(8,128)(2,1)S(1)} %collective-permute-done.24.refs_5_), channel_id=1, source_target_pairs={{0,16},{1,17},{16,32},{17,33},{32,48},{33,49},{48,64},{49,65},{64,... | collective-permute-start | bytes 430088 | tf_op jit(solution)/shard_map/ppermute | solution.py:46
  158.5 7.2 %collective-permute-start.27 = (bf16[56,1280]{1,0:T(8,128)(2,1)S(1)}, bf16[56,1280]{1,0:T(8,128)(2,1)S(1)}, u32[]{:S(2)}, u32[]{:S(2)}) collective-permute-start(bf16[56,1280]{1,0:T(8,128)(2,1)S(1)} %collective-permute-done.25.refs_6_), channel_id=1, source_target_pairs={{0,112},{1,113},{16,0},{17,1},{32,16},{33,17},{48,32},{49,33},{64,... | collective-permute-start | bytes 430088 | tf_op jit(solution)/shard_map/ppermute | solution.py:46
  162.4 6.8 %collective-permute-start.35 = (bf16[56,1280]{1,0:T(8,128)(2,1)S(1)}, bf16[56,1280]{1,0:T(8,128)(2,1)S(1)}, u32[]{:S(2)}, u32[]{:S(2)}) collective-permute-start(bf16[56,1280]{1,0:T(8,128)(2,1)S(1)} %collective-permute-done.33.refs_14_), channel_id=1, source_target_pairs={{0,16},{1,17},{16,32},{17,33},{32,48},{33,49},{48,64},{49,65},{64,... | collective-permute-start | bytes 430088 | tf_op jit(solution)/shard_map/ppermute | solution.py:46
  162.4 6.8 %collective-permute-start.36 = (bf16[56,1280]{1,0:T(8,128)(2,1)S(1)}, bf16[56,1280]{1,0:T(8,128)(2,1)S(1)}, u32[]{:S(2)}, u32[]{:S(2)}) collective-permute-start(bf16[56,1280]{1,0:T(8,128)(2,1)S(1)} %collective-permute-done.34.refs_15_), channel_id=1, source_target_pairs={{0,112},{1,113},{16,0},{17,1},{32,16},{33,17},{48,32},{49,33},{64,... | collective-permute-start | bytes 430088 | tf_op jit(solution)/shard_map/ppermute | solution.py:46
  165.7 7.0 %collective-permute-start.28 = (bf16[56,640]{1,0:T(8,128)(2,1)S(1)}, bf16[56,640]{1,0:T(8,128)(2,1)S(1)}, u32[]{:S(2)}, u32[]{:S(2)}) collective-permute-start(bf16[56,640]{1,0:T(8,128)(2,1)S(1)} %slice.39), channel_id=1, source_target_pairs={{0,16},{1,17},{16,32},{17,33},{32,48},{33,49},{48,64},{49,65},{64,... | collective-permute-start | bytes 215048 | tf_op jit(solution)/shard_map/ppermute | solution.py:46
  165.8 6.9 %collective-permute-start.29 = (bf16[56,640]{1,0:T(8,128)(2,1)S(1)}, bf16[56,640]{1,0:T(8,128)(2,1)S(1)}, u32[]{:S(2)}, u32[]{:S(2)}) collective-permute-start(bf16[56,640]{1,0:T(8,128)(2,1)S(1)} %slice.40), channel_id=1, source_target_pairs={{0,112},{1,113},{16,0},{17,1},{32,16},{33,17},{48,32},{49,33},{64,... | collective-permute-start | bytes 215048 | tf_op jit(solution)/shard_map/ppermute | solution.py:46
  169.2 5.6 %collective-permute-start.37 = (bf16[56,640]{1,0:T(8,128)(2,1)S(1)}, bf16[56,640]{1,0:T(8,128)(2,1)S(1)}, u32[]{:S(2)}, u32[]{:S(2)}) collective-permute-start(bf16[56,640]{1,0:T(8,128)(2,1)S(1)} %slice.41), channel_id=1, source_target_pairs={{0,16},{1,17},{16,32},{17,33},{32,48},{33,49},{48,64},{49,65},{64,... | collective-permute-start | bytes 215048 | tf_op jit(solution)/shard_map/ppermute | solution.py:46
  169.3 5.5 %collective-permute-start.38 = (bf16[56,640]{1,0:T(8,128)(2,1)S(1)}, bf16[56,640]{1,0:T(8,128)(2,1)S(1)}, u32[]{:S(2)}, u32[]{:S(2)}) collective-permute-start(bf16[56,640]{1,0:T(8,128)(2,1)S(1)} %slice.42), channel_id=1, source_target_pairs={{0,112},{1,113},{16,0},{17,1},{32,16},{33,17},{48,32},{49,33},{64,... | collective-permute-start | bytes 215048 | tf_op jit(solution)/shard_map/ppermute | solution.py:46
  (10 other events, 33.3 us)

commit v4 on v2

--- a/solution.py
+++ b/solution.py
@@ -27,6 +27,7 @@
 X_DOWN = moves(lambda x, y, z, c: ((x - 1) % NX, y, z, c))
 Z_UP = moves(lambda x, y, z, c: (x, y, (z + 1) % NZ, c))
 Z_DOWN = moves(lambda x, y, z, c: (x, y, (z - 1) % NZ, c))
+Z_AWAY = {d: moves(lambda x, y, z, c, d=d: (x, y, (z + d) % NZ, c)) for d in (4, 3, -3, 2, -2, 1, -1)}
 Y_MATE = moves(lambda x, y, z, c: (x, 3 - y, z, c))
 Y_CUT = moves(lambda x, y, z, c: (x, y ^ 1, z, c))
 CORE = moves(lambda x, y, z, c: (x, y, z, 1 - c))
@@ -176,48 +177,42 @@
 
 
 def finish_kernel(scale, table_ref, probe_ref, *refs):
-    out_ref = refs[-1]
-    side, j = pl.program_id(0), pl.program_id(1)
+    pieces, out_ref = refs[:9], refs[-1]
     z = table_ref[LOW - 1]
 
     def put(ref, away):
         row = jnp.minimum(lax.rem(z + away + NZ, NZ) * PIECE, out_ref.shape[0] - PIECE)
         out_ref[pl.ds(pl.multiple_of(row, 8), PIECE), :] = ref[...].astype(F32)
 
-    for at in range(2):
-        pieces = refs[9 * at : 9 * at + 9]
-
-        @pl.when(side == at)
-        def _():
-            for ref, away in zip(pieces[:7], AWAYS):
-                put(ref, away)
-
-        for end in range(2):
-            pl.when((side == at) & (j == end))(lambda: put(pieces[7 + end], AWAYS[7]))
-
+    for ref, away in zip(pieces[:7], AWAYS):
+        put(ref, away)
+    for end in range(2):
+        pl.when(pl.program_id(0) == end)(lambda: put(pieces[7 + end], AWAYS[7]))
     for row in range(0, out_ref.shape[0], 16):
         rows = slice(row, row + 16)
         out_ref[rows, :] = probe_ref[rows, :].astype(F32) * (out_ref[rows, :] * scale)
 
 
-def finish(table, probe_t, sides, scale):
+def finish(table, probe_t, pieces, side, scale, held):
     hidden, depth = probe_t.shape
     wide = depth // 4
-    column = lambda h, j, p: (0, 2 * lax.rem(p[LOW] + h, 2) + j)
-    ring = [pl.BlockSpec((PIECE, wide), lambda h, j, p, at=at: (0, jnp.where(h == at, j, 1 - at))) for at in range(2)]
-    end = pl.BlockSpec((PIECE, wide), lambda h, j, p: (0, 0))
+    column = pl.BlockSpec((hidden, wide), lambda j, p: (0, 2 * lax.rem(p[LOW] + side, 2) + j))
+    ring = pl.BlockSpec((PIECE, wide), lambda j, p: (0, j))
+    end = pl.BlockSpec((PIECE, wide), lambda j, p: (0, 0))
+    more = [] if held is None else [held]
     return pl.pallas_call(
         lambda *refs: finish_kernel(scale, *refs),
         grid_spec=pltpu.PrefetchScalarGridSpec(
             num_scalar_prefetch=1,
-            grid=(2, 2),
-            in_specs=[pl.BlockSpec((hidden, wide), column), *([ring[0]] * 7 + [end] * 2 + [ring[1]] * 7 + [end] * 2)],
-            out_specs=pl.BlockSpec((hidden, wide), column),
+            grid=(2,),
+            in_specs=[column, *[ring] * 7, *[end] * 2, *[pl.BlockSpec(memory_space=pl.ANY)] * len(more)],
+            out_specs=column,
         ),
         out_shape=jax.ShapeDtypeStruct(probe_t.shape, F32),
+        input_output_aliases={11: 0} if more else {},
         compiler_params=params(VMEM_PART),
         name="finish",
-    )(table, probe_t, *sides[0], *sides[1])
+    )(table, probe_t, *pieces, *more)
 
 
 def on_device(tokens, upstream, gate_weight, probe):
@@ -277,7 +272,15 @@
     (table,) = after((table,), late)
     (own,) = outer(table, 16 + 2 * rest + first, weighted, pieces, first * 256, F32, 256)
     late = ring_sum(late)
-    own = ring_sum((own + come.astype(F32)).astype(BF16))
+    def piece(d):
+        at = lax.rem(z + d + NZ, NZ)
+        mine, other = (lax.dynamic_index_in_dim(a, at, 0, keepdims=False) for a in (own, come))
+        return mine + other.astype(F32)
+
+    others = [send(piece(d).astype(BF16), pairs) for d, pairs in Z_AWAY.items()]
+    own = piece(0)
+    for other in others:
+        own = own + other.astype(F32)
     late = late[:, half:] + send(late[:, :half].astype(BF16), Y_CUT).astype(F32)
     own = jnp.concatenate([own.astype(BF16), late.astype(BF16)], 1)
 
@@ -291,7 +294,10 @@
         quarter = depth // 4
         sides.append([*gathered, send(up[:, :quarter], Z_UP), send(down[:, quarter:], Z_DOWN)])
     scale = 1.0 / (rows * lax.axis_size("fsdp") * lax.axis_size("cuts"))
-    return finish(table, probe_t, sides, scale).T
+    held = None
+    for side, pieces in enumerate(sides):
+        held = finish(table, probe_t, pieces, side, scale, held)
+    return held.T
 
 
 def solution(mesh):

time: 186 us -> 180 us (0.968)
  waiting for transfers between devices: 73.1 us -> 43 us
  starting transfers between devices: 56.2 us -> 76.7 us
  local copies, waits for them, and re-layouts: 11.6 us -> 14.2 us
    all_to_all x2 -> x1, waiting for transfers between devices: 27.1 us -> 0.01 us  [on_device(): lax.all_to_all(a, AXES, split_axis=0, concat_axis=0, axis_index_groups=Z_...]
    ppermute x32 -> x39, starting transfers between devices: 38.1 us -> 62.5 us  [send(): return lax.ppermute(value, AXES, pairs)]
    ppermute x32 -> x39, waiting for transfers between devices: 38 us -> 33.6 us  [send(): return lax.ppermute(value, AXES, pairs)]
    all_to_all x2 -> x1, starting transfers between devices: 12 us -> 8.47 us  [on_device(): lax.all_to_all(a, AXES, split_axis=0, concat_axis=0, axis_index_groups=Z_...]
    unnamed x42 -> x36, local copies, waits for them, and re-layouts: 7.37 us -> 9.19 us
    pallas_call x1 -> x2, Pallas kernels: 3.96 us -> 4.82 us  [finish(): pl.pallas_call(lambda *refs: finish_kernel(scale, *refs), grid_spec=pltpu...]
  transfers between devices with their start and end apart: 35 -> 41, of which waited for: 20 -> 16; matrix products, arithmetic and copies ran while one was open for 4% -> 4% of each run, Pallas kernels for 15% -> 17%
where the time goes in v4:
time: 180 us; the launch traced here: 179 us
  starting transfers between devices  76.7 us (43%)
  waiting for transfers between devices  43 us (24%)
  Pallas kernels  40.7 us (23%)
  local copies, waits for them, and re-layouts  14.2 us (8%)
  other arithmetic  3.94 us (2%)
    ppermute x39, starting transfers between devices, send(): return lax.ppermute(value, AXES, pairs)  62.5 us
    ppermute x39, waiting for transfers between devices, send(): return lax.ppermute(value, AXES, pairs)  33.6 us
    pallas_call x3, Pallas kernels, outer(): pl.pallas_call(weigh_outer_kernel if make else outer_kernel, grid_spec=pl...  20.8 us
    pallas_call x3, Pallas kernels, factor(): pl.pallas_call(lambda *refs: factor_kernel(weighing, *refs), grid_spec=pl...  15.2 us
    all_to_all x1, waiting for transfers between devices, on_device(): lax.all_to_all(turned, AXES, split_axis=0, concat_axis=0, axis_index_grou...  9.45 us
    unnamed x36, local copies, waits for them, and re-layouts  9.19 us
    all_to_all x1, starting transfers between devices, on_device(): lax.all_to_all(a, AXES, split_axis=0, concat_axis=0, axis_index_groups=Z_...  8.47 us
    all_to_all x1, starting transfers between devices, on_device(): lax.all_to_all(turned, AXES, split_axis=0, concat_axis=0, axis_index_grou...  5.73 us
  transfers between devices with their start and end apart: 41, of which 16 were waited for; matrix products, arithmetic and copies ran while one was open for 4% of the time, Pallas kernels for 17%

profile of v4, /device:TPU:16, one launch (start us, length us, event | category | flops | bytes accessed | tf_op | source)
XLA Modules:
  0.0 178.9 jit_solution(10055952569507065325)
XLA Ops:
  0.0 1.5 collective-permute-start
  1.5 1.7 collective-permute-start.1
  3.7 3.9 %copy.6 = bf16[6912,128]{1,0:T(8,128)(2,1)} copy(bf16[6912,128]{0,1:T(8,128)(2,1)} %bitcast.72) | data formatting | bytes 3538944 | tf_op jit(solution)/shard_map/transpose | solution.py:236
  7.7 10.2 %collective-permute-done = bf16[128,2560]{1,0:T(8,128)(2,1)S(1)} collective-permute-done((bf16[128,2560]{1,0:T(8,128)(2,1)}, bf16[128,2560]{1,0:T(8,128)(2,1)S(1)}, u32[]{:S(2)}, u32[]{:S(2)}) %collective-permute-start) | collective-permute-done | bytes 655392 | tf_op jit(solution)/shard_map/ppermute | solution.py:46
  17.9 1.5 collective-permute-done.2
  19.4 1.3 constant_dynamic-update-slice_fusion.2
  21.6 3.0 %collective-permute-start.6 = (bf16[128,2560]{1,0:T(8,128)(2,1)S(1)}, bf16[128,2560]{1,0:T(8,128)(2,1)S(1)}, u32[]{:S(2)}, u32[]{:S(2)}) collective-permute-start(bf16[128,2560]{1,0:T(8,128)(2,1)S(1)} %collective-permute-done.1), channel_id=1, source_target_pairs={{0,12},{1,13},{16,28},{17,29},{32,44},{33,45},{48,60},{49,61},{64,... | collective-permute-start | bytes 1966088 | tf_op jit(solution)/shard_map/ppermute | solution.py:46
  25.8 2.6 %copy-done.3 = bf16[2560,432]{0,1:T(8,128)(2,1)S(1)} copy-done((bf16[2560,432]{0,1:T(8,128)(2,1)S(1)}, bf16[2560,432]{0,1:T(8,128)(2,1)}, u32[]{:S(2)}) %copy-start.3) | copy-done | bytes 2211864
  28.4 6.9 %factor.3.refs_0_ = f32[2,432,512]{2,1,0:T(8,128)S(1)} custom-call(s32[28]{0:T(128)S(1)} %stack.115.refs_0_.table_ref, bf16[432,2560]{1,0:T(8,128)(2,1)S(1)} %bitcast.68, bf16[432,2560]{1,0:T(8,128)(2,1)S(1)} %bitcast.63, bf16[128,2560]{1,0:T(8,128)(2,1)S(1)} %copy-done.6, bf16[128,2560]{1,0:T(8,128)(2,1)S(1)} %collective-permute-done.3.refs_4_.refs_7_, ...), custom_call_target="tpu_custom_call" | custom-call | tf_op jit(solution)/shard_map/factor/pallas_call | solution.py:92
  35.3 4.0 %collective-permute-done.5 = bf16[128,2560]{1,0:T(8,128)(2,1)S(1)} collective-permute-done((bf16[128,2560]{1,0:T(8,128)(2,1)S(1)}, bf16[128,2560]{1,0:T(8,128)(2,1)S(1)}, u32[]{:S(2)}, u32[]{:S(2)}) %collective-permute-start.5) | collective-permute-done | bytes 655392 | tf_op jit(solution)/shard_map/ppermute | solution.py:46
  39.3 1.5 collective-permute-done.7
  43.5 1.5 collective-permute-start.10
  46.0 5.7 %all-to-all-start = ((bf16[16,432,128]{2,1,0:T(8,128)(2,1)}), bf16[16,432,128]{2,1,0:T(8,128)(2,1)}, u32[]{:S(2)}, u32[]{:S(2)}) async-start(bf16[16,432,128]{2,1,0:T(8,128)(2,1)} %bitcast.71), calls=%async_computation | async-start | bytes 3538944 | tf_op jit(solution)/shard_map/all_to_all | solution.py:239
  51.7 1.6 copy-done.4
  53.3 6.3 %factor.4.refs_1_ = f32[2,432,384]{2,1,0:T(8,128)S(1)} custom-call(s32[28]{0:T(128)S(1)} %stack.115.refs_0_.table_ref, bf16[432,2560]{1,0:T(8,128)(2,1)S(1)} %bitcast.69, bf16[432,2560]{1,0:T(8,128)(2,1)S(1)} %bitcast.64, bf16[384,2560]{1,0:T(8,128)(2,1)} %constant_dynamic-update-slice_fusion.3.refs_3_.refs_5_.refs_2_, ...), custom_call_target="tpu_custom_call" | custom-call | tf_op jit(solution)/shard_map/factor/pallas_call | solution.py:92
  59.7 1.1 copy-done.10
  61.2 1.9 %collective-permute-done.12.refs_4_.refs_10_.refs_7_ = bf16[128,2560]{1,0:T(8,128)(2,1)S(1)} collective-permute-done((bf16[128,2560]{1,0:T(8,128)(2,1)S(1)}, bf16[128,2560]{1,0:T(8,128)(2,1)S(1)}, u32[]{:S(2)}, u32[]{:S(2)}) %collective-permute-start.12) | collective-permute-done | bytes 655392 | tf_op jit(solution)/shard_map/ppermute | solution.py:46
  63.2 2.0 %factor.5.refs_2_ = f32[2,432,128]{2,1,0:T(8,128)S(1)} custom-call(s32[28]{0:T(128)S(1)} %stack.115.refs_0_.table_ref, bf16[432,2560]{1,0:T(8,128)(2,1)S(1)} %bitcast.70, bf16[432,2560]{1,0:T(8,128)(2,1)S(1)} %bitcast.65, bf16[128,2560]{1,0:T(8,128)(2,1)S(1)} %constant_dynamic-update-slice_fusion.6.refs_3_.refs_6_, ...), custom_call_target="tpu_custom_call" | custom-call | tf_op jit(solution)/shard_map/factor/pallas_call | solution.py:92
  66.0 9.4 %all-to-all-done.grad_ref = bf16[16,432,128]{2,1,0:T(8,128)(2,1)} async-done(((bf16[16,432,128]{2,1,0:T(8,128)(2,1)}), bf16[16,432,128]{2,1,0:T(8,128)(2,1)}, u32[]{:S(2)}, u32[]{:S(2)}) %all-to-all-start) | async-done | bytes 1769504 | tf_op jit(solution)/shard_map/all_to_all | solution.py:239
  75.4 8.8 %outer.3 = (bf16[432,2048]{1,0:T(8,128)(2,1)}, bf16[8,56,1024]{2,1,0:T(8,128)(2,1)}) custom-call(s32[28]{0:T(128)} %copy-done.12, bf16[16,432,128]{2,1,0:T(8,128)(2,1)} %all-to-all-done.grad_ref, f32[2,432,512]{2,1,0:T(8,128)} %copy-done.9, f32[2,432,384]{2,1,0:T(8,128)} %copy-done.10, f32[2,432,128]{2,1,0:T(8,128)} %copy-done.11, ...), custom_call_target="tpu_custom_call" | custom-call | flops 1811939328 | bytes 5963776 | tf_op jit(solution)/shard_map/outer/pallas_call | solution.py:156
  84.2 5.0 %collective-permute-start.13 = (bf16[8,56,1024]{2,1,0:T(8,128)(2,1)}, bf16[8,56,1024]{2,1,0:T(8,128)(2,1)}, u32[]{:S(2)}, u32[]{:S(2)}) collective-permute-start(bf16[8,56,1024]{2,1,0:T(8,128)(2,1)} %get-tuple-element.35), channel_id=1, source_target_pairs={{0,128},{1,129},{16,144},{17,145},{32,160},{33,161},{48,176},{49,1... | collective-permute-start | bytes 2752520 | tf_op jit(solution)/shard_map/ppermute | solution.py:46
  89.2 4.9 %outer.4 = bf16[8,56,512]{2,1,0:T(8,128)(2,1)} custom-call(s32[28]{0:T(128)} %copy-done.12, bf16[432,2048]{1,0:T(8,128)(2,1)} %get-tuple-element.37.weighted_ref, bf16[128,2560]{1,0:T(8,128)(2,1)} %refs_0_.3, bf16[384,2560]{1,0:T(8,128)(2,1)} %copy-done.1, bf16[384,2560]{1,0:T(8,128)(2,1)} %constant_dynamic-update-slice_fusion.3.refs_3_.refs_5_.refs_2_, ...), custom_call_target="tpu_custom_call" | custom-call | flops 905969664 | bytes 3866624 | tf_op jit(solution)/shard_map/outer/pallas_call | solution.py:156
  94.1 8.5 %all-to-all-start.1 = ((bf16[8,56,512]{2,1,0:T(8,128)(2,1)}), bf16[8,56,512]{2,1,0:T(8,128)(2,1)S(1)}, u32[]{:S(2)}, u32[]{:S(2)}) async-start(bf16[8,56,512]{2,1,0:T(8,128)(2,1)} %outer.4), calls=%async_computation.1 | async-start | bytes 917504 | tf_op jit(solution)/shard_map/all_to_all | solution.py:263
  102.6 7.1 %outer.5 = f32[8,56,1024]{2,1,0:T(8,128)} custom-call(s32[28]{0:T(128)} %copy-done.12, bf16[432,2048]{1,0:T(8,128)(2,1)} %get-tuple-element.37.weighted_ref, bf16[128,2560]{1,0:T(8,128)(2,1)} %refs_0_.3, bf16[384,2560]{1,0:T(8,128)(2,1)} %copy-done.1, bf16[384,2560]{1,0:T(8,128)(2,1)} %constant_dynamic-update-slice_fusion.3.refs_3_.refs_5_.refs_2_, ...), custom_call_target="tpu_custom_call" | custom-call | flops 1811939328 | bytes 5963776 | tf_op jit(solution)/shard_map/outer/pallas_call | solution.py:156
  110.3 2.7 %fusion.7 = (bf16[56,1024]{1,0:T(8,128)(2,1)S(1)}, bf16[56,1024]{1,0:T(8,128)(2,1)}, bf16[56,1024]{1,0:T(8,128)(2,1)}, bf16[56,1024]{1,0:T(8,128)(2,1)}, bf16[56...) fusion(f32[8,56,1024]{2,1,0:T(8,128)} %outer.5, s32[]{:T(128)S(6)} %select_n.110, ...), kind=kLoop, calls=%fused_computation.17 | loop fusion | flops 1204224 | bytes 3211292 | tf_op jit(solution)/shard_map/convert_element_type | solution.py:280
  113.0 7.3 %collective-permute-start.14 = (bf16[56,1024]{1,0:T(8,128)(2,1)S(1)}, bf16[56,1024]{1,0:T(8,128)(2,1)S(1)}, u32[]{:S(2)}, u32[]{:S(2)}) collective-permute-start(bf16[56,1024]{1,0:T(8,128)(2,1)S(1)} %get-tuple-element.39), channel_id=1, source_target_pairs={{0,64},{1,65},{16,80},{17,81},{32,96},{33,97},{48,112},{49,113},{6... | collective-permute-start | bytes 344072 | tf_op jit(solution)/shard_map/ppermute | solution.py:46
  120.3 1.9 %collective-permute-start.15 = (bf16[56,1024]{1,0:T(8,128)(2,1)}, bf16[56,1024]{1,0:T(8,128)(2,1)S(1)}, u32[]{:S(2)}, u32[]{:S(2)}) collective-permute-start(bf16[56,1024]{1,0:T(8,128)(2,1)} %get-tuple-element.45), channel_id=1, source_target_pairs={{0,48},{1,49},{16,64},{17,65},{32,80},{33,81},{48,96},{49,97},{64,... | collective-permute-start | bytes 344072 | tf_op jit(solution)/shard_map/ppermute | solution.py:46
  122.3 1.8 %collective-permute-start.21 = (bf16[56,256]{1,0:T(8,128)(2,1)S(1)}, bf16[56,256]{1,0:T(8,128)(2,1)S(1)}, u32[]{:S(2)}, u32[]{:S(2)}) collective-permute-start(bf16[56,256]{1,0:T(8,128)(2,1)S(1)} %slice.47), channel_id=1, source_target_pairs={{0,128},{1,129},{16,144},{17,145},{32,160},{33,161},{48,176},{49,1... | collective-permute-start | bytes 86024 | tf_op jit(solution)/shard_map/ppermute | solution.py:46
  124.1 3.1 %collective-permute-start.16 = (bf16[56,1024]{1,0:T(8,128)(2,1)}, bf16[56,1024]{1,0:T(8,128)(2,1)S(1)}, u32[]{:S(2)}, u32[]{:S(2)}) collective-permute-start(bf16[56,1024]{1,0:T(8,128)(2,1)} %get-tuple-element.44), channel_id=1, source_target_pairs={{0,80},{1,81},{16,96},{17,97},{32,112},{33,113},{48,0},{49,1},{64,... | collective-permute-start | bytes 344072 | tf_op jit(solution)/shard_map/ppermute | solution.py:46
  127.2 1.5 collective-permute-start.17
  128.7 2.7 %collective-permute-start.18 = (bf16[56,1024]{1,0:T(8,128)(2,1)}, bf16[56,1024]{1,0:T(8,128)(2,1)S(1)}, u32[]{:S(2)}, u32[]{:S(2)}) collective-permute-start(bf16[56,1024]{1,0:T(8,128)(2,1)} %get-tuple-element.42), channel_id=1, source_target_pairs={{0,96},{1,97},{16,112},{17,113},{32,0},{33,1},{48,16},{49,17},{64,... | collective-permute-start | bytes 344072 | tf_op jit(solution)/shard_map/ppermute | solution.py:46
  131.4 1.0 collective-permute-start.19
  132.4 2.5 %collective-permute-done.15 = bf16[56,1024]{1,0:T(8,128)(2,1)S(1)} collective-permute-done((bf16[56,1024]{1,0:T(8,128)(2,1)}, bf16[56,1024]{1,0:T(8,128)(2,1)S(1)}, u32[]{:S(2)}, u32[]{:S(2)}) %collective-permute-start.15) | collective-permute-done | bytes 114720 | tf_op jit(solution)/shard_map/ppermute | solution.py:46
  136.4 4.3 %collective-permute-done.18 = bf16[56,1024]{1,0:T(8,128)(2,1)S(1)} collective-permute-done((bf16[56,1024]{1,0:T(8,128)(2,1)}, bf16[56,1024]{1,0:T(8,128)(2,1)S(1)}, u32[]{:S(2)}, u32[]{:S(2)}) %collective-permute-start.18) | collective-permute-done | bytes 114720 | tf_op jit(solution)/shard_map/ppermute | solution.py:46
  140.7 1.8 %collective-permute-done.20 = bf16[56,1024]{1,0:T(8,128)(2,1)S(1)} collective-permute-done((bf16[56,1024]{1,0:T(8,128)(2,1)}, bf16[56,1024]{1,0:T(8,128)(2,1)S(1)}, u32[]{:S(2)}, u32[]{:S(2)}) %collective-permute-start.20) | collective-permute-done | bytes 114720 | tf_op jit(solution)/shard_map/ppermute | solution.py:46
  142.5 1.2 fusion.6
  144.7 2.8 %collective-permute-start.32 = (bf16[56,1280]{1,0:T(8,128)(2,1)S(1)}, bf16[56,1280]{1,0:T(8,128)(2,1)S(1)}, u32[]{:S(2)}, u32[]{:S(2)}) collective-permute-start(bf16[56,1280]{1,0:T(8,128)(2,1)S(1)} %pad_maximum_fusion.refs_2_), channel_id=1, source_target_pairs={{0,112},{1,113},{16,0},{17,1},{32,16},{33,17},{48,32},{49,33},{64,... | collective-permute-start | bytes 430088 | tf_op jit(solution)/shard_map/ppermute | solution.py:46
  147.5 1.4 collective-permute-done.22.refs_2_
  149.2 2.9 %collective-permute-start.24 = (bf16[56,1280]{1,0:T(8,128)(2,1)S(1)}, bf16[56,1280]{1,0:T(8,128)(2,1)S(1)}, u32[]{:S(2)}, u32[]{:S(2)}) collective-permute-start(bf16[56,1280]{1,0:T(8,128)(2,1)S(1)} %collective-permute-done.22.refs_2_), channel_id=1, source_target_pairs={{0,112},{1,113},{16,0},{17,1},{32,16},{33,17},{48,32},{49,33},{64,... | collective-permute-start | bytes 430088 | tf_op jit(solution)/shard_map/ppermute | solution.py:46
  152.1 3.2 %collective-permute-start.34 = (bf16[56,1280]{1,0:T(8,128)(2,1)S(1)}, bf16[56,1280]{1,0:T(8,128)(2,1)S(1)}, u32[]{:S(2)}, u32[]{:S(2)}) collective-permute-start(bf16[56,1280]{1,0:T(8,128)(2,1)S(1)} %collective-permute-done.32.refs_4_), channel_id=1, source_target_pairs={{0,112},{1,113},{16,0},{17,1},{32,16},{33,17},{48,32},{49,33},{64,... | collective-permute-start | bytes 430088 | tf_op jit(solution)/shard_map/ppermute | solution.py:46
  155.3 1.4 collective-permute-done.23.refs_3_
  156.7 3.2 %collective-permute-start.26 = (bf16[56,1280]{1,0:T(8,128)(2,1)S(1)}, bf16[56,1280]{1,0:T(8,128)(2,1)S(1)}, u32[]{:S(2)}, u32[]{:S(2)}) collective-permute-start(bf16[56,1280]{1,0:T(8,128)(2,1)S(1)} %collective-permute-done.24.refs_4_), channel_id=1, source_target_pairs={{0,112},{1,113},{16,0},{17,1},{32,16},{33,17},{48,32},{49,33},{64,... | collective-permute-start | bytes 430088 | tf_op jit(solution)/shard_map/ppermute | solution.py:46
  159.9 3.2 %collective-permute-start.36 = (bf16[56,1280]{1,0:T(8,128)(2,1)S(1)}, bf16[56,1280]{1,0:T(8,128)(2,1)S(1)}, u32[]{:S(2)}, u32[]{:S(2)}) collective-permute-start(bf16[56,1280]{1,0:T(8,128)(2,1)S(1)} %collective-permute-done.34.refs_6_), channel_id=1, source_target_pairs={{0,112},{1,113},{16,0},{17,1},{32,16},{33,17},{48,32},{49,33},{64,... | collective-permute-start | bytes 430088 | tf_op jit(solution)/shard_map/ppermute | solution.py:46
  163.6 3.2 %collective-permute-start.28 = (bf16[56,1280]{1,0:T(8,128)(2,1)S(1)}, bf16[56,1280]{1,0:T(8,128)(2,1)S(1)}, u32[]{:S(2)}, u32[]{:S(2)}) collective-permute-start(bf16[56,1280]{1,0:T(8,128)(2,1)S(1)} %collective-permute-done.26.refs_6_), channel_id=1, source_target_pairs={{0,112},{1,113},{16,0},{17,1},{32,16},{33,17},{48,32},{49,33},{64,... | collective-permute-start | bytes 430088 | tf_op jit(solution)/shard_map/ppermute | solution.py:46
  167.0 3.3 %collective-permute-start.38 = (bf16[56,640]{1,0:T(8,128)(2,1)S(1)}, bf16[56,640]{1,0:T(8,128)(2,1)S(1)}, u32[]{:S(2)}, u32[]{:S(2)}) collective-permute-start(bf16[56,640]{1,0:T(8,128)(2,1)S(1)} %slice.42), channel_id=1, source_target_pairs={{0,112},{1,113},{16,0},{17,1},{32,16},{33,17},{48,32},{49,33},{64,... | collective-permute-start | bytes 215048 | tf_op jit(solution)/shard_map/ppermute | solution.py:46
  170.8 3.3 %collective-permute-start.30 = (bf16[56,640]{1,0:T(8,128)(2,1)S(1)}, bf16[56,640]{1,0:T(8,128)(2,1)S(1)}, u32[]{:S(2)}, u32[]{:S(2)}) collective-permute-start(bf16[56,640]{1,0:T(8,128)(2,1)S(1)} %slice.40), channel_id=1, source_target_pairs={{0,112},{1,113},{16,0},{17,1},{32,16},{33,17},{48,32},{49,33},{64,... | collective-permute-start | bytes 215048 | tf_op jit(solution)/shard_map/ppermute | solution.py:46
  174.1 2.4 %finish.2.refs_11_ = f32[432,2560]{1,0:T(8,128)} custom-call(s32[28]{0:T(128)S(1)} %copy-done.13, bf16[432,2560]{1,0:T(8,128)(2,1)S(1)} %bitcast.66, bf16[56,1280]{1,0:T(8,128)(2,1)S(1)} %pad_maximum_fusion.refs_2_, bf16[56,1280]{1,0:T(8,128)(2,1)S(1)} %collective-permute-done.31.refs_3_, bf16[56,1280]{1,0:T(8,128)(2,1)S(1)} %collective-permute-done.32.refs_4_, ...), custom_call_target="tpu_custom_call" | custom-call | tf_op jit(solution)/shard_map/finish/pallas_call | solution.py:203
  176.5 2.4 %finish.3 = f32[432,2560]{1,0:T(8,128)} custom-call(s32[28]{0:T(128)S(1)} %copy-done.13, bf16[432,2560]{1,0:T(8,128)(2,1)S(1)} %bitcast.67, bf16[56,1280]{1,0:T(8,128)(2,1)S(1)} %collective-permute-done.22.refs_2_, bf16[56,1280]{1,0:T(8,128)(2,1)S(1)} %collective-permute-done.23.refs_3_, ...), custom_call_target="tpu_custom_call", output_to_operand_aliasing={{}: (11, {})} | custom-call | tf_op jit(solution)/shard_map/finish/pallas_call | solution.py:203
  (96 shorter events, 12.4 us)
Async XLA Ops:
  0.0 17.9 %collective-permute-start = (bf16[128,2560]{1,0:T(8,128)(2,1)}, bf16[128,2560]{1,0:T(8,128)(2,1)S(1)}, u32[]{:S(2)}, u32[]{:S(2)}) collective-permute-start(bf16[128,2560]{1,0:T(8,128)(2,1)} %refs_0_.3), channel_id=1, source_target_pairs={{0,4},{1,5},{16,20},{17,21},{32,36},{33,37},{48,52},{49,53},{64,68... | collective-permute-start | bytes 1966088 | tf_op jit(solution)/shard_map/ppermute | solution.py:46
  1.5 16.4 %collective-permute-start.1 = (bf16[128,2560]{1,0:T(8,128)(2,1)}, bf16[128,2560]{1,0:T(8,128)(2,1)S(1)}, u32[]{:S(2)}, u32[]{:S(2)}) collective-permute-start(bf16[128,2560]{1,0:T(8,128)(2,1)} %refs_0_.3), channel_id=1, source_target_pairs={{0,12},{1,13},{16,28},{17,29},{32,44},{33,45},{48,60},{49,61},{64,... | collective-permute-start | bytes 1966088 | tf_op jit(solution)/shard_map/ppermute | solution.py:46
  3.2 16.1 %collective-permute-start.2 = (bf16[128,2560]{1,0:T(8,128)(2,1)}, bf16[128,2560]{1,0:T(8,128)(2,1)S(1)}, u32[]{:S(2)}, u32[]{:S(2)}) collective-permute-start(bf16[128,2560]{1,0:T(8,128)(2,1)} %refs_0_.3), channel_id=1, source_target_pairs={{0,130},{1,131},{16,146},{17,147},{32,162},{33,163},{48,178},{49,1... | collective-permute-start | bytes 1966088 | tf_op jit(solution)/shard_map/ppermute | solution.py:46
  7.7 55.5 %copy-start.12 = (s32[28]{0:T(128)}, s32[28]{0:T(128)S(1)}, u32[]{:S(2)}) copy-start(s32[28]{0:T(128)S(1)} %stack.115.refs_0_.table_ref) | copy-start | bytes 340
  19.4 6.4 %copy-start = (bf16[2560,432]{0,1:T(8,128)(2,1)S(1)}, bf16[2560,432]{0,1:T(8,128)(2,1)}, u32[]{:S(2)}) copy-start(bf16[2560,432]{0,1:T(8,128)(2,1)} %param.7) | copy-start | bytes 6635524
  20.8 14.5 %copy-start.1 = (bf16[384,2560]{1,0:T(8,128)(2,1)}, bf16[384,2560]{1,0:T(8,128)(2,1)S(1)}, u32[]{:S(2)}) copy-start(bf16[384,2560]{1,0:T(8,128)(2,1)S(1)} %constant_dynamic-update-slice_fusion.refs_5_.refs_4_.refs_1_) | copy-start | bytes 5898244
  20.8 5.0 %collective-permute-start.4 = (bf16[384,2560]{1,0:T(8,128)(2,1)S(1)}, bf16[384,2560]{1,0:T(8,128)(2,1)S(1)}, u32[]{:S(2)}, u32[]{:S(2)}) collective-permute-start(bf16[384,2560]{1,0:T(8,128)(2,1)S(1)} %constant_dynamic-update-slice_fusion.refs_5_.refs_4_.refs_1_), channel_id=1, source_target_pairs={{0,1},{1,0},{16,17},{17,16},{32,33},{33,32},{48,49},{49,48},{64,65... | collective-permute-start | bytes 5898248 | tf_op jit(solution)/shard_map/ppermute | solution.py:46
  20.9 4.9 %collective-permute-start.3 = (bf16[128,2560]{1,0:T(8,128)(2,1)S(1)}, bf16[128,2560]{1,0:T(8,128)(2,1)S(1)}, u32[]{:S(2)}, u32[]{:S(2)}) collective-permute-start(bf16[128,2560]{1,0:T(8,128)(2,1)S(1)} %copy-done.6), channel_id=1, source_target_pairs={{0,1},{1,0},{16,17},{17,16},{32,33},{33,32},{48,49},{49,48},{64,65... | collective-permute-start | bytes 1966088 | tf_op jit(solution)/shard_map/ppermute | solution.py:46
  21.4 18.0 %collective-permute-start.5 = (bf16[128,2560]{1,0:T(8,128)(2,1)S(1)}, bf16[128,2560]{1,0:T(8,128)(2,1)S(1)}, u32[]{:S(2)}, u32[]{:S(2)}) collective-permute-start(bf16[128,2560]{1,0:T(8,128)(2,1)S(1)} %collective-permute-done.2), channel_id=1, source_target_pairs={{0,4},{1,5},{16,20},{17,21},{32,36},{33,37},{48,52},{49,53},{64,68... | collective-permute-start | bytes 1966088 | tf_op jit(solution)/shard_map/ppermute | solution.py:46
  21.6 17.7 %collective-permute-start.6 = (bf16[128,2560]{1,0:T(8,128)(2,1)S(1)}, bf16[128,2560]{1,0:T(8,128)(2,1)S(1)}, u32[]{:S(2)}, u32[]{:S(2)}) collective-permute-start(bf16[128,2560]{1,0:T(8,128)(2,1)S(1)} %collective-permute-done.1), channel_id=1, source_target_pairs={{0,12},{1,13},{16,28},{17,29},{32,44},{33,45},{48,60},{49,61},{64,... | collective-permute-start | bytes 1966088 | tf_op jit(solution)/shard_map/ppermute | solution.py:46
  24.6 16.2 %collective-permute-start.7 = (bf16[128,2560]{1,0:T(8,128)(2,1)S(1)}, bf16[128,2560]{1,0:T(8,128)(2,1)S(1)}, u32[]{:S(2)}, u32[]{:S(2)}) collective-permute-start(bf16[128,2560]{1,0:T(8,128)(2,1)S(1)} %collective-permute-done.1), channel_id=1, source_target_pairs={{0,130},{1,131},{16,146},{17,147},{32,162},{33,163},{48,178},{49,1... | collective-permute-start | bytes 1966088 | tf_op jit(solution)/shard_map/ppermute | solution.py:46
  25.8 9.5 %copy-start.7 = (bf16[128,2560]{1,0:T(8,128)(2,1)}, bf16[128,2560]{1,0:T(8,128)(2,1)S(1)}, u32[]{:S(2)}) copy-start(bf16[128,2560]{1,0:T(8,128)(2,1)S(1)} %collective-permute-done.3.refs_4_.refs_7_) | copy-start | bytes 1966084
  25.8 9.5 %copy-start.2 = (bf16[384,2560]{1,0:T(8,128)(2,1)}, bf16[384,2560]{1,0:T(8,128)(2,1)S(1)}, u32[]{:S(2)}) copy-start(bf16[384,2560]{1,0:T(8,128)(2,1)S(1)} %collective-permute-done.4.refs_6_.refs_8_.refs_5_) | copy-start | bytes 5898244
  35.3 7.3 %copy-start.9 = (f32[2,432,512]{2,1,0:T(8,128)}, f32[2,432,512]{2,1,0:T(8,128)S(1)}, u32[]{:S(2)}) copy-start(f32[2,432,512]{2,1,0:T(8,128)S(1)} %factor.3.refs_0_) | copy-start | bytes 5308420
  43.5 8.2 %collective-permute-start.8 = (bf16[384,2560]{1,0:T(8,128)(2,1)}, bf16[384,2560]{1,0:T(8,128)(2,1)}, u32[]{:S(2)}, u32[]{:S(2)}) collective-permute-start(bf16[384,2560]{1,0:T(8,128)(2,1)} %constant_dynamic-update-slice_fusion.3.refs_3_.refs_5_.refs_2_), channel_id=1, source_target_pairs={{0,1},{1,0},{16,17},{17,16},{32,33},{33,32},{48,49},{49,48},{64,65... | collective-permute-start | bytes 5898248 | tf_op jit(solution)/shard_map/ppermute | solution.py:46
  43.5 17.2 %collective-permute-start.10 = (bf16[48,2560]{1,0:T(8,128)(2,1)S(1)}, bf16[48,2560]{1,0:T(8,128)(2,1)S(1)}, u32[]{:S(2)}, u32[]{:S(2)}) collective-permute-start(bf16[48,2560]{1,0:T(8,128)(2,1)S(1)} %slice.29), channel_id=1, source_target_pairs={{0,12},{1,13},{16,28},{17,29},{32,44},{33,45},{48,60},{49,61},{64,... | collective-permute-start | bytes 737288 | tf_op jit(solution)/shard_map/ppermute | solution.py:46
  45.0 15.7 %collective-permute-start.9 = (bf16[48,2560]{1,0:T(8,128)(2,1)S(1)}, bf16[48,2560]{1,0:T(8,128)(2,1)S(1)}, u32[]{:S(2)}, u32[]{:S(2)}) collective-permute-start(bf16[48,2560]{1,0:T(8,128)(2,1)S(1)} %slice.28), channel_id=1, source_target_pairs={{0,4},{1,5},{16,20},{17,21},{32,36},{33,37},{48,52},{49,53},{64,68... | collective-permute-start | bytes 737288 | tf_op jit(solution)/shard_map/ppermute | solution.py:46
  45.5 15.2 %collective-permute-start.11 = (bf16[32,2560]{1,0:T(8,128)(2,1)S(1)}, bf16[32,2560]{1,0:T(8,128)(2,1)S(1)}, u32[]{:S(2)}, u32[]{:S(2)}) collective-permute-start(bf16[32,2560]{1,0:T(8,128)(2,1)S(1)} %slice.30), channel_id=1, source_target_pairs={{0,130},{1,131},{16,146},{17,147},{32,162},{33,163},{48,178},{49,1... | collective-permute-start | bytes 491528 | tf_op jit(solution)/shard_map/ppermute | solution.py:46
  46.0 29.5 %all-to-all-start = ((bf16[16,432,128]{2,1,0:T(8,128)(2,1)}), bf16[16,432,128]{2,1,0:T(8,128)(2,1)}, u32[]{:S(2)}, u32[]{:S(2)}) async-start(bf16[16,432,128]{2,1,0:T(8,128)(2,1)} %bitcast.71), calls=%async_computation | async-start | bytes 3538944 | tf_op jit(solution)/shard_map/all_to_all | solution.py:239
  60.8 2.4 %collective-permute-start.12 = (bf16[128,2560]{1,0:T(8,128)(2,1)S(1)}, bf16[128,2560]{1,0:T(8,128)(2,1)S(1)}, u32[]{:S(2)}, u32[]{:S(2)}) collective-permute-start(bf16[128,2560]{1,0:T(8,128)(2,1)S(1)} %constant_dynamic-update-slice_fusion.6.refs_3_.refs_6_), channel_id=1, source_target_pairs={{0,1},{1,0},{16,17},{17,16},{32,33},{33,32},{48,49},{49,48},{64,65... | collective-permute-start | bytes 1966088 | tf_op jit(solution)/shard_map/ppermute | solution.py:46
  84.2 26.1 %collective-permute-start.13 = (bf16[8,56,1024]{2,1,0:T(8,128)(2,1)}, bf16[8,56,1024]{2,1,0:T(8,128)(2,1)}, u32[]{:S(2)}, u32[]{:S(2)}) collective-permute-start(bf16[8,56,1024]{2,1,0:T(8,128)(2,1)} %get-tuple-element.35), channel_id=1, source_target_pairs={{0,128},{1,129},{16,144},{17,145},{32,160},{33,161},{48,176},{49,1... | collective-permute-start | bytes 2752520 | tf_op jit(solution)/shard_map/ppermute | solution.py:46
  94.1 28.1 %all-to-all-start.1 = ((bf16[8,56,512]{2,1,0:T(8,128)(2,1)}), bf16[8,56,512]{2,1,0:T(8,128)(2,1)S(1)}, u32[]{:S(2)}, u32[]{:S(2)}) async-start(bf16[8,56,512]{2,1,0:T(8,128)(2,1)} %outer.4), calls=%async_computation.1 | async-start | bytes 917504 | tf_op jit(solution)/shard_map/all_to_all | solution.py:263
  113.0 61.1 %copy-start.13 = (s32[28]{0:T(128)S(1)}, s32[28]{0:T(128)}, u32[]{:S(2)}) copy-start(s32[28]{0:T(128)} %copy-done.12) | copy-start | bytes 340
  113.0 18.4 %collective-permute-start.14 = (bf16[56,1024]{1,0:T(8,128)(2,1)S(1)}, bf16[56,1024]{1,0:T(8,128)(2,1)S(1)}, u32[]{:S(2)}, u32[]{:S(2)}) collective-permute-start(bf16[56,1024]{1,0:T(8,128)(2,1)S(1)} %get-tuple-element.39), channel_id=1, source_target_pairs={{0,64},{1,65},{16,80},{17,81},{32,96},{33,97},{48,112},{49,113},{6... | collective-permute-start | bytes 344072 | tf_op jit(solution)/shard_map/ppermute | solution.py:46
  120.3 14.6 %collective-permute-start.15 = (bf16[56,1024]{1,0:T(8,128)(2,1)}, bf16[56,1024]{1,0:T(8,128)(2,1)S(1)}, u32[]{:S(2)}, u32[]{:S(2)}) collective-permute-start(bf16[56,1024]{1,0:T(8,128)(2,1)} %get-tuple-element.45), channel_id=1, source_target_pairs={{0,48},{1,49},{16,64},{17,65},{32,80},{33,81},{48,96},{49,97},{64,... | collective-permute-start | bytes 344072 | tf_op jit(solution)/shard_map/ppermute | solution.py:46
  122.3 6.4 %collective-permute-start.21 = (bf16[56,256]{1,0:T(8,128)(2,1)S(1)}, bf16[56,256]{1,0:T(8,128)(2,1)S(1)}, u32[]{:S(2)}, u32[]{:S(2)}) collective-permute-start(bf16[56,256]{1,0:T(8,128)(2,1)S(1)} %slice.47), channel_id=1, source_target_pairs={{0,128},{1,129},{16,144},{17,145},{32,160},{33,161},{48,176},{49,1... | collective-permute-start | bytes 86024 | tf_op jit(solution)/shard_map/ppermute | solution.py:46
  124.1 11.4 %collective-permute-start.16 = (bf16[56,1024]{1,0:T(8,128)(2,1)}, bf16[56,1024]{1,0:T(8,128)(2,1)S(1)}, u32[]{:S(2)}, u32[]{:S(2)}) collective-permute-start(bf16[56,1024]{1,0:T(8,128)(2,1)} %get-tuple-element.44), channel_id=1, source_target_pairs={{0,80},{1,81},{16,96},{17,97},{32,112},{33,113},{48,0},{49,1},{64,... | collective-permute-start | bytes 344072 | tf_op jit(solution)/shard_map/ppermute | solution.py:46
  127.2 9.2 %collective-permute-start.17 = (bf16[56,1024]{1,0:T(8,128)(2,1)}, bf16[56,1024]{1,0:T(8,128)(2,1)S(1)}, u32[]{:S(2)}, u32[]{:S(2)}) collective-permute-start(bf16[56,1024]{1,0:T(8,128)(2,1)} %get-tuple-element.43), channel_id=1, source_target_pairs={{0,32},{1,33},{16,48},{17,49},{32,64},{33,65},{48,80},{49,81},{64,... | collective-permute-start | bytes 344072 | tf_op jit(solution)/shard_map/ppermute | solution.py:46
  128.7 11.9 %collective-permute-start.18 = (bf16[56,1024]{1,0:T(8,128)(2,1)}, bf16[56,1024]{1,0:T(8,128)(2,1)S(1)}, u32[]{:S(2)}, u32[]{:S(2)}) collective-permute-start(bf16[56,1024]{1,0:T(8,128)(2,1)} %get-tuple-element.42), channel_id=1, source_target_pairs={{0,96},{1,97},{16,112},{17,113},{32,0},{33,1},{48,16},{49,17},{64,... | collective-permute-start | bytes 344072 | tf_op jit(solution)/shard_map/ppermute | solution.py:46
  131.4 9.3 %collective-permute-start.19 = (bf16[56,1024]{1,0:T(8,128)(2,1)}, bf16[56,1024]{1,0:T(8,128)(2,1)S(1)}, u32[]{:S(2)}, u32[]{:S(2)}) collective-permute-start(bf16[56,1024]{1,0:T(8,128)(2,1)} %get-tuple-element.41), channel_id=1, source_target_pairs={{0,16},{1,17},{16,32},{17,33},{32,48},{33,49},{48,64},{49,65},{64,... | collective-permute-start | bytes 344072 | tf_op jit(solution)/shard_map/ppermute | solution.py:46
  134.9 7.6 %collective-permute-start.20 = (bf16[56,1024]{1,0:T(8,128)(2,1)}, bf16[56,1024]{1,0:T(8,128)(2,1)S(1)}, u32[]{:S(2)}, u32[]{:S(2)}) collective-permute-start(bf16[56,1024]{1,0:T(8,128)(2,1)} %get-tuple-element.40), channel_id=1, source_target_pairs={{0,112},{1,113},{16,0},{17,1},{32,16},{33,17},{48,32},{49,33},{64,... | collective-permute-start | bytes 344072 | tf_op jit(solution)/shard_map/ppermute | solution.py:46
  143.6 5.2 %collective-permute-start.22 = (bf16[56,1280]{1,0:T(8,128)(2,1)S(1)}, bf16[56,1280]{1,0:T(8,128)(2,1)S(1)}, u32[]{:S(2)}, u32[]{:S(2)}) collective-permute-start(bf16[56,1280]{1,0:T(8,128)(2,1)S(1)} %pad_maximum_fusion.refs_2_), channel_id=1, source_target_pairs={{0,128},{1,129},{16,144},{17,145},{32,160},{33,161},{48,176},{49,1... | collective-permute-start | bytes 430088 | tf_op jit(solution)/shard_map/ppermute | solution.py:46
  144.2 7.8 %collective-permute-start.31 = (bf16[56,1280]{1,0:T(8,128)(2,1)S(1)}, bf16[56,1280]{1,0:T(8,128)(2,1)S(1)}, u32[]{:S(2)}, u32[]{:S(2)}) collective-permute-start(bf16[56,1280]{1,0:T(8,128)(2,1)S(1)} %pad_maximum_fusion.refs_2_), channel_id=1, source_target_pairs={{0,16},{1,17},{16,32},{17,33},{32,48},{33,49},{48,64},{49,65},{64,... | collective-permute-start | bytes 430088 | tf_op jit(solution)/shard_map/ppermute | solution.py:46
  144.7 7.4 %collective-permute-start.32 = (bf16[56,1280]{1,0:T(8,128)(2,1)S(1)}, bf16[56,1280]{1,0:T(8,128)(2,1)S(1)}, u32[]{:S(2)}, u32[]{:S(2)}) collective-permute-start(bf16[56,1280]{1,0:T(8,128)(2,1)S(1)} %pad_maximum_fusion.refs_2_), channel_id=1, source_target_pairs={{0,112},{1,113},{16,0},{17,1},{32,16},{33,17},{48,32},{49,33},{64,... | collective-permute-start | bytes 430088 | tf_op jit(solution)/shard_map/ppermute | solution.py:46
  148.8 7.8 %collective-permute-start.23 = (bf16[56,1280]{1,0:T(8,128)(2,1)S(1)}, bf16[56,1280]{1,0:T(8,128)(2,1)S(1)}, u32[]{:S(2)}, u32[]{:S(2)}) collective-permute-start(bf16[56,1280]{1,0:T(8,128)(2,1)S(1)} %collective-permute-done.22.refs_2_), channel_id=1, source_target_pairs={{0,16},{1,17},{16,32},{17,33},{32,48},{33,49},{48,64},{49,65},{64,... | collective-permute-start | bytes 430088 | tf_op jit(solution)/shard_map/ppermute | solution.py:46
  149.2 7.5 %collective-permute-start.24 = (bf16[56,1280]{1,0:T(8,128)(2,1)S(1)}, bf16[56,1280]{1,0:T(8,128)(2,1)S(1)}, u32[]{:S(2)}, u32[]{:S(2)}) collective-permute-start(bf16[56,1280]{1,0:T(8,128)(2,1)S(1)} %collective-permute-done.22.refs_2_), channel_id=1, source_target_pairs={{0,112},{1,113},{16,0},{17,1},{32,16},{33,17},{48,32},{49,33},{64,... | collective-permute-start | bytes 430088 | tf_op jit(solution)/shard_map/ppermute | solution.py:46
  152.1 7.8 %collective-permute-start.33 = (bf16[56,1280]{1,0:T(8,128)(2,1)S(1)}, bf16[56,1280]{1,0:T(8,128)(2,1)S(1)}, u32[]{:S(2)}, u32[]{:S(2)}) collective-permute-start(bf16[56,1280]{1,0:T(8,128)(2,1)S(1)} %collective-permute-done.31.refs_3_), channel_id=1, source_target_pairs={{0,16},{1,17},{16,32},{17,33},{32,48},{33,49},{48,64},{49,65},{64,... | collective-permute-start | bytes 430088 | tf_op jit(solution)/shard_map/ppermute | solution.py:46
  152.1 7.8 %collective-permute-start.34 = (bf16[56,1280]{1,0:T(8,128)(2,1)S(1)}, bf16[56,1280]{1,0:T(8,128)(2,1)S(1)}, u32[]{:S(2)}, u32[]{:S(2)}) collective-permute-start(bf16[56,1280]{1,0:T(8,128)(2,1)S(1)} %collective-permute-done.32.refs_4_), channel_id=1, source_target_pairs={{0,112},{1,113},{16,0},{17,1},{32,16},{33,17},{48,32},{49,33},{64,... | collective-permute-start | bytes 430088 | tf_op jit(solution)/shard_map/ppermute | solution.py:46
  156.7 6.9 %collective-permute-start.25 = (bf16[56,1280]{1,0:T(8,128)(2,1)S(1)}, bf16[56,1280]{1,0:T(8,128)(2,1)S(1)}, u32[]{:S(2)}, u32[]{:S(2)}) collective-permute-start(bf16[56,1280]{1,0:T(8,128)(2,1)S(1)} %collective-permute-done.23.refs_3_), channel_id=1, source_target_pairs={{0,16},{1,17},{16,32},{17,33},{32,48},{33,49},{48,64},{49,65},{64,... | collective-permute-start | bytes 430088 | tf_op jit(solution)/shard_map/ppermute | solution.py:46
  156.7 6.9 %collective-permute-start.26 = (bf16[56,1280]{1,0:T(8,128)(2,1)S(1)}, bf16[56,1280]{1,0:T(8,128)(2,1)S(1)}, u32[]{:S(2)}, u32[]{:S(2)}) collective-permute-start(bf16[56,1280]{1,0:T(8,128)(2,1)S(1)} %collective-permute-done.24.refs_4_), channel_id=1, source_target_pairs={{0,112},{1,113},{16,0},{17,1},{32,16},{33,17},{48,32},{49,33},{64,... | collective-permute-start | bytes 430088 | tf_op jit(solution)/shard_map/ppermute | solution.py:46
  159.9 6.9 %collective-permute-start.35 = (bf16[56,1280]{1,0:T(8,128)(2,1)S(1)}, bf16[56,1280]{1,0:T(8,128)(2,1)S(1)}, u32[]{:S(2)}, u32[]{:S(2)}) collective-permute-start(bf16[56,1280]{1,0:T(8,128)(2,1)S(1)} %collective-permute-done.33.refs_5_), channel_id=1, source_target_pairs={{0,16},{1,17},{16,32},{17,33},{32,48},{33,49},{48,64},{49,65},{64,... | collective-permute-start | bytes 430088 | tf_op jit(solution)/shard_map/ppermute | solution.py:46
  159.9 7.0 %collective-permute-start.36 = (bf16[56,1280]{1,0:T(8,128)(2,1)S(1)}, bf16[56,1280]{1,0:T(8,128)(2,1)S(1)}, u32[]{:S(2)}, u32[]{:S(2)}) collective-permute-start(bf16[56,1280]{1,0:T(8,128)(2,1)S(1)} %collective-permute-done.34.refs_6_), channel_id=1, source_target_pairs={{0,112},{1,113},{16,0},{17,1},{32,16},{33,17},{48,32},{49,33},{64,... | collective-permute-start | bytes 430088 | tf_op jit(solution)/shard_map/ppermute | solution.py:46
  163.6 7.0 %collective-permute-start.27 = (bf16[56,1280]{1,0:T(8,128)(2,1)S(1)}, bf16[56,1280]{1,0:T(8,128)(2,1)S(1)}, u32[]{:S(2)}, u32[]{:S(2)}) collective-permute-start(bf16[56,1280]{1,0:T(8,128)(2,1)S(1)} %collective-permute-done.25.refs_5_), channel_id=1, source_target_pairs={{0,16},{1,17},{16,32},{17,33},{32,48},{33,49},{48,64},{49,65},{64,... | collective-permute-start | bytes 430088 | tf_op jit(solution)/shard_map/ppermute | solution.py:46
  163.6 7.1 %collective-permute-start.28 = (bf16[56,1280]{1,0:T(8,128)(2,1)S(1)}, bf16[56,1280]{1,0:T(8,128)(2,1)S(1)}, u32[]{:S(2)}, u32[]{:S(2)}) collective-permute-start(bf16[56,1280]{1,0:T(8,128)(2,1)S(1)} %collective-permute-done.26.refs_6_), channel_id=1, source_target_pairs={{0,112},{1,113},{16,0},{17,1},{32,16},{33,17},{48,32},{49,33},{64,... | collective-permute-start | bytes 430088 | tf_op jit(solution)/shard_map/ppermute | solution.py:46
  166.9 7.2 %collective-permute-start.37 = (bf16[56,640]{1,0:T(8,128)(2,1)S(1)}, bf16[56,640]{1,0:T(8,128)(2,1)S(1)}, u32[]{:S(2)}, u32[]{:S(2)}) collective-permute-start(bf16[56,640]{1,0:T(8,128)(2,1)S(1)} %slice.41), channel_id=1, source_target_pairs={{0,16},{1,17},{16,32},{17,33},{32,48},{33,49},{48,64},{49,65},{64,... | collective-permute-start | bytes 215048 | tf_op jit(solution)/shard_map/ppermute | solution.py:46
  167.0 7.1 %collective-permute-start.38 = (bf16[56,640]{1,0:T(8,128)(2,1)S(1)}, bf16[56,640]{1,0:T(8,128)(2,1)S(1)}, u32[]{:S(2)}, u32[]{:S(2)}) collective-permute-start(bf16[56,640]{1,0:T(8,128)(2,1)S(1)} %slice.42), channel_id=1, source_target_pairs={{0,112},{1,113},{16,0},{17,1},{32,16},{33,17},{48,32},{49,33},{64,... | collective-permute-start | bytes 215048 | tf_op jit(solution)/shard_map/ppermute | solution.py:46
  170.7 5.8 %collective-permute-start.29 = (bf16[56,640]{1,0:T(8,128)(2,1)S(1)}, bf16[56,640]{1,0:T(8,128)(2,1)S(1)}, u32[]{:S(2)}, u32[]{:S(2)}) collective-permute-start(bf16[56,640]{1,0:T(8,128)(2,1)S(1)} %slice.39), channel_id=1, source_target_pairs={{0,16},{1,17},{16,32},{17,33},{32,48},{33,49},{48,64},{49,65},{64,... | collective-permute-start | bytes 215048 | tf_op jit(solution)/shard_map/ppermute | solution.py:46
  170.8 5.7 %collective-permute-start.30 = (bf16[56,640]{1,0:T(8,128)(2,1)S(1)}, bf16[56,640]{1,0:T(8,128)(2,1)S(1)}, u32[]{:S(2)}, u32[]{:S(2)}) collective-permute-start(bf16[56,640]{1,0:T(8,128)(2,1)S(1)} %slice.40), channel_id=1, source_target_pairs={{0,112},{1,113},{16,0},{17,1},{32,16},{33,17},{48,32},{49,33},{64,... | collective-permute-start | bytes 215048 | tf_op jit(solution)/shard_map/ppermute | solution.py:46
  (8 other events, 15.4 us)

commit v5 on v4

--- a/solution.py
+++ b/solution.py
@@ -246,10 +246,9 @@
     near = (tokens, core_tokens, ring, core_ring)
     weight_0 = factor(table, 0, gate_t, probe_t, None, *near)
     beside, across, over = after((beside, across, over), weight_0)
-    cuts = (0, 48, 96, rows)
-    last = [a[n:m] for a, n, m in zip((beside, over, across), cuts, cuts[1:])]
+    last = [beside[: rows // 2], over[rows // 2 :]]
     beside, across, over = after((beside, across, over), *last)
-    last = [send(last[0], X_UP), send(last[1], X_DOWN), send(last[2], Y_MATE)]
+    last = [send(last[0], X_UP), send(last[1], X_DOWN)]
     far = jnp.concatenate([across, beside, over], 0)
     core_far = send(far, CORE)
     weight_1 = factor(table, 8, gate_t, probe_t, None, far, core_far)

time: 180 us -> 178 us (0.989)
  starting transfers between devices: 76.7 us -> 74.8 us
    ppermute x39 -> x38, starting transfers between devices: 62.5 us -> 60.8 us  [send(): return lax.ppermute(value, AXES, pairs)]
    ppermute x39 -> x38, waiting for transfers between devices: 33.6 us -> 33.5 us  [send(): return lax.ppermute(value, AXES, pairs)]
    unnamed x36 -> x35, local copies, waits for them, and re-layouts: 9.19 us -> 9.18 us
  transfers between devices with their start and end apart: 41 -> 40, of which waited for: 16 -> 16; matrix products, arithmetic and copies ran while one was open for 4% -> 4% of each run, Pallas kernels for 17% -> 17%
where the time goes in v5:
time: 178 us; the launch traced here: 177 us
  starting transfers between devices  74.8 us (42%)
  waiting for transfers between devices  42.9 us (24%)
  Pallas kernels  40.8 us (23%)
  local copies, waits for them, and re-layouts  14.2 us (8%)
  other arithmetic  3.94 us (2%)
    ppermute x38, starting transfers between devices, send(): return lax.ppermute(value, AXES, pairs)  60.8 us
    ppermute x38, waiting for transfers between devices, send(): return lax.ppermute(value, AXES, pairs)  33.5 us
    pallas_call x3, Pallas kernels, outer(): pl.pallas_call(weigh_outer_kernel if make else outer_kernel, grid_spec=pl...  20.8 us
    pallas_call x3, Pallas kernels, factor(): pl.pallas_call(lambda *refs: factor_kernel(weighing, *refs), grid_spec=pl...  15.2 us
    all_to_all x1, waiting for transfers between devices, on_device(): lax.all_to_all(turned, AXES, split_axis=0, concat_axis=0, axis_index_grou...  9.44 us
    unnamed x35, local copies, waits for them, and re-layouts  9.18 us
    all_to_all x1, starting transfers between devices, on_device(): lax.all_to_all(a, AXES, split_axis=0, concat_axis=0, axis_index_groups=Z_...  8.47 us
    all_to_all x1, starting transfers between devices, on_device(): lax.all_to_all(turned, AXES, split_axis=0, concat_axis=0, axis_index_grou...  5.46 us
  transfers between devices with their start and end apart: 40, of which 16 were waited for; matrix products, arithmetic and copies ran while one was open for 4% of the time, Pallas kernels for 17%

profile of v5, /device:TPU:16, one launch (start us, length us, event | category | flops | bytes accessed | tf_op | source)
XLA Modules:
  0.0 177.0 jit_solution(5061196221555245772)
XLA Ops:
  0.0 1.5 collective-permute-start
  1.5 1.7 collective-permute-start.1
  3.7 3.9 %copy.6 = bf16[6912,128]{1,0:T(8,128)(2,1)} copy(bf16[6912,128]{0,1:T(8,128)(2,1)} %bitcast.72) | data formatting | bytes 3538944 | tf_op jit(solution)/shard_map/transpose | solution.py:236
  7.7 10.2 %collective-permute-done = bf16[128,2560]{1,0:T(8,128)(2,1)S(1)} collective-permute-done((bf16[128,2560]{1,0:T(8,128)(2,1)}, bf16[128,2560]{1,0:T(8,128)(2,1)S(1)}, u32[]{:S(2)}, u32[]{:S(2)}) %collective-permute-start) | collective-permute-done | bytes 655392 | tf_op jit(solution)/shard_map/ppermute | solution.py:46
  17.9 1.5 collective-permute-done.2
  19.4 1.3 constant_dynamic-update-slice_fusion.2
  21.6 3.0 %collective-permute-start.6 = (bf16[128,2560]{1,0:T(8,128)(2,1)S(1)}, bf16[128,2560]{1,0:T(8,128)(2,1)S(1)}, u32[]{:S(2)}, u32[]{:S(2)}) collective-permute-start(bf16[128,2560]{1,0:T(8,128)(2,1)S(1)} %collective-permute-done.1), channel_id=1, source_target_pairs={{0,12},{1,13},{16,28},{17,29},{32,44},{33,45},{48,60},{49,61},{64,... | collective-permute-start | bytes 1966088 | tf_op jit(solution)/shard_map/ppermute | solution.py:46
  25.8 2.6 %copy-done.3 = bf16[2560,432]{0,1:T(8,128)(2,1)S(1)} copy-done((bf16[2560,432]{0,1:T(8,128)(2,1)S(1)}, bf16[2560,432]{0,1:T(8,128)(2,1)}, u32[]{:S(2)}) %copy-start.3) | copy-done | bytes 2211864
  28.4 6.9 %factor.3.refs_0_ = f32[2,432,512]{2,1,0:T(8,128)S(1)} custom-call(s32[28]{0:T(128)S(1)} %stack.115.refs_0_.table_ref, bf16[432,2560]{1,0:T(8,128)(2,1)S(1)} %bitcast.68, bf16[432,2560]{1,0:T(8,128)(2,1)S(1)} %bitcast.63, bf16[128,2560]{1,0:T(8,128)(2,1)S(1)} %copy-done.6, bf16[128,2560]{1,0:T(8,128)(2,1)S(1)} %collective-permute-done.3.refs_4_.refs_7_, ...), custom_call_target="tpu_custom_call" | custom-call | tf_op jit(solution)/shard_map/factor/pallas_call | solution.py:92
  35.3 4.0 %collective-permute-done.5 = bf16[128,2560]{1,0:T(8,128)(2,1)S(1)} collective-permute-done((bf16[128,2560]{1,0:T(8,128)(2,1)S(1)}, bf16[128,2560]{1,0:T(8,128)(2,1)S(1)}, u32[]{:S(2)}, u32[]{:S(2)}) %collective-permute-start.5) | collective-permute-done | bytes 655392 | tf_op jit(solution)/shard_map/ppermute | solution.py:46
  39.3 1.5 collective-permute-done.7
  43.5 1.5 collective-permute-start.10
  45.5 5.5 %all-to-all-start = ((bf16[16,432,128]{2,1,0:T(8,128)(2,1)}), bf16[16,432,128]{2,1,0:T(8,128)(2,1)}, u32[]{:S(2)}, u32[]{:S(2)}) async-start(bf16[16,432,128]{2,1,0:T(8,128)(2,1)} %bitcast.71), calls=%async_computation | async-start | bytes 3538944 | tf_op jit(solution)/shard_map/all_to_all | solution.py:239
  51.0 1.6 copy-done.4
  52.6 6.3 %factor.4.refs_1_ = f32[2,432,384]{2,1,0:T(8,128)S(1)} custom-call(s32[28]{0:T(128)S(1)} %stack.115.refs_0_.table_ref, bf16[432,2560]{1,0:T(8,128)(2,1)S(1)} %bitcast.69, bf16[432,2560]{1,0:T(8,128)(2,1)S(1)} %bitcast.64, bf16[384,2560]{1,0:T(8,128)(2,1)} %constant_dynamic-update-slice_fusion.3.refs_3_.refs_5_.refs_2_, ...), custom_call_target="tpu_custom_call" | custom-call | tf_op jit(solution)/shard_map/factor/pallas_call | solution.py:92
  58.9 1.1 copy-done.10
  60.5 1.9 %collective-permute-done.11.refs_4_.refs_10_.refs_7_ = bf16[128,2560]{1,0:T(8,128)(2,1)S(1)} collective-permute-done((bf16[128,2560]{1,0:T(8,128)(2,1)S(1)}, bf16[128,2560]{1,0:T(8,128)(2,1)S(1)}, u32[]{:S(2)}, u32[]{:S(2)}) %collective-permute-start.11) | collective-permute-done | bytes 655392 | tf_op jit(solution)/shard_map/ppermute | solution.py:46
  62.5 2.0 %factor.5.refs_2_ = f32[2,432,128]{2,1,0:T(8,128)S(1)} custom-call(s32[28]{0:T(128)S(1)} %stack.115.refs_0_.table_ref, bf16[432,2560]{1,0:T(8,128)(2,1)S(1)} %bitcast.70, bf16[432,2560]{1,0:T(8,128)(2,1)S(1)} %bitcast.65, bf16[128,2560]{1,0:T(8,128)(2,1)S(1)} %constant_dynamic-update-slice_fusion.6.refs_3_.refs_6_, ...), custom_call_target="tpu_custom_call" | custom-call | tf_op jit(solution)/shard_map/factor/pallas_call | solution.py:92
  65.2 9.4 %all-to-all-done.grad_ref = bf16[16,432,128]{2,1,0:T(8,128)(2,1)} async-done(((bf16[16,432,128]{2,1,0:T(8,128)(2,1)}), bf16[16,432,128]{2,1,0:T(8,128)(2,1)}, u32[]{:S(2)}, u32[]{:S(2)}) %all-to-all-start) | async-done | bytes 1769504 | tf_op jit(solution)/shard_map/all_to_all | solution.py:239
  74.7 8.7 %outer.3 = (bf16[432,2048]{1,0:T(8,128)(2,1)}, bf16[8,56,1024]{2,1,0:T(8,128)(2,1)}) custom-call(s32[28]{0:T(128)} %copy-done.12, bf16[16,432,128]{2,1,0:T(8,128)(2,1)} %all-to-all-done.grad_ref, f32[2,432,512]{2,1,0:T(8,128)} %copy-done.9, f32[2,432,384]{2,1,0:T(8,128)} %copy-done.10, f32[2,432,128]{2,1,0:T(8,128)} %copy-done.11, ...), custom_call_target="tpu_custom_call" | custom-call | flops 1811939328 | bytes 5963776 | tf_op jit(solution)/shard_map/outer/pallas_call | solution.py:156
  83.4 3.8 %collective-permute-start.12 = (bf16[8,56,1024]{2,1,0:T(8,128)(2,1)}, bf16[8,56,1024]{2,1,0:T(8,128)(2,1)}, u32[]{:S(2)}, u32[]{:S(2)}) collective-permute-start(bf16[8,56,1024]{2,1,0:T(8,128)(2,1)} %get-tuple-element.33), channel_id=1, source_target_pairs={{0,128},{1,129},{16,144},{17,145},{32,160},{33,161},{48,176},{49,1... | collective-permute-start | bytes 2752520 | tf_op jit(solution)/shard_map/ppermute | solution.py:46
  87.3 4.9 %outer.4 = bf16[8,56,512]{2,1,0:T(8,128)(2,1)} custom-call(s32[28]{0:T(128)} %copy-done.12, bf16[432,2048]{1,0:T(8,128)(2,1)} %get-tuple-element.35.weighted_ref, bf16[128,2560]{1,0:T(8,128)(2,1)} %refs_0_.3, bf16[384,2560]{1,0:T(8,128)(2,1)} %copy-done.1, bf16[384,2560]{1,0:T(8,128)(2,1)} %constant_dynamic-update-slice_fusion.3.refs_3_.refs_5_.refs_2_, ...), custom_call_target="tpu_custom_call" | custom-call | flops 905969664 | bytes 3866624 | tf_op jit(solution)/shard_map/outer/pallas_call | solution.py:156
  92.2 8.5 %all-to-all-start.1 = ((bf16[8,56,512]{2,1,0:T(8,128)(2,1)}), bf16[8,56,512]{2,1,0:T(8,128)(2,1)S(1)}, u32[]{:S(2)}, u32[]{:S(2)}) async-start(bf16[8,56,512]{2,1,0:T(8,128)(2,1)} %outer.4), calls=%async_computation.1 | async-start | bytes 917504 | tf_op jit(solution)/shard_map/all_to_all | solution.py:262
  100.6 7.2 %outer.5 = f32[8,56,1024]{2,1,0:T(8,128)} custom-call(s32[28]{0:T(128)} %copy-done.12, bf16[432,2048]{1,0:T(8,128)(2,1)} %get-tuple-element.35.weighted_ref, bf16[128,2560]{1,0:T(8,128)(2,1)} %refs_0_.3, bf16[384,2560]{1,0:T(8,128)(2,1)} %copy-done.1, bf16[384,2560]{1,0:T(8,128)(2,1)} %constant_dynamic-update-slice_fusion.3.refs_3_.refs_5_.refs_2_, ...), custom_call_target="tpu_custom_call" | custom-call | flops 1811939328 | bytes 5963776 | tf_op jit(solution)/shard_map/outer/pallas_call | solution.py:156
  108.4 2.7 %fusion.7 = (bf16[56,1024]{1,0:T(8,128)(2,1)S(1)}, bf16[56,1024]{1,0:T(8,128)(2,1)}, bf16[56,1024]{1,0:T(8,128)(2,1)}, bf16[56,1024]{1,0:T(8,128)(2,1)}, bf16[56...) fusion(f32[8,56,1024]{2,1,0:T(8,128)} %outer.5, s32[]{:T(128)S(6)} %select_n.110, ...), kind=kLoop, calls=%fused_computation.17 | loop fusion | flops 1204224 | bytes 3211292 | tf_op jit(solution)/shard_map/convert_element_type | solution.py:279
  111.1 7.3 %collective-permute-start.13 = (bf16[56,1024]{1,0:T(8,128)(2,1)S(1)}, bf16[56,1024]{1,0:T(8,128)(2,1)S(1)}, u32[]{:S(2)}, u32[]{:S(2)}) collective-permute-start(bf16[56,1024]{1,0:T(8,128)(2,1)S(1)} %get-tuple-element.37), channel_id=1, source_target_pairs={{0,64},{1,65},{16,80},{17,81},{32,96},{33,97},{48,112},{49,113},{6... | collective-permute-start | bytes 344072 | tf_op jit(solution)/shard_map/ppermute | solution.py:46
  118.4 1.9 %collective-permute-start.14 = (bf16[56,1024]{1,0:T(8,128)(2,1)}, bf16[56,1024]{1,0:T(8,128)(2,1)S(1)}, u32[]{:S(2)}, u32[]{:S(2)}) collective-permute-start(bf16[56,1024]{1,0:T(8,128)(2,1)} %get-tuple-element.43), channel_id=1, source_target_pairs={{0,48},{1,49},{16,64},{17,65},{32,80},{33,81},{48,96},{49,97},{64,... | collective-permute-start | bytes 344072 | tf_op jit(solution)/shard_map/ppermute | solution.py:46
  120.4 1.8 %collective-permute-start.20 = (bf16[56,256]{1,0:T(8,128)(2,1)S(1)}, bf16[56,256]{1,0:T(8,128)(2,1)S(1)}, u32[]{:S(2)}, u32[]{:S(2)}) collective-permute-start(bf16[56,256]{1,0:T(8,128)(2,1)S(1)} %slice.43), channel_id=1, source_target_pairs={{0,128},{1,129},{16,144},{17,145},{32,160},{33,161},{48,176},{49,1... | collective-permute-start | bytes 86024 | tf_op jit(solution)/shard_map/ppermute | solution.py:46
  122.2 3.1 %collective-permute-start.15 = (bf16[56,1024]{1,0:T(8,128)(2,1)}, bf16[56,1024]{1,0:T(8,128)(2,1)S(1)}, u32[]{:S(2)}, u32[]{:S(2)}) collective-permute-start(bf16[56,1024]{1,0:T(8,128)(2,1)} %get-tuple-element.42), channel_id=1, source_target_pairs={{0,80},{1,81},{16,96},{17,97},{32,112},{33,113},{48,0},{49,1},{64,... | collective-permute-start | bytes 344072 | tf_op jit(solution)/shard_map/ppermute | solution.py:46
  125.3 1.5 collective-permute-start.16
  126.8 2.7 %collective-permute-start.17 = (bf16[56,1024]{1,0:T(8,128)(2,1)}, bf16[56,1024]{1,0:T(8,128)(2,1)S(1)}, u32[]{:S(2)}, u32[]{:S(2)}) collective-permute-start(bf16[56,1024]{1,0:T(8,128)(2,1)} %get-tuple-element.40), channel_id=1, source_target_pairs={{0,96},{1,97},{16,112},{17,113},{32,0},{33,1},{48,16},{49,17},{64,... | collective-permute-start | bytes 344072 | tf_op jit(solution)/shard_map/ppermute | solution.py:46
  129.5 1.0 collective-permute-start.18
  130.5 2.5 %collective-permute-done.14 = bf16[56,1024]{1,0:T(8,128)(2,1)S(1)} collective-permute-done((bf16[56,1024]{1,0:T(8,128)(2,1)}, bf16[56,1024]{1,0:T(8,128)(2,1)S(1)}, u32[]{:S(2)}, u32[]{:S(2)}) %collective-permute-start.14) | collective-permute-done | bytes 114720 | tf_op jit(solution)/shard_map/ppermute | solution.py:46
  134.5 4.3 %collective-permute-done.17 = bf16[56,1024]{1,0:T(8,128)(2,1)S(1)} collective-permute-done((bf16[56,1024]{1,0:T(8,128)(2,1)}, bf16[56,1024]{1,0:T(8,128)(2,1)S(1)}, u32[]{:S(2)}, u32[]{:S(2)}) %collective-permute-start.17) | collective-permute-done | bytes 114720 | tf_op jit(solution)/shard_map/ppermute | solution.py:46
  138.7 1.8 %collective-permute-done.19 = bf16[56,1024]{1,0:T(8,128)(2,1)S(1)} collective-permute-done((bf16[56,1024]{1,0:T(8,128)(2,1)}, bf16[56,1024]{1,0:T(8,128)(2,1)S(1)}, u32[]{:S(2)}, u32[]{:S(2)}) %collective-permute-start.19) | collective-permute-done | bytes 114720 | tf_op jit(solution)/shard_map/ppermute | solution.py:46
  140.5 1.2 fusion.6
  142.8 2.8 %collective-permute-start.31 = (bf16[56,1280]{1,0:T(8,128)(2,1)S(1)}, bf16[56,1280]{1,0:T(8,128)(2,1)S(1)}, u32[]{:S(2)}, u32[]{:S(2)}) collective-permute-start(bf16[56,1280]{1,0:T(8,128)(2,1)S(1)} %pad_maximum_fusion.refs_2_), channel_id=1, source_target_pairs={{0,112},{1,113},{16,0},{17,1},{32,16},{33,17},{48,32},{49,33},{64,... | collective-permute-start | bytes 430088 | tf_op jit(solution)/shard_map/ppermute | solution.py:46
  145.6 1.4 collective-permute-done.21.refs_2_
  147.2 2.9 %collective-permute-start.23 = (bf16[56,1280]{1,0:T(8,128)(2,1)S(1)}, bf16[56,1280]{1,0:T(8,128)(2,1)S(1)}, u32[]{:S(2)}, u32[]{:S(2)}) collective-permute-start(bf16[56,1280]{1,0:T(8,128)(2,1)S(1)} %collective-permute-done.21.refs_2_), channel_id=1, source_target_pairs={{0,112},{1,113},{16,0},{17,1},{32,16},{33,17},{48,32},{49,33},{64,... | collective-permute-start | bytes 430088 | tf_op jit(solution)/shard_map/ppermute | solution.py:46
  150.2 3.2 %collective-permute-start.33 = (bf16[56,1280]{1,0:T(8,128)(2,1)S(1)}, bf16[56,1280]{1,0:T(8,128)(2,1)S(1)}, u32[]{:S(2)}, u32[]{:S(2)}) collective-permute-start(bf16[56,1280]{1,0:T(8,128)(2,1)S(1)} %collective-permute-done.31.refs_4_), channel_id=1, source_target_pairs={{0,112},{1,113},{16,0},{17,1},{32,16},{33,17},{48,32},{49,33},{64,... | collective-permute-start | bytes 430088 | tf_op jit(solution)/shard_map/ppermute | solution.py:46
  153.4 1.4 collective-permute-done.22.refs_3_
  154.8 3.2 %collective-permute-start.25 = (bf16[56,1280]{1,0:T(8,128)(2,1)S(1)}, bf16[56,1280]{1,0:T(8,128)(2,1)S(1)}, u32[]{:S(2)}, u32[]{:S(2)}) collective-permute-start(bf16[56,1280]{1,0:T(8,128)(2,1)S(1)} %collective-permute-done.23.refs_4_), channel_id=1, source_target_pairs={{0,112},{1,113},{16,0},{17,1},{32,16},{33,17},{48,32},{49,33},{64,... | collective-permute-start | bytes 430088 | tf_op jit(solution)/shard_map/ppermute | solution.py:46
  158.0 3.2 %collective-permute-start.35 = (bf16[56,1280]{1,0:T(8,128)(2,1)S(1)}, bf16[56,1280]{1,0:T(8,128)(2,1)S(1)}, u32[]{:S(2)}, u32[]{:S(2)}) collective-permute-start(bf16[56,1280]{1,0:T(8,128)(2,1)S(1)} %collective-permute-done.33.refs_6_), channel_id=1, source_target_pairs={{0,112},{1,113},{16,0},{17,1},{32,16},{33,17},{48,32},{49,33},{64,... | collective-permute-start | bytes 430088 | tf_op jit(solution)/shard_map/ppermute | solution.py:46
  161.7 3.2 %collective-permute-start.27 = (bf16[56,1280]{1,0:T(8,128)(2,1)S(1)}, bf16[56,1280]{1,0:T(8,128)(2,1)S(1)}, u32[]{:S(2)}, u32[]{:S(2)}) collective-permute-start(bf16[56,1280]{1,0:T(8,128)(2,1)S(1)} %collective-permute-done.25.refs_6_), channel_id=1, source_target_pairs={{0,112},{1,113},{16,0},{17,1},{32,16},{33,17},{48,32},{49,33},{64,... | collective-permute-start | bytes 430088 | tf_op jit(solution)/shard_map/ppermute | solution.py:46
  165.1 3.3 %collective-permute-start.37 = (bf16[56,640]{1,0:T(8,128)(2,1)S(1)}, bf16[56,640]{1,0:T(8,128)(2,1)S(1)}, u32[]{:S(2)}, u32[]{:S(2)}) collective-permute-start(bf16[56,640]{1,0:T(8,128)(2,1)S(1)} %slice.38), channel_id=1, source_target_pairs={{0,112},{1,113},{16,0},{17,1},{32,16},{33,17},{48,32},{49,33},{64,... | collective-permute-start | bytes 215048 | tf_op jit(solution)/shard_map/ppermute | solution.py:46
  168.9 3.3 %collective-permute-start.29 = (bf16[56,640]{1,0:T(8,128)(2,1)S(1)}, bf16[56,640]{1,0:T(8,128)(2,1)S(1)}, u32[]{:S(2)}, u32[]{:S(2)}) collective-permute-start(bf16[56,640]{1,0:T(8,128)(2,1)S(1)} %slice.36), channel_id=1, source_target_pairs={{0,112},{1,113},{16,0},{17,1},{32,16},{33,17},{48,32},{49,33},{64,... | collective-permute-start | bytes 215048 | tf_op jit(solution)/shard_map/ppermute | solution.py:46
  172.2 2.4 %finish.2.refs_11_ = f32[432,2560]{1,0:T(8,128)} custom-call(s32[28]{0:T(128)S(1)} %copy-done.13, bf16[432,2560]{1,0:T(8,128)(2,1)S(1)} %bitcast.66, bf16[56,1280]{1,0:T(8,128)(2,1)S(1)} %pad_maximum_fusion.refs_2_, bf16[56,1280]{1,0:T(8,128)(2,1)S(1)} %collective-permute-done.30.refs_3_, bf16[56,1280]{1,0:T(8,128)(2,1)S(1)} %collective-permute-done.31.refs_4_, ...), custom_call_target="tpu_custom_call" | custom-call | tf_op jit(solution)/shard_map/finish/pallas_call | solution.py:203
  174.6 2.4 %finish.3 = f32[432,2560]{1,0:T(8,128)} custom-call(s32[28]{0:T(128)S(1)} %copy-done.13, bf16[432,2560]{1,0:T(8,128)(2,1)S(1)} %bitcast.67, bf16[56,1280]{1,0:T(8,128)(2,1)S(1)} %collective-permute-done.21.refs_2_, bf16[56,1280]{1,0:T(8,128)(2,1)S(1)} %collective-permute-done.22.refs_3_, ...), custom_call_target="tpu_custom_call", output_to_operand_aliasing={{}: (11, {})} | custom-call | tf_op jit(solution)/shard_map/finish/pallas_call | solution.py:203
  (92 shorter events, 11.8 us)
Async XLA Ops:
  0.0 17.9 %collective-permute-start = (bf16[128,2560]{1,0:T(8,128)(2,1)}, bf16[128,2560]{1,0:T(8,128)(2,1)S(1)}, u32[]{:S(2)}, u32[]{:S(2)}) collective-permute-start(bf16[128,2560]{1,0:T(8,128)(2,1)} %refs_0_.3), channel_id=1, source_target_pairs={{0,4},{1,5},{16,20},{17,21},{32,36},{33,37},{48,52},{49,53},{64,68... | collective-permute-start | bytes 1966088 | tf_op jit(solution)/shard_map/ppermute | solution.py:46
  1.5 16.4 %collective-permute-start.1 = (bf16[128,2560]{1,0:T(8,128)(2,1)}, bf16[128,2560]{1,0:T(8,128)(2,1)S(1)}, u32[]{:S(2)}, u32[]{:S(2)}) collective-permute-start(bf16[128,2560]{1,0:T(8,128)(2,1)} %refs_0_.3), channel_id=1, source_target_pairs={{0,12},{1,13},{16,28},{17,29},{32,44},{33,45},{48,60},{49,61},{64,... | collective-permute-start | bytes 1966088 | tf_op jit(solution)/shard_map/ppermute | solution.py:46
  3.2 16.1 %collective-permute-start.2 = (bf16[128,2560]{1,0:T(8,128)(2,1)}, bf16[128,2560]{1,0:T(8,128)(2,1)S(1)}, u32[]{:S(2)}, u32[]{:S(2)}) collective-permute-start(bf16[128,2560]{1,0:T(8,128)(2,1)} %refs_0_.3), channel_id=1, source_target_pairs={{0,130},{1,131},{16,146},{17,147},{32,162},{33,163},{48,178},{49,1... | collective-permute-start | bytes 1966088 | tf_op jit(solution)/shard_map/ppermute | solution.py:46
  7.7 54.8 %copy-start.12 = (s32[28]{0:T(128)}, s32[28]{0:T(128)S(1)}, u32[]{:S(2)}) copy-start(s32[28]{0:T(128)S(1)} %stack.115.refs_0_.table_ref) | copy-start | bytes 340
  19.4 6.4 %copy-start = (bf16[2560,432]{0,1:T(8,128)(2,1)S(1)}, bf16[2560,432]{0,1:T(8,128)(2,1)}, u32[]{:S(2)}) copy-start(bf16[2560,432]{0,1:T(8,128)(2,1)} %param.7) | copy-start | bytes 6635524
  20.8 14.5 %copy-start.1 = (bf16[384,2560]{1,0:T(8,128)(2,1)}, bf16[384,2560]{1,0:T(8,128)(2,1)S(1)}, u32[]{:S(2)}) copy-start(bf16[384,2560]{1,0:T(8,128)(2,1)S(1)} %constant_dynamic-update-slice_fusion.refs_5_.refs_4_.refs_1_) | copy-start | bytes 5898244
  20.8 5.0 %collective-permute-start.4 = (bf16[384,2560]{1,0:T(8,128)(2,1)S(1)}, bf16[384,2560]{1,0:T(8,128)(2,1)S(1)}, u32[]{:S(2)}, u32[]{:S(2)}) collective-permute-start(bf16[384,2560]{1,0:T(8,128)(2,1)S(1)} %constant_dynamic-update-slice_fusion.refs_5_.refs_4_.refs_1_), channel_id=1, source_target_pairs={{0,1},{1,0},{16,17},{17,16},{32,33},{33,32},{48,49},{49,48},{64,65... | collective-permute-start | bytes 5898248 | tf_op jit(solution)/shard_map/ppermute | solution.py:46
  20.9 4.9 %collective-permute-start.3 = (bf16[128,2560]{1,0:T(8,128)(2,1)S(1)}, bf16[128,2560]{1,0:T(8,128)(2,1)S(1)}, u32[]{:S(2)}, u32[]{:S(2)}) collective-permute-start(bf16[128,2560]{1,0:T(8,128)(2,1)S(1)} %copy-done.6), channel_id=1, source_target_pairs={{0,1},{1,0},{16,17},{17,16},{32,33},{33,32},{48,49},{49,48},{64,65... | collective-permute-start | bytes 1966088 | tf_op jit(solution)/shard_map/ppermute | solution.py:46
  21.4 18.0 %collective-permute-start.5 = (bf16[128,2560]{1,0:T(8,128)(2,1)S(1)}, bf16[128,2560]{1,0:T(8,128)(2,1)S(1)}, u32[]{:S(2)}, u32[]{:S(2)}) collective-permute-start(bf16[128,2560]{1,0:T(8,128)(2,1)S(1)} %collective-permute-done.2), channel_id=1, source_target_pairs={{0,4},{1,5},{16,20},{17,21},{32,36},{33,37},{48,52},{49,53},{64,68... | collective-permute-start | bytes 1966088 | tf_op jit(solution)/shard_map/ppermute | solution.py:46
  21.6 17.7 %collective-permute-start.6 = (bf16[128,2560]{1,0:T(8,128)(2,1)S(1)}, bf16[128,2560]{1,0:T(8,128)(2,1)S(1)}, u32[]{:S(2)}, u32[]{:S(2)}) collective-permute-start(bf16[128,2560]{1,0:T(8,128)(2,1)S(1)} %collective-permute-done.1), channel_id=1, source_target_pairs={{0,12},{1,13},{16,28},{17,29},{32,44},{33,45},{48,60},{49,61},{64,... | collective-permute-start | bytes 1966088 | tf_op jit(solution)/shard_map/ppermute | solution.py:46
  24.6 16.2 %collective-permute-start.7 = (bf16[128,2560]{1,0:T(8,128)(2,1)S(1)}, bf16[128,2560]{1,0:T(8,128)(2,1)S(1)}, u32[]{:S(2)}, u32[]{:S(2)}) collective-permute-start(bf16[128,2560]{1,0:T(8,128)(2,1)S(1)} %collective-permute-done.1), channel_id=1, source_target_pairs={{0,130},{1,131},{16,146},{17,147},{32,162},{33,163},{48,178},{49,1... | collective-permute-start | bytes 1966088 | tf_op jit(solution)/shard_map/ppermute | solution.py:46
  25.8 9.5 %copy-start.7 = (bf16[128,2560]{1,0:T(8,128)(2,1)}, bf16[128,2560]{1,0:T(8,128)(2,1)S(1)}, u32[]{:S(2)}) copy-start(bf16[128,2560]{1,0:T(8,128)(2,1)S(1)} %collective-permute-done.3.refs_4_.refs_7_) | copy-start | bytes 1966084
  25.8 9.5 %copy-start.2 = (bf16[384,2560]{1,0:T(8,128)(2,1)}, bf16[384,2560]{1,0:T(8,128)(2,1)S(1)}, u32[]{:S(2)}) copy-start(bf16[384,2560]{1,0:T(8,128)(2,1)S(1)} %collective-permute-done.4.refs_6_.refs_8_.refs_5_) | copy-start | bytes 5898244
  35.3 7.3 %copy-start.9 = (f32[2,432,512]{2,1,0:T(8,128)}, f32[2,432,512]{2,1,0:T(8,128)S(1)}, u32[]{:S(2)}) copy-start(f32[2,432,512]{2,1,0:T(8,128)S(1)} %factor.3.refs_0_) | copy-start | bytes 5308420
  43.5 7.5 %collective-permute-start.8 = (bf16[384,2560]{1,0:T(8,128)(2,1)}, bf16[384,2560]{1,0:T(8,128)(2,1)}, u32[]{:S(2)}, u32[]{:S(2)}) collective-permute-start(bf16[384,2560]{1,0:T(8,128)(2,1)} %constant_dynamic-update-slice_fusion.3.refs_3_.refs_5_.refs_2_), channel_id=1, source_target_pairs={{0,1},{1,0},{16,17},{17,16},{32,33},{33,32},{48,49},{49,48},{64,65... | collective-permute-start | bytes 5898248 | tf_op jit(solution)/shard_map/ppermute | solution.py:46
  43.5 16.5 %collective-permute-start.10 = (bf16[64,2560]{1,0:T(8,128)(2,1)S(1)}, bf16[64,2560]{1,0:T(8,128)(2,1)S(1)}, u32[]{:S(2)}, u32[]{:S(2)}) collective-permute-start(bf16[64,2560]{1,0:T(8,128)(2,1)S(1)} %slice.26), channel_id=1, source_target_pairs={{0,12},{1,13},{16,28},{17,29},{32,44},{33,45},{48,60},{49,61},{64,... | collective-permute-start | bytes 983048 | tf_op jit(solution)/shard_map/ppermute | solution.py:46
  45.0 15.0 %collective-permute-start.9 = (bf16[64,2560]{1,0:T(8,128)(2,1)S(1)}, bf16[64,2560]{1,0:T(8,128)(2,1)S(1)}, u32[]{:S(2)}, u32[]{:S(2)}) collective-permute-start(bf16[64,2560]{1,0:T(8,128)(2,1)S(1)} %slice.25), channel_id=1, source_target_pairs={{0,4},{1,5},{16,20},{17,21},{32,36},{33,37},{48,52},{49,53},{64,68... | collective-permute-start | bytes 983048 | tf_op jit(solution)/shard_map/ppermute | solution.py:46
  45.5 29.2 %all-to-all-start = ((bf16[16,432,128]{2,1,0:T(8,128)(2,1)}), bf16[16,432,128]{2,1,0:T(8,128)(2,1)}, u32[]{:S(2)}, u32[]{:S(2)}) async-start(bf16[16,432,128]{2,1,0:T(8,128)(2,1)} %bitcast.71), calls=%async_computation | async-start | bytes 3538944 | tf_op jit(solution)/shard_map/all_to_all | solution.py:239
  60.1 4.4 %copy-start.5 = (bf16[128,2560]{1,0:T(8,128)(2,1)}, bf16[128,2560]{1,0:T(8,128)(2,1)S(1)}, u32[]{:S(2)}) copy-start(bf16[128,2560]{1,0:T(8,128)(2,1)S(1)} %constant_dynamic-update-slice_fusion.6.refs_3_.refs_6_) | copy-start | bytes 1966084
  60.1 2.4 %collective-permute-start.11 = (bf16[128,2560]{1,0:T(8,128)(2,1)S(1)}, bf16[128,2560]{1,0:T(8,128)(2,1)S(1)}, u32[]{:S(2)}, u32[]{:S(2)}) collective-permute-start(bf16[128,2560]{1,0:T(8,128)(2,1)S(1)} %constant_dynamic-update-slice_fusion.6.refs_3_.refs_6_), channel_id=1, source_target_pairs={{0,1},{1,0},{16,17},{17,16},{32,33},{33,32},{48,49},{49,48},{64,65... | collective-permute-start | bytes 1966088 | tf_op jit(solution)/shard_map/ppermute | solution.py:46
  83.4 25.0 %collective-permute-start.12 = (bf16[8,56,1024]{2,1,0:T(8,128)(2,1)}, bf16[8,56,1024]{2,1,0:T(8,128)(2,1)}, u32[]{:S(2)}, u32[]{:S(2)}) collective-permute-start(bf16[8,56,1024]{2,1,0:T(8,128)(2,1)} %get-tuple-element.33), channel_id=1, source_target_pairs={{0,128},{1,129},{16,144},{17,145},{32,160},{33,161},{48,176},{49,1... | collective-permute-start | bytes 2752520 | tf_op jit(solution)/shard_map/ppermute | solution.py:46
  92.2 28.1 %all-to-all-start.1 = ((bf16[8,56,512]{2,1,0:T(8,128)(2,1)}), bf16[8,56,512]{2,1,0:T(8,128)(2,1)S(1)}, u32[]{:S(2)}, u32[]{:S(2)}) async-start(bf16[8,56,512]{2,1,0:T(8,128)(2,1)} %outer.4), calls=%async_computation.1 | async-start | bytes 917504 | tf_op jit(solution)/shard_map/all_to_all | solution.py:262
  111.1 61.1 %copy-start.13 = (s32[28]{0:T(128)S(1)}, s32[28]{0:T(128)}, u32[]{:S(2)}) copy-start(s32[28]{0:T(128)} %copy-done.12) | copy-start | bytes 340
  111.1 18.4 %collective-permute-start.13 = (bf16[56,1024]{1,0:T(8,128)(2,1)S(1)}, bf16[56,1024]{1,0:T(8,128)(2,1)S(1)}, u32[]{:S(2)}, u32[]{:S(2)}) collective-permute-start(bf16[56,1024]{1,0:T(8,128)(2,1)S(1)} %get-tuple-element.37), channel_id=1, source_target_pairs={{0,64},{1,65},{16,80},{17,81},{32,96},{33,97},{48,112},{49,113},{6... | collective-permute-start | bytes 344072 | tf_op jit(solution)/shard_map/ppermute | solution.py:46
  118.4 14.6 %collective-permute-start.14 = (bf16[56,1024]{1,0:T(8,128)(2,1)}, bf16[56,1024]{1,0:T(8,128)(2,1)S(1)}, u32[]{:S(2)}, u32[]{:S(2)}) collective-permute-start(bf16[56,1024]{1,0:T(8,128)(2,1)} %get-tuple-element.43), channel_id=1, source_target_pairs={{0,48},{1,49},{16,64},{17,65},{32,80},{33,81},{48,96},{49,97},{64,... | collective-permute-start | bytes 344072 | tf_op jit(solution)/shard_map/ppermute | solution.py:46
  120.4 6.4 %collective-permute-start.20 = (bf16[56,256]{1,0:T(8,128)(2,1)S(1)}, bf16[56,256]{1,0:T(8,128)(2,1)S(1)}, u32[]{:S(2)}, u32[]{:S(2)}) collective-permute-start(bf16[56,256]{1,0:T(8,128)(2,1)S(1)} %slice.43), channel_id=1, source_target_pairs={{0,128},{1,129},{16,144},{17,145},{32,160},{33,161},{48,176},{49,1... | collective-permute-start | bytes 86024 | tf_op jit(solution)/shard_map/ppermute | solution.py:46
  122.2 11.4 %collective-permute-start.15 = (bf16[56,1024]{1,0:T(8,128)(2,1)}, bf16[56,1024]{1,0:T(8,128)(2,1)S(1)}, u32[]{:S(2)}, u32[]{:S(2)}) collective-permute-start(bf16[56,1024]{1,0:T(8,128)(2,1)} %get-tuple-element.42), channel_id=1, source_target_pairs={{0,80},{1,81},{16,96},{17,97},{32,112},{33,113},{48,0},{49,1},{64,... | collective-permute-start | bytes 344072 | tf_op jit(solution)/shard_map/ppermute | solution.py:46
  125.3 9.2 %collective-permute-start.16 = (bf16[56,1024]{1,0:T(8,128)(2,1)}, bf16[56,1024]{1,0:T(8,128)(2,1)S(1)}, u32[]{:S(2)}, u32[]{:S(2)}) collective-permute-start(bf16[56,1024]{1,0:T(8,128)(2,1)} %get-tuple-element.41), channel_id=1, source_target_pairs={{0,32},{1,33},{16,48},{17,49},{32,64},{33,65},{48,80},{49,81},{64,... | collective-permute-start | bytes 344072 | tf_op jit(solution)/shard_map/ppermute | solution.py:46
  126.8 11.9 %collective-permute-start.17 = (bf16[56,1024]{1,0:T(8,128)(2,1)}, bf16[56,1024]{1,0:T(8,128)(2,1)S(1)}, u32[]{:S(2)}, u32[]{:S(2)}) collective-permute-start(bf16[56,1024]{1,0:T(8,128)(2,1)} %get-tuple-element.40), channel_id=1, source_target_pairs={{0,96},{1,97},{16,112},{17,113},{32,0},{33,1},{48,16},{49,17},{64,... | collective-permute-start | bytes 344072 | tf_op jit(solution)/shard_map/ppermute | solution.py:46
  129.5 9.3 %collective-permute-start.18 = (bf16[56,1024]{1,0:T(8,128)(2,1)}, bf16[56,1024]{1,0:T(8,128)(2,1)S(1)}, u32[]{:S(2)}, u32[]{:S(2)}) collective-permute-start(bf16[56,1024]{1,0:T(8,128)(2,1)} %get-tuple-element.39), channel_id=1, source_target_pairs={{0,16},{1,17},{16,32},{17,33},{32,48},{33,49},{48,64},{49,65},{64,... | collective-permute-start | bytes 344072 | tf_op jit(solution)/shard_map/ppermute | solution.py:46
  133.0 7.6 %collective-permute-start.19 = (bf16[56,1024]{1,0:T(8,128)(2,1)}, bf16[56,1024]{1,0:T(8,128)(2,1)S(1)}, u32[]{:S(2)}, u32[]{:S(2)}) collective-permute-start(bf16[56,1024]{1,0:T(8,128)(2,1)} %get-tuple-element.38), channel_id=1, source_target_pairs={{0,112},{1,113},{16,0},{17,1},{32,16},{33,17},{48,32},{49,33},{64,... | collective-permute-start | bytes 344072 | tf_op jit(solution)/shard_map/ppermute | solution.py:46
  141.7 5.2 %collective-permute-start.21 = (bf16[56,1280]{1,0:T(8,128)(2,1)S(1)}, bf16[56,1280]{1,0:T(8,128)(2,1)S(1)}, u32[]{:S(2)}, u32[]{:S(2)}) collective-permute-start(bf16[56,1280]{1,0:T(8,128)(2,1)S(1)} %pad_maximum_fusion.refs_2_), channel_id=1, source_target_pairs={{0,128},{1,129},{16,144},{17,145},{32,160},{33,161},{48,176},{49,1... | collective-permute-start | bytes 430088 | tf_op jit(solution)/shard_map/ppermute | solution.py:46
  142.3 7.8 %collective-permute-start.30 = (bf16[56,1280]{1,0:T(8,128)(2,1)S(1)}, bf16[56,1280]{1,0:T(8,128)(2,1)S(1)}, u32[]{:S(2)}, u32[]{:S(2)}) collective-permute-start(bf16[56,1280]{1,0:T(8,128)(2,1)S(1)} %pad_maximum_fusion.refs_2_), channel_id=1, source_target_pairs={{0,16},{1,17},{16,32},{17,33},{32,48},{33,49},{48,64},{49,65},{64,... | collective-permute-start | bytes 430088 | tf_op jit(solution)/shard_map/ppermute | solution.py:46
  142.8 7.4 %collective-permute-start.31 = (bf16[56,1280]{1,0:T(8,128)(2,1)S(1)}, bf16[56,1280]{1,0:T(8,128)(2,1)S(1)}, u32[]{:S(2)}, u32[]{:S(2)}) collective-permute-start(bf16[56,1280]{1,0:T(8,128)(2,1)S(1)} %pad_maximum_fusion.refs_2_), channel_id=1, source_target_pairs={{0,112},{1,113},{16,0},{17,1},{32,16},{33,17},{48,32},{49,33},{64,... | collective-permute-start | bytes 430088 | tf_op jit(solution)/shard_map/ppermute | solution.py:46
  146.9 7.8 %collective-permute-start.22 = (bf16[56,1280]{1,0:T(8,128)(2,1)S(1)}, bf16[56,1280]{1,0:T(8,128)(2,1)S(1)}, u32[]{:S(2)}, u32[]{:S(2)}) collective-permute-start(bf16[56,1280]{1,0:T(8,128)(2,1)S(1)} %collective-permute-done.21.refs_2_), channel_id=1, source_target_pairs={{0,16},{1,17},{16,32},{17,33},{32,48},{33,49},{48,64},{49,65},{64,... | collective-permute-start | bytes 430088 | tf_op jit(solution)/shard_map/ppermute | solution.py:46
  147.2 7.5 %collective-permute-start.23 = (bf16[56,1280]{1,0:T(8,128)(2,1)S(1)}, bf16[56,1280]{1,0:T(8,128)(2,1)S(1)}, u32[]{:S(2)}, u32[]{:S(2)}) collective-permute-start(bf16[56,1280]{1,0:T(8,128)(2,1)S(1)} %collective-permute-done.21.refs_2_), channel_id=1, source_target_pairs={{0,112},{1,113},{16,0},{17,1},{32,16},{33,17},{48,32},{49,33},{64,... | collective-permute-start | bytes 430088 | tf_op jit(solution)/shard_map/ppermute | solution.py:46
  150.2 7.8 %collective-permute-start.32 = (bf16[56,1280]{1,0:T(8,128)(2,1)S(1)}, bf16[56,1280]{1,0:T(8,128)(2,1)S(1)}, u32[]{:S(2)}, u32[]{:S(2)}) collective-permute-start(bf16[56,1280]{1,0:T(8,128)(2,1)S(1)} %collective-permute-done.30.refs_3_), channel_id=1, source_target_pairs={{0,16},{1,17},{16,32},{17,33},{32,48},{33,49},{48,64},{49,65},{64,... | collective-permute-start | bytes 430088 | tf_op jit(solution)/shard_map/ppermute | solution.py:46
  150.2 7.8 %collective-permute-start.33 = (bf16[56,1280]{1,0:T(8,128)(2,1)S(1)}, bf16[56,1280]{1,0:T(8,128)(2,1)S(1)}, u32[]{:S(2)}, u32[]{:S(2)}) collective-permute-start(bf16[56,1280]{1,0:T(8,128)(2,1)S(1)} %collective-permute-done.31.refs_4_), channel_id=1, source_target_pairs={{0,112},{1,113},{16,0},{17,1},{32,16},{33,17},{48,32},{49,33},{64,... | collective-permute-start | bytes 430088 | tf_op jit(solution)/shard_map/ppermute | solution.py:46
  154.8 6.9 %collective-permute-start.24 = (bf16[56,1280]{1,0:T(8,128)(2,1)S(1)}, bf16[56,1280]{1,0:T(8,128)(2,1)S(1)}, u32[]{:S(2)}, u32[]{:S(2)}) collective-permute-start(bf16[56,1280]{1,0:T(8,128)(2,1)S(1)} %collective-permute-done.22.refs_3_), channel_id=1, source_target_pairs={{0,16},{1,17},{16,32},{17,33},{32,48},{33,49},{48,64},{49,65},{64,... | collective-permute-start | bytes 430088 | tf_op jit(solution)/shard_map/ppermute | solution.py:46
  154.8 6.9 %collective-permute-start.25 = (bf16[56,1280]{1,0:T(8,128)(2,1)S(1)}, bf16[56,1280]{1,0:T(8,128)(2,1)S(1)}, u32[]{:S(2)}, u32[]{:S(2)}) collective-permute-start(bf16[56,1280]{1,0:T(8,128)(2,1)S(1)} %collective-permute-done.23.refs_4_), channel_id=1, source_target_pairs={{0,112},{1,113},{16,0},{17,1},{32,16},{33,17},{48,32},{49,33},{64,... | collective-permute-start | bytes 430088 | tf_op jit(solution)/shard_map/ppermute | solution.py:46
  158.0 6.9 %collective-permute-start.34 = (bf16[56,1280]{1,0:T(8,128)(2,1)S(1)}, bf16[56,1280]{1,0:T(8,128)(2,1)S(1)}, u32[]{:S(2)}, u32[]{:S(2)}) collective-permute-start(bf16[56,1280]{1,0:T(8,128)(2,1)S(1)} %collective-permute-done.32.refs_5_), channel_id=1, source_target_pairs={{0,16},{1,17},{16,32},{17,33},{32,48},{33,49},{48,64},{49,65},{64,... | collective-permute-start | bytes 430088 | tf_op jit(solution)/shard_map/ppermute | solution.py:46
  158.0 7.0 %collective-permute-start.35 = (bf16[56,1280]{1,0:T(8,128)(2,1)S(1)}, bf16[56,1280]{1,0:T(8,128)(2,1)S(1)}, u32[]{:S(2)}, u32[]{:S(2)}) collective-permute-start(bf16[56,1280]{1,0:T(8,128)(2,1)S(1)} %collective-permute-done.33.refs_6_), channel_id=1, source_target_pairs={{0,112},{1,113},{16,0},{17,1},{32,16},{33,17},{48,32},{49,33},{64,... | collective-permute-start | bytes 430088 | tf_op jit(solution)/shard_map/ppermute | solution.py:46
  161.7 7.0 %collective-permute-start.26 = (bf16[56,1280]{1,0:T(8,128)(2,1)S(1)}, bf16[56,1280]{1,0:T(8,128)(2,1)S(1)}, u32[]{:S(2)}, u32[]{:S(2)}) collective-permute-start(bf16[56,1280]{1,0:T(8,128)(2,1)S(1)} %collective-permute-done.24.refs_5_), channel_id=1, source_target_pairs={{0,16},{1,17},{16,32},{17,33},{32,48},{33,49},{48,64},{49,65},{64,... | collective-permute-start | bytes 430088 | tf_op jit(solution)/shard_map/ppermute | solution.py:46
  161.7 7.1 %collective-permute-start.27 = (bf16[56,1280]{1,0:T(8,128)(2,1)S(1)}, bf16[56,1280]{1,0:T(8,128)(2,1)S(1)}, u32[]{:S(2)}, u32[]{:S(2)}) collective-permute-start(bf16[56,1280]{1,0:T(8,128)(2,1)S(1)} %collective-permute-done.25.refs_6_), channel_id=1, source_target_pairs={{0,112},{1,113},{16,0},{17,1},{32,16},{33,17},{48,32},{49,33},{64,... | collective-permute-start | bytes 430088 | tf_op jit(solution)/shard_map/ppermute | solution.py:46
  165.0 7.2 %collective-permute-start.36 = (bf16[56,640]{1,0:T(8,128)(2,1)S(1)}, bf16[56,640]{1,0:T(8,128)(2,1)S(1)}, u32[]{:S(2)}, u32[]{:S(2)}) collective-permute-start(bf16[56,640]{1,0:T(8,128)(2,1)S(1)} %slice.37), channel_id=1, source_target_pairs={{0,16},{1,17},{16,32},{17,33},{32,48},{33,49},{48,64},{49,65},{64,... | collective-permute-start | bytes 215048 | tf_op jit(solution)/shard_map/ppermute | solution.py:46
  165.1 7.1 %collective-permute-start.37 = (bf16[56,640]{1,0:T(8,128)(2,1)S(1)}, bf16[56,640]{1,0:T(8,128)(2,1)S(1)}, u32[]{:S(2)}, u32[]{:S(2)}) collective-permute-start(bf16[56,640]{1,0:T(8,128)(2,1)S(1)} %slice.38), channel_id=1, source_target_pairs={{0,112},{1,113},{16,0},{17,1},{32,16},{33,17},{48,32},{49,33},{64,... | collective-permute-start | bytes 215048 | tf_op jit(solution)/shard_map/ppermute | solution.py:46
  168.8 5.8 %collective-permute-start.28 = (bf16[56,640]{1,0:T(8,128)(2,1)S(1)}, bf16[56,640]{1,0:T(8,128)(2,1)S(1)}, u32[]{:S(2)}, u32[]{:S(2)}) collective-permute-start(bf16[56,640]{1,0:T(8,128)(2,1)S(1)} %slice.35), channel_id=1, source_target_pairs={{0,16},{1,17},{16,32},{17,33},{32,48},{33,49},{48,64},{49,65},{64,... | collective-permute-start | bytes 215048 | tf_op jit(solution)/shard_map/ppermute | solution.py:46
  168.9 5.7 %collective-permute-start.29 = (bf16[56,640]{1,0:T(8,128)(2,1)S(1)}, bf16[56,640]{1,0:T(8,128)(2,1)S(1)}, u32[]{:S(2)}, u32[]{:S(2)}) collective-permute-start(bf16[56,640]{1,0:T(8,128)(2,1)S(1)} %slice.36), channel_id=1, source_target_pairs={{0,112},{1,113},{16,0},{17,1},{32,16},{33,17},{48,32},{49,33},{64,... | collective-permute-start | bytes 215048 | tf_op jit(solution)/shard_map/ppermute | solution.py:46
  (7 other events, 11.0 us)
